TPU v7x, 128 devices: a whole 4x4x4 slice. The times are simulated.
128 devices in a mesh: row: 8 (over z, core), col: 16 (over y, x).
Axes of the slice: x: 4, y: 4, z: 4, core: 2. Of those that a mesh axis runs over, the one named last changes fastest.
Arguments:
- volume: float32 [1280, 16, 256], P(('row', 'col')), may hold values from 0 to 1
- velocity: float32 [3, 1280, 16, 256], P(None, ('row', 'col')), may hold values from -4 to 4
- source: float32 [1280, 16, 256], P(('row', 'col')), may hold values from -6 to 6
- pressure_prev: float32 [1280, 16, 256], P(('row', 'col')), may hold values from -6 to 6
- neighbours: int32 [1024, 6], replicated, may hold values from -1 to 1023, as said below
- levels: int32 [1024], replicated, may hold values from 0 to 2
- refine: int32 [1024], replicated, may hold values 0 or 1
- bounds_old: int32 [129], replicated, may hold values from 0 to 1024, as said below
- bounds_new: int32 [129], replicated, may hold values from 0 to 1024, as said below
Outputs:
- vof_new: float32 [1280, 16, 256], P(('row', 'col'))
- pressure: float32 [1280, 16, 256], P(('row', 'col'))
Inputs may be any that keep to these rules, and one draw needn't show every extreme that they name: The grid is a forest of two octrees side by side along i: tiles below 512 form the first tree, the others the second; within a tree, local index g mod (512) gives local coordinates from its bits (bit b is bit b // 3 of coordinate b mod 3), and the second tree's i runs mirrored, so that its tile with local i coordinate q sits at global i = 2 E - 1 - q, E being a tree's extent along i; neighbours[g, f] is the tile one step across face f in global coordinates, or -1 at the grid's boundary and where the face is closed by a wall; faces between the two trees are open; neighbours[g, 2a + 1] = p >= 0 exactly when neighbours[p, 2a] = g. `bounds_old`: entry 0 is 0, the last entry is 1024, and every entry d differs from d * 8 by at most 1; on some device both its first entry is 1 below and its next entry 1 above the even place. `bounds_new`: entry 0 is 0, the last entry is 1024, and every entry d differs from d * 8 by at most 1; on some device both its first entry is 1 below and its next entry 1 above the even place.
All inputs are finite; a program needn't handle non-finite values.
Results may differ from a plain program's by a relative error of at most 0.0003.
Values sent between devices are 32-bit elements; how exact they have to be, the bound alone decides.
No kernel may reach another device: no remote copies, remote signals or barrier semaphores. Data moves between devices by JAX's collectives and lax.ppermute only.
A program may use at most 64 MiB of HBM per device.

v0:
```python
import jax
import jax.numpy as jnp
from jax import lax
from jax.experimental import pallas as pl
from jax.experimental.pallas import tpu as pltpu
from jax.sharding import PartitionSpec as P

SWEEPS = 4
CFL = 0.4
SIGMA = 0.05
RHO_GAS = 0.05
RHO_LIQ = 1.0
AXES = ("row", "col")
DEVS = 128
F32 = jnp.float32


def block_coords(d):
    tree, low = d >> 6, d & 63
    i = (low & 1) | (((low >> 3) & 1) << 1)
    j = ((low >> 1) & 1) | (((low >> 4) & 1) << 1)
    k = ((low >> 2) & 1) | (((low >> 5) & 1) << 1)
    return (7 - i if tree else i), j, k


PLACE = {block_coords(d): d for d in range(DEVS)}


def axis_pairs(axis, odd):
    count = (8, 4, 4)[axis]
    pairs = []
    for d in range(DEVS):
        c = list(block_coords(d))
        step = 1 if (c[axis] % 2 == 0) != bool(odd) else -1
        c[axis] = (c[axis] + step) % count
        pairs.append((d, PLACE[tuple(c)]))
    return pairs


def flip_pairs(bits):
    return [(d, d ^ bits) for d in range(DEVS)]


EVEN_PAIRS = flip_pairs(1)
ODD_PAIRS = [(d, d + 1 if d % 2 else d - 1) for d in range(1, DEVS - 1)]


def send(x, pairs):
    return lax.ppermute(x, AXES, pairs)


def where_am_i():
    d = lax.axis_index("row") * 16 + lax.axis_index("col")
    tree = d >> 6
    i = (d & 1) | (((d >> 3) & 1) << 1)
    gi = jnp.where(tree == 1, 7 - i, i)
    gj = ((d >> 1) & 1) | (((d >> 4) & 1) << 1)
    gk = ((d >> 2) & 1) | (((d >> 5) & 1) << 1)
    return d, tree, gi, gj, gk


def iotas():
    sub = lax.broadcasted_iota(jnp.int32, (8, 128), 0)
    lane = lax.broadcasted_iota(jnp.int32, (8, 128), 1)
    return sub, lane


def rl(x, shift):
    return pltpu.roll(x, shift % 128, 1)


def rs(x, shift):
    n = x.shape[0]
    return pltpu.roll(x, shift % n, 0)


def halves(h):
    return pl.ds(128 * h, 128)


def old_slice(fields, f, slot, start, count, h):
    vol, vel, src, prev = fields
    rows = pl.ds(pl.multiple_of(start, 8), count)
    if f == 0:
        return vol[slot, rows, halves(h)]
    if f < 4:
        return vel[f - 1, slot, rows, halves(h)]
    return (src if f == 4 else prev)[slot, rows, halves(h)]


def slab_groups(get, high, sub):
    nat = (sub >= 4) == high
    return (
        get(0),
        get(1),
        jnp.where(nat, get(2), rs(get(3), 4)),
        jnp.where(nat, get(5), rs(get(4), 4)),
    )


def first_kernel(vol, vel, src, prev, levels, bounds, ra, rb, peak):
    d, tree, gi, gj, gk = where_am_i()
    sub, lane = iotas()
    fields = (vol, vel, src, prev)
    start = bounds[d]
    count = bounds[d + 1] - start
    off = 8 * d - start
    even = d % 2 == 0
    slot_a = jnp.where(even, 8 + off, 0)
    slot_b = jnp.where(even, 0, 8 + off)
    for f in range(6):
        for r in range(2):
            for h in range(2):
                ra[f * 4 + r * 2 + h] = old_slice(fields, f, slot_a, 8 * r, 8, h)
                rb[f * 4 + r * 2 + h] = old_slice(fields, f, slot_b, 8 * r, 8, h)
    high = gi % 2 == 0
    row0 = jnp.where(high, 8, 0)
    bit = jnp.where(even, 1, 0)
    for q in range(4):
        slot = jnp.clip(bit + 2 * q + off, 0, 9)
        for h in range(2):
            groups = slab_groups(
                lambda f: old_slice(fields, f, slot, row0, 8, h), high, sub
            )
            for g in range(4):
                ra[24 + (g * 4 + q) * 2 + h] = groups[g]
    top = jnp.zeros((8, 128), F32)
    for s in range(10):
        level = levels[jnp.minimum(start + s, 1023)]
        inv = jnp.where(s < count, jnp.left_shift(1, level), 0).astype(F32)
        part = jnp.zeros((8, 128), F32)
        for r in range(2):
            for h in range(2):
                u = [jnp.abs(vel[a, s, pl.ds(8 * r, 8), halves(h)]) for a in range(3)]
                part = jnp.maximum(part, u[0] + u[1] + u[2])
        top = jnp.maximum(top, part * inv)
    ra[56] = top
    peak[0] = top


def second_kernel(vol, vel, src, prev, bounds, peak, ra, rb, x8, x9, ib, peak_out):
    d, tree, gi, gj, gk = where_am_i()
    sub, lane = iotas()
    fields = (vol, vel, src, prev)
    off = 8 * d - bounds[d]
    even = d % 2 == 0
    missing_first = bounds[d] == 8 * d + 1
    missing_last = bounds[d + 1] == 8 * d + 7
    high = gi % 2 == 1
    row0 = jnp.where(high, 8, 0)
    block = jnp.where(high, 2, 0)
    bit = jnp.where(even, 0, 1)
    for q in range(4):
        slot = jnp.clip(bit + 2 * q + off, 0, 9)
        for h in range(2):

            def get(f):
                x = old_slice(fields, f, slot, row0, 8, h)
                if q == 0:
                    x = jnp.where(even & missing_first, rb[f * 4 + block + h], x)
                if q == 3:
                    x = jnp.where(jnp.logical_not(even) & missing_last, rb[f * 4 + block + h], x)
                return x

            groups = slab_groups(get, high, sub)
            for g in range(4):
                ib[(g * 4 + q) * 2 + h] = groups[g]
    peak_out[0] = jnp.maximum(jnp.maximum(peak[0], ra[56]), jnp.maximum(x8[0], x9[0]))


def gather_kernel(vol, vel, src, prev, bounds, ra, rb, ext, ia):
    d, tree, gi, gj, gk = where_am_i()
    sub, lane = iotas()
    fields = (vol, vel, src, prev)
    off = 8 * d - bounds[d]
    even = d % 2 == 0
    missing_first = bounds[d] == 8 * d + 1
    missing_last = bounds[d + 1] == 8 * d + 7
    for t in range(8):
        slot = jnp.clip(t + off, 0, 9)
        bj, bk = (t >> 1) & 1, (t >> 2) & 1
        row0 = 16 * ((t & 1) ^ tree)
        for f in range(6):
            for r in range(2):
                for h in range(2):
                    x = old_slice(fields, f, slot, 8 * r, 8, h)
                    n = f * 4 + r * 2 + h
                    if t == 0:
                        x = jnp.where(missing_first, jnp.where(even, rb[n], ra[n]), x)
                    if t == 7:
                        x = jnp.where(missing_last, jnp.where(even, ra[n], rb[n]), x)
                    ext[f, 2 * bj + h, bk, pl.ds(pl.multiple_of(row0 + 8 * r, 8), 8), :] = x
    high = gi % 2 == 1
    row0 = jnp.where(high, 8, 0)
    slot_a = jnp.where(even, 8 + off, 0)
    sent_first = even & (bounds[d + 1] == 8 * d + 9)
    sent_last = jnp.logical_not(even) & (bounds[d] == 8 * d - 1)
    for q in range(4):
        for h in range(2):
            if q in (0, 3):
                groups = slab_groups(
                    lambda f: old_slice(fields, f, slot_a, row0, 8, h), high, sub
                )
            for g in range(4):
                n = (g * 4 + q) * 2 + h
                x = ra[24 + n]
                if q == 0:
                    x = jnp.where(sent_first, groups[g], x)
                if q == 3:
                    x = jnp.where(sent_last, groups[g], x)
                ia[n] = x


def make_block(ext, ia, ib, gi, sub):
    first_high = gi % 2 == 0

    def pair(g, jq, kt):
        n = (g * 4 + jq // 2 + 2 * kt) * 2 + jq % 2
        a, b = ia[n], ib[n]
        return jnp.where(first_high, a, b), jnp.where(first_high, b, a)

    def rows(f, jq, kt, b):
        if b < 4:
            return ext[f, jq, kt, pl.ds(8 * b, 8), :]
        if f == 0:
            return pair(0, jq, kt)[b - 4]
        hi, lo = pair((1, 1, 2, 2, 3, 3)[f], jq, kt)
        if f in (3, 4):
            return rs(jnp.where(sub < 4, lo, hi), 4)
        return jnp.where(sub < 4, hi, lo)

    return rows, pair


def third_kernel(ext, ia, ib, peak, xa, xb, xc, ja, jb, peak_out):
    d, tree, gi, gj, gk = where_am_i()
    sub, lane = iotas()
    rows, _ = make_block(ext, ia, ib, gi, sub)
    even = gj % 2 == 0

    def pack(jq, kt, g, b):
        if g == 0:
            return rows(0, jq, kt, b)
        if g == 1:
            return rows(2, jq, kt, b)
        fa, fb = ((1, 3), (5, 4))[g - 2]
        nat = lane < 64 if jq == 0 else lane >= 64
        return jnp.where(nat, rows(fa, jq, kt, b), rl(rows(fb, jq, kt, b), 64))

    for g in range(4):
        for kt in range(2):
            for b in range(6 if g == 0 else 5):
                n = kt * 6 + b if g == 0 else 12 + ((g - 1) * 2 + kt) * 5 + b
                lo, hi = pack(0, kt, g, b), pack(3, kt, g, b)
                ja[n] = jnp.where(even, hi, lo)
                jb[n] = jnp.where(even, lo, hi)
    top = jnp.maximum(jnp.maximum(peak[0], xa[0]), jnp.maximum(xb[0], xc[0]))
    ja[42] = top
    peak_out[0] = top


def make_wide(rows, ja, jb, gj):
    first_high = gj % 2 == 0

    def wide(f, jq, kt, b):
        if jq < 4:
            return rows(f, jq, kt, b)
        if f == 0:
            n = kt * 6 + b
        else:
            n = 12 + ((1, 1, 0, 1, 2, 2)[f] * 2 + kt) * 5 + b
        if jq == 4:
            x = jnp.where(first_high, ja[n], jb[n])
        else:
            x = jnp.where(first_high, jb[n], ja[n])
        return rl(x, 64) if f in (3, 4) else x

    return wide


def fourth_kernel(ext, ia, ib, ja, jb, peak, xa, xb, ka, kb):
    d, tree, gi, gj, gk = where_am_i()
    sub, lane = iotas()
    rows, _ = make_block(ext, ia, ib, gi, sub)
    wide = make_wide(rows, ja, jb, gj)
    even = gk % 2 == 0
    near = lane % 16 < 8
    small = lane % 8 < 4

    def squeeze(f, jt, kt, b):
        first, last = wide(f, 2 * jt, kt, b), wide(f, 2 * jt + 1, kt, b)
        if kt == 0:
            return jnp.where(near, first, rl(last, 8))
        return jnp.where(near, rl(first, -8), last)

    def pack(jt, kt, g, b):
        if g == 0:
            return squeeze(0, jt, kt, b)
        if g == 1:
            return squeeze(3, jt, kt, b)
        fa, fb = ((1, 2), (5, 4))[g - 2]
        one, two = squeeze(fa, jt, kt, b), squeeze(fb, jt, kt, b)
        if kt == 0:
            return jnp.where(small, one, rl(two, 4))
        return jnp.where(small, rl(two, -4), one)

    for g in range(4):
        for jt in range(3):
            for b in range(6 if g == 0 else 5):
                n = jt * 6 + b if g == 0 else 18 + ((g - 1) * 3 + jt) * 5 + b
                lo, hi = pack(jt, 0, g, b), pack(jt, 1, g, b)
                ka[n] = jnp.where(even, hi, lo)
                kb[n] = jnp.where(even, lo, hi)
    ka[63] = jnp.maximum(jnp.maximum(peak[0], ja[42]), jnp.maximum(xa[0], xb[0]))


def coefficient_kernel(neighbours, levels, refine, out, table, ratio):
    d, tree, gi, gj, gk = where_am_i()
    sub, lane = iotas()
    for n in range(7):
        ratio[n] = 2.0 / (1.0 + 2.0 ** (n - 3))

    def one(pos, carry):
        ip, jp, kp = pos >> 4, (pos >> 2) & 3, pos & 3
        x = 2 * gi + jnp.where(ip == 3, -1, ip)
        y = 2 * gj + jnp.where(jp == 3, -1, jp)
        z = 2 * gk + jnp.where(kp == 3, -1, kp)
        inside = (x >= 0) & (x < 16) & (y >= 0) & (y < 8) & (z >= 0) & (z < 8)
        upper = x >= 8
        lx = jnp.where(upper, 15 - x, x)
        code = jnp.where(upper, 512, 0)
        for bit in range(3):
            for axis, v in enumerate((lx, y, z)):
                code = code | (((v >> bit) & 1) << (3 * bit + axis))
        code = jnp.where(inside, code, 0)
        level = levels[code]
        depth = level + refine[code]
        for f in range(6):
            p = neighbours[code * 6 + f]
            opened = inside & (p >= 0)
            safe = jnp.maximum(p, 0)
            other = levels[safe] + refine[safe]
            table[f * 64 + pos] = jnp.where(opened, 1.0, 0.0)
            table[(6 + f) * 64 + pos] = jnp.where(opened, ratio[depth - other + 3], 1.0)
        table[12 * 64 + pos] = jnp.left_shift(1, level).astype(F32)
        table[13 * 64 + pos] = jnp.left_shift(1, 6 - 2 * depth).astype(F32) * (2.0 / 64.0)
        return carry

    lax.fori_loop(0, 64, one, 0)

    def expand(step, carry):
        item, jp = step >> 2, step & 3
        base = item * 64 + jp * 4
        vals = {}
        for ip in range(4):
            v = [jnp.full((8, 128), table[base + ip * 16 + kp], F32) for kp in range(4)]
            vals[ip] = (v[0], v[1], jnp.where(lane % 16 < 8, v[2], v[3]))
        for kt in range(3):
            mixed = jnp.where(sub < 4, vals[2][kt], vals[3][kt])
            for b, v in enumerate((vals[0][kt], vals[0][kt], vals[1][kt], vals[1][kt], mixed)):
                out[item, jp, kt, pl.ds(8 * b, 8), :] = v
        return carry

    lax.fori_loop(0, 56, expand, 0)


def minmod(a, b):
    return jnp.maximum(jnp.minimum(a, b), 0.0) + jnp.minimum(jnp.maximum(a, b), 0.0)


def face_change(c, up1, up2, dn1, dn2, u, u_up, u_dn):
    upper, lower = up1 - c, c - dn1
    half = 0.5 * minmod(upper, lower)
    half_up = 0.5 * minmod(up2 - up1, upper)
    half_dn = 0.5 * minmod(lower, dn1 - dn2)
    w_up, w_dn = 0.5 * (u + u_up), 0.5 * (u_dn + u)
    flux_up = jnp.maximum(w_up, 0.0) * (c + half) + jnp.minimum(w_up, 0.0) * (up1 - half_up)
    flux_dn = jnp.maximum(w_dn, 0.0) * (dn1 + half_dn) + jnp.minimum(w_dn, 0.0) * (c - half)
    return flux_up - flux_dn


def main_kernel(
    ext, ia, ib, ja, jb, ka, kb, peak, coef, bounds,
    vof, pres, send_a, send_b,
    c48, v48, c40, u1, u2, src, p0, p1, adv, mob, hgt, rhs, wts,
):
    d, tree, gi, gj, gk = where_am_i()
    sub, lane = iotas()
    rows, pair = make_block(ext, ia, ib, gi, sub)
    wide = make_wide(rows, ja, jb, gj)
    near = lane % 16 < 8
    k_even = gk % 2 == 0
    dest = {1: v48, 2: u1, 3: u2, 4: src, 5: p0}

    def put(f, jq, kt, b, x):
        if f == 0:
            c48[jq, kt, pl.ds(8 * b, 8), :] = x
            if b < 4:
                c40[jq, kt, pl.ds(8 * b, 8), :] = x
        else:
            dest[f][jq, kt, pl.ds(8 * b, 8), :] = x

    for f in range(6):
        for b in range(6 if f == 0 else 5):
            for jq in range(6):
                for kt in range(2):
                    if f == 1 and b == 4:
                        if jq < 4:
                            hi, lo = pair(1, jq, kt)
                        else:
                            hi = lo = wide(1, jq, kt, 4)
                        put(f, jq, kt, 4, hi)
                        put(f, jq, kt, 5, lo)
                    else:
                        put(f, jq, kt, b, wide(f, jq, kt, b))
            for jt in range(3):
                if f == 0:
                    n = jt * 6 + b
                else:
                    n = 18 + ((1, 1, 1, 0, 2, 2)[f] * 3 + jt) * 5 + b
                a, e = ka[n], kb[n]
                low_pack = jnp.where(k_even, a, e)
                high_pack = jnp.where(k_even, e, a)
                if f in (2, 4):
                    low_pack, high_pack = rl(low_pack, -4), rl(high_pack, 4)
                first = jnp.where(near, low_pack, rl(high_pack, 8))
                last = jnp.where(near, rl(low_pack, -8), high_pack)
                put(f, 2 * jt, 2, b, first)
                put(f, 2 * jt + 1, 2, b, last)
                if f == 1 and b == 4:
                    put(f, 2 * jt, 2, 5, first)
                    put(f, 2 * jt + 1, 2, 5, last)
    for jq in range(6):
        for kt in range(3):
            c40[jq, kt, pl.ds(32, 8), :] = jnp.where(
                sub < 4, c48[jq, kt, pl.ds(32, 8), :], c48[jq, kt, pl.ds(40, 8), :]
            )

    top = jnp.max(jnp.maximum(peak[63], ka[63]), keepdims=True)
    step = jnp.broadcast_to(CFL / top, (8, 128))
    step = jnp.concatenate([step] * 5, axis=0)

    row = lax.broadcasted_iota(jnp.int32, (40, 128), 0)
    lane5 = lax.broadcasted_iota(jnp.int32, (40, 128), 1)
    k16 = lane5 % 16
    i_top1 = (row == 15) | (row == 31) | (row == 39)
    i_top2 = i_top1 | (row == 14) | (row == 30) | (row == 38)
    i_bot1 = (row == 0) | (row == 16) | (row == 32)
    i_bot2 = i_bot1 | (row == 1) | (row == 17) | (row == 33)
    sub4 = sub < 4

    def tile_j(jq):
        return jnp.where(jq < 4, jq >> 1, jq - 2)

    def wrap(x):
        return jnp.concatenate([x[:32], jnp.where(sub4, x[32:40], x[40:48])], axis=0)

    def k_up(x, nxt, n, m):
        return jnp.where(k16 < 16 - n, rl(x, -n), m * rl(nxt, 16 - n))

    def k_dn(x, prv, n, m):
        return jnp.where(k16 >= n, rl(x, n), m * rl(prv, n - 16))

    def j_up(x, nxt, n):
        return rl(jnp.where(lane5 < 16 * n, nxt, x), -16 * n)

    def j_dn(x, prv, n):
        return rl(jnp.where(lane5 >= 128 - 16 * n, prv, x), 16 * n)

    def advance(jq, carry):
        jt = tile_j(jq)
        jn, jp = lax.rem(jq + 1, 6), lax.rem(jq + 5, 6)
        odd = jq % 2 == 1
        for kt in range(3):
            kn, kp = (kt + 1) % 3, (kt + 2) % 3
            c = c40[jq, kt]
            m_dn, m_up = coef[4, jt, kt], coef[5, jt, kt]
            cn, cp = c40[jq, kn], c40[jq, kp]
            up1, up2 = k_up(c, cn, 1, m_up), k_up(c, cn, 2, m_up)
            dn1, dn2 = k_dn(c, cp, 1, m_dn), k_dn(c, cp, 2, m_dn)
            hgt[jq, kt] = dn2 + dn1 + c + up1 + up2
            u = u2[jq, kt]
            change = face_change(
                c, up1, up2, dn1, dn2, u, k_up(u, u2[jq, kn], 1, m_up), k_dn(u, u2[jq, kp], 1, m_dn)
            )
            m_dn = jnp.where(odd, 1.0, coef[2, jt, kt])
            m_up = jnp.where(odd, coef[3, jt, kt], 1.0)
            up_m1 = jnp.where(lane5 >= 112, m_up, 1.0)
            up_m2 = jnp.where(lane5 >= 96, m_up, 1.0)
            dn_m1 = jnp.where(lane5 < 16, m_dn, 1.0)
            dn_m2 = jnp.where(lane5 < 32, m_dn, 1.0)
            cn, cp = c40[jn, kt], c40[jp, kt]
            u = u1[jq, kt]
            change = change + face_change(
                c, j_up(c, cn, 1) * up_m1, j_up(c, cn, 2) * up_m2,
                j_dn(c, cp, 1) * dn_m1, j_dn(c, cp, 2) * dn_m2,
                u, j_up(u, u1[jn, kt], 1) * up_m1, j_dn(u, u1[jp, kt], 1) * dn_m1,
            )
            m_dn, m_up = coef[0, jt, kt], coef[1, jt, kt]
            up_m1, up_m2 = jnp.where(i_top1, m_up, 1.0), jnp.where(i_top2, m_up, 1.0)
            dn_m1, dn_m2 = jnp.where(i_bot1, m_dn, 1.0), jnp.where(i_bot2, m_dn, 1.0)
            cc, uu = c48[jq, kt], v48[jq, kt]
            change = change + face_change(
                c, wrap(rs(cc, -1)) * up_m1, wrap(rs(cc, -2)) * up_m2,
                wrap(rs(cc, 1)) * dn_m1, wrap(rs(cc, 2)) * dn_m2,
                wrap(uu), wrap(rs(uu, -1)) * up_m1, wrap(rs(uu, 1)) * dn_m1,
            )
            a = jnp.clip(c - step * coef[12, jt, kt] * change, 0.0, 1.0)
            adv[jq, kt] = a
            mob[jq, kt] = 1.0 / (RHO_GAS + (RHO_LIQ - RHO_GAS) * a)
        return carry

    lax.fori_loop(0, 6, advance, 0)

    def weigh(jq, carry):
        jt = tile_j(jq)
        jn, jp = lax.rem(jq + 1, 6), lax.rem(jq + 5, 6)
        odd = jq % 2 == 1
        for kt in range(3):
            kn, kp = (kt + 1) % 3, (kt + 2) % 3
            mi_dn = jnp.where(i_bot1, coef[0, jt, kt], 1.0)
            mi_up = jnp.where(i_top1, coef[1, jt, kt], 1.0)
            at_dn = (lane5 < 16) & jnp.logical_not(odd)
            at_up = (lane5 >= 112) & odd
            mj_dn = jnp.where(at_dn, coef[2, jt, kt], 1.0)
            mj_up = jnp.where(at_up, coef[3, jt, kt], 1.0)
            h = hgt[jq, kt]
            h_up, h_dn = rs(h, -1) * mi_up, rs(h, 1) * mi_dn
            gx, sx = 0.5 * (h_up - h_dn), h_up - 2.0 * h + h_dn
            h_up = j_up(h, hgt[jn, kt], 1) * mj_up
            h_dn = j_dn(h, hgt[jp, kt], 1) * mj_dn
            gy, sy = 0.5 * (h_up - h_dn), h_up - 2.0 * h + h_dn
            gx2, gy2 = gx * gx, gy * gy
            root = lax.rsqrt(1.0 + gx2 + gy2)
            bend = (sx * (1.0 + gy2) + sy * (1.0 + gx2)) * coef[12, jt, kt] * (root * root * root)
            right = src[jq, kt] - SIGMA * bend * adv[jq, kt]
            m = mob[jq, kt]
            mk_dn = jnp.where(k16 < 1, coef[4, jt, kt], 1.0)
            mk_up = jnp.where(k16 >= 15, coef[5, jt, kt], 1.0)
            across = (
                rs(m, 1), rs(m, -1),
                j_dn(m, mob[jp, kt], 1), j_up(m, mob[jn, kt], 1),
                k_dn(m, mob[jq, kp], 1, 1.0), k_up(m, mob[jq, kn], 1, 1.0),
            )
            masks = (mi_dn, mi_up, mj_dn, mj_up, mk_dn, mk_up)
            edges = (i_bot1, i_top1, at_dn, at_up, k16 < 1, k16 >= 15)
            diag = jnp.zeros_like(m)
            parts = []
            for f in range(6):
                w = (m + masks[f] * across[f]) * jnp.where(edges[f], coef[6 + f, jt, kt], 1.0)
                diag = diag + w
                parts.append(w * masks[f])
            inv = 1.0 / diag
            for f in range(6):
                wts[f, jq, kt] = parts[f] * inv
            rhs[jq, kt] = right * coef[13, jt, kt] * inv
        return carry

    lax.fori_loop(0, 6, weigh, 0)

    for sweep in range(SWEEPS):
        old, new = (p0, p1) if sweep % 2 == 0 else (p1, p0)
        last = sweep == SWEEPS - 1

        def relax(jq, carry, old=old, new=new, last=last):
            jn, jp = lax.rem(jq + 1, 6), lax.rem(jq + 5, 6)
            for kt in range(2 if last else 3):
                kn, kp = (kt + 1) % 3, (kt + 2) % 3
                p = old[jq, kt]
                total = wts[0, jq, kt] * rs(p, 1) + wts[1, jq, kt] * rs(p, -1)
                total = total + wts[2, jq, kt] * j_dn(p, old[jp, kt], 1)
                total = total + wts[3, jq, kt] * j_up(p, old[jn, kt], 1)
                total = total + wts[4, jq, kt] * k_dn(p, old[jq, kp], 1, 1.0)
                total = total + wts[5, jq, kt] * k_up(p, old[jq, kn], 1, 1.0)
                new[jq, kt] = total - rhs[jq, kt]
            return carry

        lax.fori_loop(0, 4 if last else 6, relax, 0)
    final = p0 if SWEEPS % 2 == 0 else p1

    start = bounds[d]
    count = bounds[d + 1] - start
    off = 8 * d - start
    vof[...] = jnp.zeros_like(vof)
    pres[...] = jnp.zeros_like(pres)
    even = d % 2 == 0

    def tile_half(ref, t, h):
        row0 = pl.multiple_of(16 * ((t & 1) ^ tree), 16)
        return ref[2 * ((t >> 1) & 1) + h, (t >> 2) & 1, pl.ds(row0, 16), :]

    for t in range(8):
        slot = t + off

        @pl.when((slot >= 0) & (slot < count))
        def _(t=t, slot=slot):
            for h in range(2):
                vof[slot, :, halves(h)] = tile_half(adv, t, h)
                pres[slot, :, halves(h)] = tile_half(final, t, h)

    for h in range(2):
        for n, ref in enumerate((adv, final)):
            low, high = tile_half(ref, 0, h), tile_half(ref, 7, h)
            send_a[n, :, halves(h)] = jnp.where(even, high, low)
            send_b[n, :, halves(h)] = jnp.where(even, low, high)


VM = pl.BlockSpec(memory_space=pltpu.VMEM)
SM = pl.BlockSpec(memory_space=pltpu.SMEM)


def blocks(n):
    return jax.ShapeDtypeStruct((n, 8, 128), F32)


def call(kernel, specs, outs, args, scratch=(), cost=1):
    return pl.pallas_call(
        kernel,
        out_shape=outs,
        in_specs=specs,
        out_specs=jax.tree.map(lambda _: VM, outs),
        scratch_shapes=list(scratch),
        compiler_params=pltpu.CompilerParams(vmem_limit_bytes=48 * 1024 * 1024),
        cost_estimate=pl.CostEstimate(
            flops=cost * 1000000, bytes_accessed=cost * 1000000, transcendentals=0
        ),
    )(*args)


def local(volume, velocity, source, pressure_prev, neighbours, levels, refine, bounds_old, bounds_new):
    d = lax.axis_index("row") * 16 + lax.axis_index("col")
    old = (volume, velocity, source, pressure_prev)
    one = blocks(1)
    ra, rb, peak = call(
        first_kernel, [VM] * 4 + [SM] * 2, (blocks(57), blocks(24), one), (*old, levels, bounds_old)
    )
    x8, x9 = send(peak, flip_pairs(8)), send(peak, flip_pairs(9))
    rb, ra = send(rb, ODD_PAIRS), send(ra, EVEN_PAIRS)
    coef = call(
        coefficient_kernel,
        [SM] * 3,
        jax.ShapeDtypeStruct((14, 4, 3, 40, 128), F32),
        (neighbours.reshape(-1), levels, refine),
        [pltpu.SMEM((14 * 64,), F32), pltpu.SMEM((7,), F32)],
        5,
    )
    ib, peak = call(
        second_kernel,
        [VM] * 4 + [SM] + [VM] * 5,
        (blocks(32), one),
        (*old, bounds_old, peak, ra, rb, x8, x9),
    )
    xs = [send(peak, flip_pairs(b)) for b in (16, 64, 80)]
    ib = send(ib, axis_pairs(0, 1))
    ext, ia = call(
        gather_kernel,
        [VM] * 4 + [SM] + [VM] * 2,
        (jax.ShapeDtypeStruct((6, 4, 2, 32, 128), F32), blocks(32)),
        (*old, bounds_old, ra, rb),
    )
    ja, jb, peak = call(
        third_kernel,
        [VM] * 7,
        (blocks(43), blocks(42), one),
        (ext, ia, ib, peak, *xs),
    )
    xs = [send(peak, flip_pairs(b)) for b in (32, 34)]
    ja, jb = send(ja, axis_pairs(1, 0)), send(jb, axis_pairs(1, 1))
    ka, kb = call(
        fourth_kernel,
        [VM] * 8,
        (blocks(64), blocks(63)),
        (ext, ia, ib, ja, jb, peak, *xs),
    )
    peak = ka
    ka, kb = send(ka, axis_pairs(2, 0)), send(kb, axis_pairs(2, 1))
    grid = (6, 3, 40, 128)
    tall = (6, 3, 48, 128)
    vof, pres, sa, sb = call(
        main_kernel,
        [VM] * 9 + [SM],
        (
            jax.ShapeDtypeStruct((10, 16, 256), F32),
            jax.ShapeDtypeStruct((10, 16, 256), F32),
            jax.ShapeDtypeStruct((2, 16, 256), F32),
            jax.ShapeDtypeStruct((2, 16, 256), F32),
        ),
        (ext, ia, ib, ja, jb, ka, kb, peak, coef, bounds_new),
        [pltpu.VMEM(tall, F32)] * 2 + [pltpu.VMEM(grid, F32)] * 10 + [pltpu.VMEM((6, *grid), F32)],
        20,
    )
    sb, sa = send(sb, ODD_PAIRS), send(sa, EVEN_PAIRS)
    even = d % 2 == 0
    low, high = jnp.where(even, sb, sa), jnp.where(even, sa, sb)
    start, stop = bounds_new[d], bounds_new[d + 1]
    slots = jnp.arange(10, dtype=jnp.int32)
    at_low = ((slots == 0) & (start == 8 * d - 1))[:, None, None]
    at_high = ((slots == 8 * d + 8 - start) & (stop == 8 * d + 9))[:, None, None]
    outs = [
        jnp.where(at_low, low[n][None], jnp.where(at_high, high[n][None], x))
        for n, x in enumerate((vof, pres))
    ]
    return tuple(outs)


def solution(mesh):
    in_specs = (
        P(AXES, None, None),
        P(None, AXES, None, None),
        P(AXES, None, None),
        P(AXES, None, None),
        P(),
        P(),
        P(),
        P(),
        P(),
    )
    out_specs = (P(AXES, None, None), P(AXES, None, None))
    return jax.shard_map(local, mesh=mesh, in_specs=in_specs, out_specs=out_specs, check_vma=False)
```

profile of v0, /device:TPU:1, one launch (start us, length us, event | category | flops | bytes accessed | tf_op | source)
XLA Modules:
  0.0 81.3 jit_solution(11894639504432389822)
XLA Ops:
  0.6 1.0 %copy-done = f32[3,10,16,256]{3,2,1,0:T(8,128)S(1)} copy-done((f32[3,10,16,256]{3,2,1,0:T(8,128)S(1)}, f32[3,10,16,256]{3,2,1,0:T(8,128)}, u32[]{:S(2)}) %copy-start) | copy-done | bytes 491544
  1.7 0.9 %copy-done.1 = f32[10,16,256]{2,1,0:T(8,128)S(1)} copy-done((f32[10,16,256]{2,1,0:T(8,128)S(1)}, f32[10,16,256]{2,1,0:T(8,128)}, u32[]{:S(2)}) %copy-start.1) | copy-done | bytes 163864
  2.6 0.9 %copy-done.2 = f32[10,16,256]{2,1,0:T(8,128)S(1)} copy-done((f32[10,16,256]{2,1,0:T(8,128)S(1)}, f32[10,16,256]{2,1,0:T(8,128)}, u32[]{:S(2)}) %copy-start.2) | copy-done | bytes 163864
  3.5 0.9 %copy-done.3 = f32[10,16,256]{2,1,0:T(8,128)S(1)} copy-done((f32[10,16,256]{2,1,0:T(8,128)S(1)}, f32[10,16,256]{2,1,0:T(8,128)}, u32[]{:S(2)}) %copy-start.3) | copy-done | bytes 163864
  6.5 2.1 %collective-permute-start = (f32[57,8,128]{2,1,0:T(8,128)S(1)}, f32[57,8,128]{2,1,0:T(8,128)S(1)}, u32[]{:S(2)}, u32[]{:S(2)}) collective-permute-start(f32[57,8,128]{2,1,0:T(8,128)S(1)} %get-tuple-element.18), channel_id=1, source_target_pairs={{0,1},{1,0},{2,3},{3,2},{4,5},{5,4},{6,7},{7,6},{8,9},{9,8},{10,11... | collective-permute-start | bytes 700424 | tf_op jit(solution)/shard_map/ppermute | solution.py:49
  8.6 7.0 %collective-permute-start.1 = (f32[24,8,128]{2,1,0:T(8,128)S(1)}, f32[24,8,128]{2,1,0:T(8,128)S(1)}, u32[]{:S(2)}, u32[]{:S(2)}) collective-permute-start(f32[24,8,128]{2,1,0:T(8,128)S(1)} %get-tuple-element.19), channel_id=1, source_target_pairs={{1,2},{2,1},{3,4},{4,3},{5,6},{6,5},{7,8},{8,7},{9,10},{10,9},{11,... | collective-permute-start | bytes 294920 | tf_op jit(solution)/shard_map/ppermute | solution.py:49
  15.8 4.2 %collective-permute-done.2.x8 = f32[1,8,128]{2,1,0:T(8,128)S(1)} collective-permute-done((f32[1,8,128]{2,1,0:T(8,128)S(1)}, f32[1,8,128]{2,1,0:T(8,128)S(1)}, u32[]{:S(2)}, u32[]{:S(2)}) %collective-permute-start.2) | collective-permute-done | bytes 4128 | tf_op jit(solution)/shard_map/ppermute | solution.py:49
  22.0 3.7 %collective-permute-start.4 = (f32[32,8,128]{2,1,0:T(8,128)S(1)}, f32[32,8,128]{2,1,0:T(8,128)S(1)}, u32[]{:S(2)}, u32[]{:S(2)}) collective-permute-start(f32[32,8,128]{2,1,0:T(8,128)S(1)} %get-tuple-element.23), channel_id=1, source_target_pairs={{0,64},{1,8},{2,66},{3,10},{4,68},{5,12},{6,70},{7,14},{8,1},{9,73... | collective-permute-start | bytes 393224 | tf_op jit(solution)/shard_map/ppermute | solution.py:49
  25.6 2.4 %collective-permute-start.5 = (f32[1,8,128]{2,1,0:T(8,128)S(1)}, f32[1,8,128]{2,1,0:T(8,128)S(1)}, u32[]{:S(2)}, u32[]{:S(2)}) collective-permute-start(f32[1,8,128]{2,1,0:T(8,128)S(1)} %get-tuple-element.24.peak), channel_id=1, source_target_pairs={{0,16},{1,17},{2,18},{3,19},{4,20},{5,21},{6,22},{7,23},{8,24},{9,... | collective-permute-start | bytes 12296 | tf_op jit(solution)/shard_map/ppermute | solution.py:49
  28.0 3.1 %collective-permute-start.7 = (f32[1,8,128]{2,1,0:T(8,128)S(1)}, f32[1,8,128]{2,1,0:T(8,128)S(1)}, u32[]{:S(2)}, u32[]{:S(2)}) collective-permute-start(f32[1,8,128]{2,1,0:T(8,128)S(1)} %get-tuple-element.24.peak), channel_id=1, source_target_pairs={{0,80},{1,81},{2,82},{3,83},{4,84},{5,85},{6,86},{7,87},{8,88},{9,... | collective-permute-start | bytes 12296 | tf_op jit(solution)/shard_map/ppermute | solution.py:49
  33.4 3.1 %collective-permute-start.9 = (f32[42,8,128]{2,1,0:T(8,128)S(1)}, f32[42,8,128]{2,1,0:T(8,128)S(1)}, u32[]{:S(2)}, u32[]{:S(2)}) collective-permute-start(f32[42,8,128]{2,1,0:T(8,128)S(1)} %get-tuple-element.26), channel_id=1, source_target_pairs={{0,18},{1,19},{2,16},{3,17},{4,22},{5,23},{6,20},{7,21},{8,26},{9,... | collective-permute-start | bytes 516104 | tf_op jit(solution)/shard_map/ppermute | solution.py:49
  36.5 0.8 collective-permute-start.10
  37.2 0.9 %collective-permute-start.11 = (f32[1,8,128]{2,1,0:T(8,128)S(1)}, f32[1,8,128]{2,1,0:T(8,128)S(1)}, u32[]{:S(2)}, u32[]{:S(2)}) collective-permute-start(f32[1,8,128]{2,1,0:T(8,128)S(1)} %get-tuple-element.27.peak), channel_id=1, source_target_pairs={{0,34},{1,35},{2,32},{3,33},{4,38},{5,39},{6,36},{7,37},{8,42},{9,... | collective-permute-start | bytes 12296 | tf_op jit(solution)/shard_map/ppermute | solution.py:49
  38.2 1.1 %collective-permute-done.10.xa = f32[1,8,128]{2,1,0:T(8,128)S(1)} collective-permute-done((f32[1,8,128]{2,1,0:T(8,128)S(1)}, f32[1,8,128]{2,1,0:T(8,128)S(1)}, u32[]{:S(2)}, u32[]{:S(2)}) %collective-permute-start.10) | collective-permute-done | bytes 4128 | tf_op jit(solution)/shard_map/ppermute | solution.py:49
  39.2 5.0 %collective-permute-done.11.xb = f32[1,8,128]{2,1,0:T(8,128)S(1)} collective-permute-done((f32[1,8,128]{2,1,0:T(8,128)S(1)}, f32[1,8,128]{2,1,0:T(8,128)S(1)}, u32[]{:S(2)}, u32[]{:S(2)}) %collective-permute-start.11) | collective-permute-done | bytes 4128 | tf_op jit(solution)/shard_map/ppermute | solution.py:49
  44.4 3.2 %shard_map.108 = (f32[64,8,128]{2,1,0:T(8,128)S(1)}, f32[63,8,128]{2,1,0:T(8,128)S(1)}) custom-call(f32[6,4,2,32,128]{4,3,2,1,0:T(8,128)S(1)} %get-tuple-element.20.ext, f32[32,8,128]{2,1,0:T(8,128)S(1)} %get-tuple-element.21.ia, f32[32,8,128]{2,1,0:T(8,128)S(1)} %collective-permute-done.4.ib, f32[43,8,128]{2,1,0:T(8,128)S(1)} %collective-permute-done.8.ja, ...), custom_call_target="tpu_custom_call" | custom-call | flops 1000000 | bytes 1000000 | tf_op jit(solution)/shard_map/pallas_call | solution.py:617
  47.6 0.8 collective-permute-start.12
  48.3 1.6 %collective-permute-start.13 = (f32[63,8,128]{2,1,0:T(8,128)S(1)}, f32[63,8,128]{2,1,0:T(8,128)S(1)}, u32[]{:S(2)}, u32[]{:S(2)}) collective-permute-start(f32[63,8,128]{2,1,0:T(8,128)S(1)} %get-tuple-element.29), channel_id=1, source_target_pairs={{0,36},{1,37},{2,38},{3,39},{4,32},{5,33},{6,34},{7,35},{8,44},{9,... | collective-permute-start | bytes 774152 | tf_op jit(solution)/shard_map/ppermute | solution.py:49
  53.1 5.8 %shard_map.109.coef = f32[14,4,3,40,128]{4,3,2,1,0:T(8,128)S(1)} custom-call(s32[6144]{0:T(1024)S(1)} %reshape.17.neighbours, s32[1024]{0:T(1024)S(1)} %copy-done.5, s32[1024]{0:T(1024)S(1)} %copy-done.8), custom_call_target="tpu_custom_call" | custom-call | flops 5000000 | bytes 5000000 | tf_op jit(solution)/shard_map/pallas_call | solution.py:617
  58.9 2.2 %collective-permute-done.13.kb = f32[63,8,128]{2,1,0:T(8,128)S(1)} collective-permute-done((f32[63,8,128]{2,1,0:T(8,128)S(1)}, f32[63,8,128]{2,1,0:T(8,128)S(1)}, u32[]{:S(2)}, u32[]{:S(2)}) %collective-permute-start.13) | collective-permute-done | bytes 258080 | tf_op jit(solution)/shard_map/ppermute | solution.py:49
  61.0 10.6 %shard_map.110 = (f32[10,16,256]{2,1,0:T(8,128)S(1)}, f32[10,16,256]{2,1,0:T(8,128)S(1)}, f32[2,16,256]{2,1,0:T(8,128)S(1)}, f32[2,16,256]{2,1,0:T(8,128)S(1)}) custom-call(f32[6,4,2,32,128]{4,3,2,1,0:T(8,128)S(1)} %get-tuple-element.20.ext, f32[32,8,128]{2,1,0:T(8,128)S(1)} %get-tuple-element.21.ia, f32[32,8,128]{2,1,0:T(8,128)S(1)} %collective-permute-done.4.ib, ...), custom_call_target="tpu_custom_call" | custom-call | flops 20000000 | bytes 20000000 | tf_op jit(solution)/shard_map/pallas_call | solution.py:617
  71.7 6.0 %collective-permute-start.14 = (f32[2,16,256]{2,1,0:T(8,128)S(1)}, f32[2,16,256]{2,1,0:T(8,128)S(1)}, u32[]{:S(2)}, u32[]{:S(2)}) collective-permute-start(f32[2,16,256]{2,1,0:T(8,128)S(1)} %get-tuple-element.30), channel_id=1, source_target_pairs={{1,2},{2,1},{3,4},{4,3},{5,6},{6,5},{7,8},{8,7},{9,10},{10,9},{11,... | collective-permute-start | bytes 98312 | tf_op jit(solution)/shard_map/ppermute | solution.py:49
  77.8 2.5 %collective-permute-done.14 = f32[2,16,256]{2,1,0:T(8,128)S(1)} collective-permute-done((f32[2,16,256]{2,1,0:T(8,128)S(1)}, f32[2,16,256]{2,1,0:T(8,128)S(1)}, u32[]{:S(2)}, u32[]{:S(2)}) %collective-permute-start.14) | collective-permute-done | bytes 32800 | tf_op jit(solution)/shard_map/ppermute | solution.py:49
  80.5 0.8 %select_select_fusion = (f32[10,16,256]{2,1,0:T(8,128)}, f32[10,16,256]{2,1,0:T(8,128)}) fusion(f32[10,16,256]{2,1,0:T(8,128)S(1)} %get-tuple-element.33, f32[16,256]{1,0:T(8,128)S(1)} %get-tuple-element.38, f32[16,256]{1,0:T(8,128)S(1)} %get-tuple-element.45, pred[10]{0:T(512)(128)(4,1)S(1)} %get-tuple-element.46, pred[10]{0:T(512)(128)(4,1)S(1)} %get-tuple-element.47, ...), kind=kLoop, calls=%fused_computation | loop fusion | flops 163840 | bytes 720916 | tf_op jit(solution)/shard_map/jit(_where)/select_n | solution.py:700
  (44 shorter events, 8.2 us)
Async XLA Ops:
  0.6 1.0 %copy-start = (f32[3,10,16,256]{3,2,1,0:T(8,128)S(1)}, f32[3,10,16,256]{3,2,1,0:T(8,128)}, u32[]{:S(2)}) copy-start(f32[3,10,16,256]{3,2,1,0:T(8,128)} %vel.5) | copy-start | bytes 1474564
  1.7 0.9 %copy-start.1 = (f32[10,16,256]{2,1,0:T(8,128)S(1)}, f32[10,16,256]{2,1,0:T(8,128)}, u32[]{:S(2)}) copy-start(f32[10,16,256]{2,1,0:T(8,128)} %vol.5) | copy-start | bytes 491524
  2.6 0.9 %copy-start.2 = (f32[10,16,256]{2,1,0:T(8,128)S(1)}, f32[10,16,256]{2,1,0:T(8,128)}, u32[]{:S(2)}) copy-start(f32[10,16,256]{2,1,0:T(8,128)} %src.5) | copy-start | bytes 491524
  3.5 0.9 %copy-start.3 = (f32[10,16,256]{2,1,0:T(8,128)S(1)}, f32[10,16,256]{2,1,0:T(8,128)}, u32[]{:S(2)}) copy-start(f32[10,16,256]{2,1,0:T(8,128)} %prev.5) | copy-start | bytes 491524
  5.8 44.2 %copy-start.10 = (s32[1024,6]{0,1:T(8,128)S(1)}, s32[1024,6]{0,1:T(8,128)}, u32[]{:S(2)}) copy-start(s32[1024,6]{0,1:T(8,128)} %param.13) | copy-start | bytes 73732
  5.8 44.7 %copy-start.9 = (s32[129]{0:T(256)S(1)}, s32[129]{0:T(256)}, u32[]{:S(2)}) copy-start(s32[129]{0:T(256)} %bounds.7) | copy-start | bytes 1552
  5.8 47.3 %copy-start.5 = (s32[1024]{0:T(1024)S(1)}, s32[1024]{0:T(1024)}, u32[]{:S(2)}) copy-start(s32[1024]{0:T(1024)} %levels.3) | copy-start | bytes 12292
  5.8 47.3 %copy-start.8 = (s32[1024]{0:T(1024)S(1)}, s32[1024]{0:T(1024)}, u32[]{:S(2)}) copy-start(s32[1024]{0:T(1024)} %refine.1) | copy-start | bytes 12292
  6.5 14.2 %collective-permute-start = (f32[57,8,128]{2,1,0:T(8,128)S(1)}, f32[57,8,128]{2,1,0:T(8,128)S(1)}, u32[]{:S(2)}, u32[]{:S(2)}) collective-permute-start(f32[57,8,128]{2,1,0:T(8,128)S(1)} %get-tuple-element.18), channel_id=1, source_target_pairs={{0,1},{1,0},{2,3},{3,2},{4,5},{5,4},{6,7},{7,6},{8,9},{9,8},{10,11... | collective-permute-start | bytes 700424 | tf_op jit(solution)/shard_map/ppermute | solution.py:49
  8.6 12.0 %collective-permute-start.1 = (f32[24,8,128]{2,1,0:T(8,128)S(1)}, f32[24,8,128]{2,1,0:T(8,128)S(1)}, u32[]{:S(2)}, u32[]{:S(2)}) collective-permute-start(f32[24,8,128]{2,1,0:T(8,128)S(1)} %get-tuple-element.19), channel_id=1, source_target_pairs={{1,2},{2,1},{3,4},{4,3},{5,6},{6,5},{7,8},{8,7},{9,10},{10,9},{11,... | collective-permute-start | bytes 294920 | tf_op jit(solution)/shard_map/ppermute | solution.py:49
  15.6 4.4 %collective-permute-start.2 = (f32[1,8,128]{2,1,0:T(8,128)S(1)}, f32[1,8,128]{2,1,0:T(8,128)S(1)}, u32[]{:S(2)}, u32[]{:S(2)}) collective-permute-start(f32[1,8,128]{2,1,0:T(8,128)S(1)} %get-tuple-element.22.peak), channel_id=1, source_target_pairs={{0,8},{1,9},{2,10},{3,11},{4,12},{5,13},{6,14},{7,15},{8,0},{9,1},... | collective-permute-start | bytes 12296 | tf_op jit(solution)/shard_map/ppermute | solution.py:49
  15.7 4.9 %collective-permute-start.3 = (f32[1,8,128]{2,1,0:T(8,128)S(1)}, f32[1,8,128]{2,1,0:T(8,128)S(1)}, u32[]{:S(2)}, u32[]{:S(2)}) collective-permute-start(f32[1,8,128]{2,1,0:T(8,128)S(1)} %get-tuple-element.22.peak), channel_id=1, source_target_pairs={{0,9},{1,8},{2,11},{3,10},{4,13},{5,12},{6,15},{7,14},{8,1},{9,0},... | collective-permute-start | bytes 12296 | tf_op jit(solution)/shard_map/ppermute | solution.py:49
  22.0 10.8 %collective-permute-start.4 = (f32[32,8,128]{2,1,0:T(8,128)S(1)}, f32[32,8,128]{2,1,0:T(8,128)S(1)}, u32[]{:S(2)}, u32[]{:S(2)}) collective-permute-start(f32[32,8,128]{2,1,0:T(8,128)S(1)} %get-tuple-element.23), channel_id=1, source_target_pairs={{0,64},{1,8},{2,66},{3,10},{4,68},{5,12},{6,70},{7,14},{8,1},{9,73... | collective-permute-start | bytes 393224 | tf_op jit(solution)/shard_map/ppermute | solution.py:49
  25.6 6.2 %collective-permute-start.5 = (f32[1,8,128]{2,1,0:T(8,128)S(1)}, f32[1,8,128]{2,1,0:T(8,128)S(1)}, u32[]{:S(2)}, u32[]{:S(2)}) collective-permute-start(f32[1,8,128]{2,1,0:T(8,128)S(1)} %get-tuple-element.24.peak), channel_id=1, source_target_pairs={{0,16},{1,17},{2,18},{3,19},{4,20},{5,21},{6,22},{7,23},{8,24},{9,... | collective-permute-start | bytes 12296 | tf_op jit(solution)/shard_map/ppermute | solution.py:49
  28.0 4.0 %collective-permute-start.6 = (f32[1,8,128]{2,1,0:T(8,128)S(1)}, f32[1,8,128]{2,1,0:T(8,128)S(1)}, u32[]{:S(2)}, u32[]{:S(2)}) collective-permute-start(f32[1,8,128]{2,1,0:T(8,128)S(1)} %get-tuple-element.24.peak), channel_id=1, source_target_pairs={{0,64},{1,65},{2,66},{3,67},{4,68},{5,69},{6,70},{7,71},{8,72},{9,... | collective-permute-start | bytes 12296 | tf_op jit(solution)/shard_map/ppermute | solution.py:49
  28.0 4.7 %collective-permute-start.7 = (f32[1,8,128]{2,1,0:T(8,128)S(1)}, f32[1,8,128]{2,1,0:T(8,128)S(1)}, u32[]{:S(2)}, u32[]{:S(2)}) collective-permute-start(f32[1,8,128]{2,1,0:T(8,128)S(1)} %get-tuple-element.24.peak), channel_id=1, source_target_pairs={{0,80},{1,81},{2,82},{3,83},{4,84},{5,85},{6,86},{7,87},{8,88},{9,... | collective-permute-start | bytes 12296 | tf_op jit(solution)/shard_map/ppermute | solution.py:49
  32.8 11.5 %collective-permute-start.8 = (f32[43,8,128]{2,1,0:T(8,128)S(1)}, f32[43,8,128]{2,1,0:T(8,128)S(1)}, u32[]{:S(2)}, u32[]{:S(2)}) collective-permute-start(f32[43,8,128]{2,1,0:T(8,128)S(1)} %get-tuple-element.25), channel_id=1, source_target_pairs={{0,2},{1,3},{2,0},{3,1},{4,6},{5,7},{6,4},{7,5},{8,10},{9,11},{10,... | collective-permute-start | bytes 528392 | tf_op jit(solution)/shard_map/ppermute | solution.py:49
  33.4 10.9 %collective-permute-start.9 = (f32[42,8,128]{2,1,0:T(8,128)S(1)}, f32[42,8,128]{2,1,0:T(8,128)S(1)}, u32[]{:S(2)}, u32[]{:S(2)}) collective-permute-start(f32[42,8,128]{2,1,0:T(8,128)S(1)} %get-tuple-element.26), channel_id=1, source_target_pairs={{0,18},{1,19},{2,16},{3,17},{4,22},{5,23},{6,20},{7,21},{8,26},{9,... | collective-permute-start | bytes 516104 | tf_op jit(solution)/shard_map/ppermute | solution.py:49
  36.5 2.8 %collective-permute-start.10 = (f32[1,8,128]{2,1,0:T(8,128)S(1)}, f32[1,8,128]{2,1,0:T(8,128)S(1)}, u32[]{:S(2)}, u32[]{:S(2)}) collective-permute-start(f32[1,8,128]{2,1,0:T(8,128)S(1)} %get-tuple-element.27.peak), channel_id=1, source_target_pairs={{0,32},{1,33},{2,34},{3,35},{4,36},{5,37},{6,38},{7,39},{8,40},{9,... | collective-permute-start | bytes 12296 | tf_op jit(solution)/shard_map/ppermute | solution.py:49
  37.2 7.0 %collective-permute-start.11 = (f32[1,8,128]{2,1,0:T(8,128)S(1)}, f32[1,8,128]{2,1,0:T(8,128)S(1)}, u32[]{:S(2)}, u32[]{:S(2)}) collective-permute-start(f32[1,8,128]{2,1,0:T(8,128)S(1)} %get-tuple-element.27.peak), channel_id=1, source_target_pairs={{0,34},{1,35},{2,32},{3,33},{4,38},{5,39},{6,36},{7,37},{8,42},{9,... | collective-permute-start | bytes 12296 | tf_op jit(solution)/shard_map/ppermute | solution.py:49
  47.6 13.5 %collective-permute-start.12 = (f32[64,8,128]{2,1,0:T(8,128)S(1)}, f32[64,8,128]{2,1,0:T(8,128)S(1)}, u32[]{:S(2)}, u32[]{:S(2)}) collective-permute-start(f32[64,8,128]{2,1,0:T(8,128)S(1)} %get-tuple-element.28.peak), channel_id=1, source_target_pairs={{0,4},{1,5},{2,6},{3,7},{4,0},{5,1},{6,2},{7,3},{8,12},{9,13},{10,... | collective-permute-start | bytes 786440 | tf_op jit(solution)/shard_map/ppermute | solution.py:49
  48.3 12.7 %collective-permute-start.13 = (f32[63,8,128]{2,1,0:T(8,128)S(1)}, f32[63,8,128]{2,1,0:T(8,128)S(1)}, u32[]{:S(2)}, u32[]{:S(2)}) collective-permute-start(f32[63,8,128]{2,1,0:T(8,128)S(1)} %get-tuple-element.29), channel_id=1, source_target_pairs={{0,36},{1,37},{2,38},{3,39},{4,32},{5,33},{6,34},{7,35},{8,44},{9,... | collective-permute-start | bytes 774152 | tf_op jit(solution)/shard_map/ppermute | solution.py:49
  71.7 8.6 %collective-permute-start.14 = (f32[2,16,256]{2,1,0:T(8,128)S(1)}, f32[2,16,256]{2,1,0:T(8,128)S(1)}, u32[]{:S(2)}, u32[]{:S(2)}) collective-permute-start(f32[2,16,256]{2,1,0:T(8,128)S(1)} %get-tuple-element.30), channel_id=1, source_target_pairs={{1,2},{2,1},{3,4},{4,3},{5,6},{6,5},{7,8},{8,7},{9,10},{10,9},{11,... | collective-permute-start | bytes 98312 | tf_op jit(solution)/shard_map/ppermute | solution.py:49
  77.6 2.8 %collective-permute-start.15 = (f32[2,16,256]{2,1,0:T(8,128)S(1)}, f32[2,16,256]{2,1,0:T(8,128)S(1)}, u32[]{:S(2)}, u32[]{:S(2)}) collective-permute-start(f32[2,16,256]{2,1,0:T(8,128)S(1)} %get-tuple-element.31), channel_id=1, source_target_pairs={{0,1},{1,0},{2,3},{3,2},{4,5},{5,4},{6,7},{7,6},{8,9},{9,8},{10,11... | collective-permute-start | bytes 98312 | tf_op jit(solution)/shard_map/ppermute | solution.py:49
  (3 other events, 2.0 us)
where the time goes:
time: 82.1 us; the launch traced here: 81.3 us
  starting transfers between devices  32.2 us (39%)
  Pallas kernels  21.7 us (26%)
  waiting for transfers between devices  16.8 us (20%)
  local copies, waits for them, and re-layouts  6.99 us (9%)
  between operations  2.78 us (3%)
  other arithmetic  0.85 us (1%)
    ppermute x16, starting transfers between devices, send(): return lax.ppermute(x, AXES, pairs)  32.2 us
    pallas_call x7, Pallas kernels, call(): pl.pallas_call(kernel, out_shape=outs, in_specs=specs, out_specs=jax.tree...  21.7 us
    ppermute x16, waiting for transfers between devices, send(): return lax.ppermute(x, AXES, pairs)  16.8 us
    unnamed x23, local copies, waits for them, and re-layouts  6.05 us
  transfers between devices with their start and end apart: 16, of which 10 were waited for; matrix products, arithmetic and copies ran while one was open for 1% of the time, Pallas kernels for 8%

commit v1 on v0

v1 whole, which is shorter than its diff:
```python
import jax
import jax.numpy as jnp
from jax import lax
from jax.experimental import pallas as pl
from jax.experimental.pallas import tpu as pltpu
from jax.sharding import PartitionSpec as P

SWEEPS = 4
CFL = 0.4
SIGMA = 0.05
RHO_GAS = 0.05
RHO_LIQ = 1.0
AXES = ("row", "col")
DEVS = 128
F32 = jnp.float32


def block_coords(d):
    tree, low = d >> 6, d & 63
    i = (low & 1) | (((low >> 3) & 1) << 1)
    j = ((low >> 1) & 1) | (((low >> 4) & 1) << 1)
    k = ((low >> 2) & 1) | (((low >> 5) & 1) << 1)
    return (7 - i if tree else i), j, k


PLACE = {block_coords(d): d for d in range(DEVS)}


def axis_pairs(axis, odd):
    count = (8, 4, 4)[axis]
    pairs = []
    for d in range(DEVS):
        c = list(block_coords(d))
        step = 1 if (c[axis] % 2 == 0) != bool(odd) else -1
        c[axis] = (c[axis] + step) % count
        pairs.append((d, PLACE[tuple(c)]))
    return pairs


def flip_pairs(bits):
    return [(d, d ^ bits) for d in range(DEVS)]


EVEN_PAIRS = flip_pairs(1)
ODD_PAIRS = [(d, d + 1 if d % 2 else d - 1) for d in range(1, DEVS - 1)]
FAR_PAIRS = [(d, dict(axis_pairs(0, 1))[e]) for d, e in ODD_PAIRS]


def send(x, pairs):
    return lax.ppermute(x, AXES, pairs)


def where_is(d):
    tree = d >> 6
    i = (d & 1) | (((d >> 3) & 1) << 1)
    gi = jnp.where(tree == 1, 7 - i, i)
    gj = ((d >> 1) & 1) | (((d >> 4) & 1) << 1)
    gk = ((d >> 2) & 1) | (((d >> 5) & 1) << 1)
    return tree, gi, gj, gk


def where_am_i():
    d = lax.axis_index("row") * 16 + lax.axis_index("col")
    return d, *where_is(d)


def iotas():
    sub = lax.broadcasted_iota(jnp.int32, (8, 128), 0)
    lane = lax.broadcasted_iota(jnp.int32, (8, 128), 1)
    return sub, lane


def rl(x, shift):
    return pltpu.roll(x, shift % 128, 1)


def rs(x, shift):
    n = x.shape[0]
    return pltpu.roll(x, shift % n, 0)


def halves(h):
    return pl.ds(128 * h, 128)


def old_slice(old, f, slot, start, h):
    return old[f, slot, pl.ds(pl.multiple_of(start, 8), 8), halves(h)]


def slab_groups(get, high, sub):
    nat = (sub >= 4) == high
    return (
        get(0),
        get(1),
        jnp.where(nat, get(2), rs(get(3), 4)),
        jnp.where(nat, get(5), rs(get(4), 4)),
    )


def first_kernel(
    vol, vel, src, prev, levels_in, bounds_in, ra, rb, ib, ic, peak, old, levels, bounds, sems
):
    copies = [
        pltpu.make_async_copy(bounds_in, bounds, sems.at[0]),
        pltpu.make_async_copy(levels_in, levels, sems.at[1]),
        pltpu.make_async_copy(vol, old.at[0], sems.at[2]),
        pltpu.make_async_copy(vel, old.at[pl.ds(1, 3)], sems.at[3]),
        pltpu.make_async_copy(src, old.at[4], sems.at[4]),
        pltpu.make_async_copy(prev, old.at[5], sems.at[5]),
    ]
    for copy in copies:
        copy.start()
    d, tree, gi, gj, gk = where_am_i()
    sub, lane = iotas()
    for copy in copies:
        copy.wait()
    start = bounds[d]
    count = bounds[d + 1] - start
    off = 8 * d - start
    even = d % 2 == 0
    slot_a = jnp.where(even, 8 + off, 0)
    slot_b = jnp.where(even, 0, 8 + off)
    for f in range(6):
        for r in range(2):
            for h in range(2):
                ra[f * 4 + r * 2 + h] = old_slice(old, f, slot_a, 8 * r, h)
                rb[f * 4 + r * 2 + h] = old_slice(old, f, slot_b, 8 * r, h)
    high = gi % 2 == 0
    bit = jnp.where(even, 1, 0)
    for q in range(4):
        for h in range(2):
            slot = jnp.clip(bit + 2 * q + off, 0, 9)
            row0 = jnp.where(high, 8, 0)
            groups = slab_groups(lambda f: old_slice(old, f, slot, row0, h), high, sub)
            for g in range(4):
                ra[24 + (g * 4 + q) * 2 + h] = groups[g]
            slot = jnp.clip(1 - bit + 2 * q + off, 0, 9)
            groups = slab_groups(
                lambda f: old_slice(old, f, slot, 8 - row0, h), jnp.logical_not(high), sub
            )
            for g in range(4):
                ib[(g * 4 + q) * 2 + h] = groups[g]
    other = jnp.where(even, d - 1, d + 1)
    gi_other = where_is(other)[1]
    high = gi_other % 2 == 1
    row0 = jnp.where(high, 8, 0)
    for h in range(2):
        groups = slab_groups(lambda f: old_slice(old, f, slot_b, row0, h), high, sub)
        for g in range(4):
            ic[g * 2 + h] = groups[g]
    top = jnp.zeros((8, 128), F32)
    for s in range(10):
        level = levels[jnp.minimum(start + s, 1023)]
        inv = jnp.where(s < count, jnp.left_shift(1, level), 0).astype(F32)
        part = jnp.zeros((8, 128), F32)
        for r in range(2):
            for h in range(2):
                u = [jnp.abs(old[1 + a, s, pl.ds(8 * r, 8), halves(h)]) for a in range(3)]
                part = jnp.maximum(part, u[0] + u[1] + u[2])
        top = jnp.maximum(top, part * inv)
    ra[56] = top
    peak[0] = top


FLAG_COUNT = 6


def own_kernel(old, bounds, ext, mine, flags):
    d, tree, gi, gj, gk = where_am_i()
    sub, lane = iotas()
    off = 8 * d - bounds[d]
    even = d % 2 == 0
    for t in range(8):
        slot = jnp.clip(t + off, 0, 9)
        bj, bk = (t >> 1) & 1, (t >> 2) & 1
        row0 = 16 * ((t & 1) ^ tree)
        for f in range(6):
            for r in range(2):
                for h in range(2):
                    rows = pl.ds(pl.multiple_of(row0 + 8 * r, 8), 8)
                    ext[f, 2 * bj + h, bk, rows, :] = old_slice(old, f, slot, 8 * r, h)
    high = gi % 2 == 1
    row0 = jnp.where(high, 8, 0)
    slot_a = jnp.where(even, 8 + off, 0)
    for h in range(2):
        groups = slab_groups(lambda f: old_slice(old, f, slot_a, row0, h), high, sub)
        for g in range(4):
            mine[g * 2 + h] = groups[g]
    near_gi = (gi + jnp.where(gi % 2 == 1, 1, 7)) % 8
    upper = near_gi >= 4
    li = jnp.where(upper, 7 - near_gi, near_gi)
    e = (d & 54) | (li & 1) | ((li >> 1) << 3) | jnp.where(upper, 64, 0)
    e_even = e % 2 == 0
    odd, e_odd = jnp.logical_not(even), jnp.logical_not(e_even)
    values = (
        bounds[d] == 8 * d + 1,
        bounds[d + 1] == 8 * d + 7,
        even & (bounds[d + 1] == 8 * d + 9),
        odd & (bounds[d] == 8 * d - 1),
        e_even & (bounds[e] == 8 * e + 1),
        e_odd & (bounds[e + 1] == 8 * e + 7),
    )
    for n, value in enumerate(values):
        flags[n] = jnp.full((8, 128), jnp.where(value, 1.0, 0.0), F32)


def block_kernel(
    own, mine, flags, ra, rb, ib_in, ic, peak, x64, coef, ext, ia, ib, ja, jb, peak_out
):
    d, tree, gi, gj, gk = where_am_i()
    sub, lane = iotas()
    even = d % 2 == 0
    flag = [flags[n] > 0.5 for n in range(FLAG_COUNT)]
    ext[...] = own[...]
    for t, missing in ((0, flag[0]), (7, flag[1])):
        bj, bk = (t >> 1) & 1, (t >> 2) & 1
        row0 = 16 * ((t & 1) ^ tree)
        use_b = even if t == 0 else jnp.logical_not(even)
        for f in range(6):
            for r in range(2):
                for h in range(2):
                    n = f * 4 + r * 2 + h
                    rows = pl.ds(pl.multiple_of(row0 + 8 * r, 8), 8)
                    came = jnp.where(use_b, rb[n], ra[n])
                    ext[f, 2 * bj + h, bk, rows, :] = jnp.where(
                        missing, came, own[f, 2 * bj + h, bk, rows, :]
                    )
    for q in range(4):
        for h in range(2):
            for g in range(4):
                n = (g * 4 + q) * 2 + h
                x, y = ra[24 + n], ib_in[n]
                if q == 0:
                    x = jnp.where(flag[2], mine[g * 2 + h], x)
                    y = jnp.where(flag[4], ic[g * 2 + h], y)
                if q == 3:
                    x = jnp.where(flag[3], mine[g * 2 + h], x)
                    y = jnp.where(flag[5], ic[g * 2 + h], y)
                ia[n] = x
                ib[n] = y
    top = jnp.maximum(peak[0], x64[0])
    pack_j(ext, ia, ib, ja, jb, gi, gj, sub, lane)
    ja[42] = top
    jb[42] = top
    peak_out[0] = top


def make_block(ext, ia, ib, gi, sub):
    first_high = gi % 2 == 0

    def pair(g, jq, kt):
        n = (g * 4 + jq // 2 + 2 * kt) * 2 + jq % 2
        a, b = ia[n], ib[n]
        return jnp.where(first_high, a, b), jnp.where(first_high, b, a)

    def rows(f, jq, kt, b):
        if b < 4:
            return ext[f, jq, kt, pl.ds(8 * b, 8), :]
        if f == 0:
            return pair(0, jq, kt)[b - 4]
        hi, lo = pair((1, 1, 2, 2, 3, 3)[f], jq, kt)
        if f in (3, 4):
            return rs(jnp.where(sub < 4, lo, hi), 4)
        return jnp.where(sub < 4, hi, lo)

    return rows, pair


def pack_j(ext, ia, ib, ja, jb, gi, gj, sub, lane):
    rows, _ = make_block(ext, ia, ib, gi, sub)
    even = gj % 2 == 0

    def pack(jq, kt, g, b):
        if g == 0:
            return rows(0, jq, kt, b)
        if g == 1:
            return rows(2, jq, kt, b)
        fa, fb = ((1, 3), (5, 4))[g - 2]
        nat = lane < 64 if jq == 0 else lane >= 64
        return jnp.where(nat, rows(fa, jq, kt, b), rl(rows(fb, jq, kt, b), 64))

    for g in range(4):
        for kt in range(2):
            for b in range(6 if g == 0 else 5):
                n = kt * 6 + b if g == 0 else 12 + ((g - 1) * 2 + kt) * 5 + b
                lo, hi = pack(0, kt, g, b), pack(3, kt, g, b)
                ja[n] = jnp.where(even, hi, lo)
                jb[n] = jnp.where(even, lo, hi)


def make_wide(rows, ja, jb, gj):
    first_high = gj % 2 == 0

    def wide(f, jq, kt, b):
        if jq < 4:
            return rows(f, jq, kt, b)
        if f == 0:
            n = kt * 6 + b
        else:
            n = 12 + ((1, 1, 0, 1, 2, 2)[f] * 2 + kt) * 5 + b
        if jq == 4:
            x = jnp.where(first_high, ja[n], jb[n])
        else:
            x = jnp.where(first_high, jb[n], ja[n])
        return rl(x, 64) if f in (3, 4) else x

    return wide


def k_place(g, jt, b):
    return jt * 6 + b if g == 0 else 18 + ((g - 1) * 3 + jt) * 5 + b


def pack_k(wide, jt, ka, kb, gk, lane):
    even = gk % 2 == 0
    near = lane % 16 < 8
    small = lane % 8 < 4

    def squeeze(f, kt, b):
        first, last = wide(f, 2 * jt, kt, b), wide(f, 2 * jt + 1, kt, b)
        if kt == 0:
            return jnp.where(near, first, rl(last, 8))
        return jnp.where(near, rl(first, -8), last)

    def pack(kt, g, b):
        if g == 0:
            return squeeze(0, kt, b)
        if g == 1:
            return squeeze(3, kt, b)
        fa, fb = ((1, 2), (5, 4))[g - 2]
        one, two = squeeze(fa, kt, b), squeeze(fb, kt, b)
        if kt == 0:
            return jnp.where(small, one, rl(two, 4))
        return jnp.where(small, rl(two, -4), one)

    for g in range(4):
        for b in range(6 if g == 0 else 5):
            n = k_place(g, jt, b)
            lo, hi = pack(0, g, b), pack(1, g, b)
            ka[n] = jnp.where(even, hi, lo)
            kb[n] = jnp.where(even, lo, hi)


def early_k_kernel(ext, ia, ib, ka, kb):
    d, tree, gi, gj, gk = where_am_i()
    sub, lane = iotas()
    rows, _ = make_block(ext, ia, ib, gi, sub)
    for jt in range(2):
        pack_k(rows, jt, ka, kb, gk, lane)


def late_k_kernel(ka_in, kb_in, ja, jb, peak, x16, ka, kb, peak_out):
    d, tree, gi, gj, gk = where_am_i()
    sub, lane = iotas()
    wide = make_wide(None, ja, jb, gj)
    for jt in range(2):
        for g in range(4):
            for b in range(6 if g == 0 else 5):
                n = k_place(g, jt, b)
                ka[n] = ka_in[n]
                kb[n] = kb_in[n]
    pack_k(wide, 2, ka, kb, gk, lane)
    top = jnp.maximum(jnp.maximum(peak[0], x16[0]), jnp.maximum(ja[42], jb[42]))
    ka[63] = top
    kb[63] = top
    peak_out[0] = top


def coefficient_kernel(neighbours, levels, refine, out, table, ratio):
    d, tree, gi, gj, gk = where_am_i()
    sub, lane = iotas()
    for n in range(7):
        ratio[n] = 2.0 / (1.0 + 2.0 ** (n - 3))

    def one(pos, carry):
        ip, jp, kp = pos >> 4, (pos >> 2) & 3, pos & 3
        x = 2 * gi + jnp.where(ip == 3, -1, ip)
        y = 2 * gj + jnp.where(jp == 3, -1, jp)
        z = 2 * gk + jnp.where(kp == 3, -1, kp)
        inside = (x >= 0) & (x < 16) & (y >= 0) & (y < 8) & (z >= 0) & (z < 8)
        upper = x >= 8
        lx = jnp.where(upper, 15 - x, x)
        code = jnp.where(upper, 512, 0)
        for bit in range(3):
            for axis, v in enumerate((lx, y, z)):
                code = code | (((v >> bit) & 1) << (3 * bit + axis))
        code = jnp.where(inside, code, 0)
        level = levels[code]
        depth = level + refine[code]
        for f in range(6):
            p = neighbours[code * 6 + f]
            opened = inside & (p >= 0)
            safe = jnp.maximum(p, 0)
            other = levels[safe] + refine[safe]
            table[f * 64 + pos] = jnp.where(opened, 1.0, 0.0)
            table[(6 + f) * 64 + pos] = jnp.where(opened, ratio[depth - other + 3], 1.0)
        table[12 * 64 + pos] = jnp.left_shift(1, level).astype(F32)
        table[13 * 64 + pos] = jnp.left_shift(1, 6 - 2 * depth).astype(F32) * (2.0 / 64.0)
        return carry

    lax.fori_loop(0, 64, one, 0)

    def expand(step, carry):
        item, jp = step >> 2, step & 3
        base = item * 64 + jp * 4
        vals = {}
        for ip in range(4):
            v = [jnp.full((8, 128), table[base + ip * 16 + kp], F32) for kp in range(4)]
            vals[ip] = (v[0], v[1], jnp.where(lane % 16 < 8, v[2], v[3]))
        for kt in range(3):
            mixed = jnp.where(sub < 4, vals[2][kt], vals[3][kt])
            for b, v in enumerate((vals[0][kt], vals[0][kt], vals[1][kt], vals[1][kt], mixed)):
                out[item, jp, kt, pl.ds(8 * b, 8), :] = v
        return carry

    lax.fori_loop(0, 56, expand, 0)


def minmod(a, b):
    return jnp.maximum(jnp.minimum(a, b), 0.0) + jnp.minimum(jnp.maximum(a, b), 0.0)


def face_change(c, up1, up2, dn1, dn2, u, u_up, u_dn):
    upper, lower = up1 - c, c - dn1
    half = 0.5 * minmod(upper, lower)
    half_up = 0.5 * minmod(up2 - up1, upper)
    half_dn = 0.5 * minmod(lower, dn1 - dn2)
    w_up, w_dn = 0.5 * (u + u_up), 0.5 * (u_dn + u)
    flux_up = jnp.maximum(w_up, 0.0) * (c + half) + jnp.minimum(w_up, 0.0) * (up1 - half_up)
    flux_dn = jnp.maximum(w_dn, 0.0) * (dn1 + half_dn) + jnp.minimum(w_dn, 0.0) * (c - half)
    return flux_up - flux_dn


def wrap48(x, sub):
    return jnp.concatenate([x[:32], jnp.where(sub < 4, x[32:40], x[40:48])], axis=0)


class Shifts:
    def __init__(self):
        self.sub, self.lane = iotas()
        self.row = lax.broadcasted_iota(jnp.int32, (40, 128), 0)
        self.lane5 = lax.broadcasted_iota(jnp.int32, (40, 128), 1)
        self.k16 = self.lane5 % 16
        row = self.row
        self.i_top1 = (row == 15) | (row == 31) | (row == 39)
        self.i_top2 = self.i_top1 | (row == 14) | (row == 30) | (row == 38)
        self.i_bot1 = (row == 0) | (row == 16) | (row == 32)
        self.i_bot2 = self.i_bot1 | (row == 1) | (row == 17) | (row == 33)

    def wrap(self, x):
        return wrap48(x, self.sub)

    def k_up(self, x, nxt, n, m=None):
        nxt = rl(nxt, 16 - n)
        return jnp.where(self.k16 < 16 - n, rl(x, -n), nxt if m is None else m * nxt)

    def k_dn(self, x, prv, n, m=None):
        prv = rl(prv, n - 16)
        return jnp.where(self.k16 >= n, rl(x, n), prv if m is None else m * prv)

    def j_up(self, x, nxt, n):
        return rl(jnp.where(self.lane5 < 16 * n, nxt, x), -16 * n)

    def j_dn(self, x, prv, n):
        return rl(jnp.where(self.lane5 >= 128 - 16 * n, prv, x), 16 * n)

    def change_ij(self, jq, kt, coef, c40, u1, c48, v48):
        jt = tile_j(jq)
        jn, jp = lax.rem(jq + 1, 6), lax.rem(jq + 5, 6)
        odd = jq % 2 == 1
        lane5 = self.lane5
        c = c40(jq)
        m_dn = jnp.where(odd, 1.0, coef[2, jt, kt])
        m_up = jnp.where(odd, coef[3, jt, kt], 1.0)
        up_m1 = jnp.where(lane5 >= 112, m_up, 1.0)
        up_m2 = jnp.where(lane5 >= 96, m_up, 1.0)
        dn_m1 = jnp.where(lane5 < 16, m_dn, 1.0)
        dn_m2 = jnp.where(lane5 < 32, m_dn, 1.0)
        cn, cp = c40(jn), c40(jp)
        u = u1(jq)
        change = face_change(
            c, self.j_up(c, cn, 1) * up_m1, self.j_up(c, cn, 2) * up_m2,
            self.j_dn(c, cp, 1) * dn_m1, self.j_dn(c, cp, 2) * dn_m2,
            u, self.j_up(u, u1(jn), 1) * up_m1, self.j_dn(u, u1(jp), 1) * dn_m1,
        )
        m_dn, m_up = coef[0, jt, kt], coef[1, jt, kt]
        up_m1, up_m2 = jnp.where(self.i_top1, m_up, 1.0), jnp.where(self.i_top2, m_up, 1.0)
        dn_m1, dn_m2 = jnp.where(self.i_bot1, m_dn, 1.0), jnp.where(self.i_bot2, m_dn, 1.0)
        wrap = self.wrap
        return change + face_change(
            c, wrap(rs(c48, -1)) * up_m1, wrap(rs(c48, -2)) * up_m2,
            wrap(rs(c48, 1)) * dn_m1, wrap(rs(c48, 2)) * dn_m2,
            wrap(v48), wrap(rs(v48, -1)) * up_m1, wrap(rs(v48, 1)) * dn_m1,
        )


def tile_j(jq):
    return jnp.where(jq < 4, jq >> 1, jq - 2)


def early_kernel(ext, ia, ib, ja, jb, coef, c40, u2, src, prs, chg, c48, v48, u1):
    d, tree, gi, gj, gk = where_am_i()
    sh = Shifts()
    sub = sh.sub
    rows, pair = make_block(ext, ia, ib, gi, sub)
    wide = make_wide(rows, ja, jb, gj)
    dest = (c48, v48, u1, u2, src, prs)
    for f in range(6):
        for jq in range(6):
            for kt in range(2):
                for b in range(6 if f == 0 else 5):
                    x = wide(f, jq, kt, b)
                    if f == 1 and b == 4:
                        hi, lo = pair(1, jq, kt) if jq < 4 else (x, x)
                        v48[jq, kt, pl.ds(32, 8), :] = hi
                        v48[jq, kt, pl.ds(40, 8), :] = lo
                    else:
                        dest[f][jq, kt, pl.ds(8 * b, 8), :] = x
                    if f == 0 and b < 4:
                        c40[jq, kt, pl.ds(8 * b, 8), :] = x
                if f == 0:
                    c40[jq, kt, pl.ds(32, 8), :] = jnp.where(
                        sub < 4, c48[jq, kt, pl.ds(32, 8), :], c48[jq, kt, pl.ds(40, 8), :]
                    )

    def step(jq, carry):
        for kt in range(2):
            chg[jq, kt] = sh.change_ij(
                jq, kt, coef, lambda n: c40[n, kt], lambda n: u1[n, kt], c48[jq, kt], v48[jq, kt]
            )
        return carry

    lax.fori_loop(0, 6, step, 0)


def main_kernel(
    c_in, u_in, s_in, p_in, chg, ka, kb, peak, x32, coef,
    out_adv, out_p, send_a, send_b,
    c48, v48, c_k, u1, u2, src, p_k, p0, p1, adv, mob, hgt, rhs, wts,
):
    d, tree, gi, gj, gk = where_am_i()
    sh = Shifts()
    sub, lane, lane5, k16 = sh.sub, sh.lane, sh.lane5, sh.k16
    near = lane % 16 < 8
    k_even = gk % 2 == 0
    dest = (c48, v48, u1, u2, src, p_k)
    for f in range(6):
        for b in range(6 if f == 0 else 5):
            for jt in range(3):
                n = k_place((0, 2, 2, 1, 3, 3)[f], jt, b)
                a, e = ka[n], kb[n]
                low_pack = jnp.where(k_even, a, e)
                high_pack = jnp.where(k_even, e, a)
                if f in (2, 4):
                    low_pack, high_pack = rl(low_pack, -4), rl(high_pack, 4)
                first = jnp.where(near, low_pack, rl(high_pack, 8))
                last = jnp.where(near, rl(low_pack, -8), high_pack)
                for jq, x in ((2 * jt, first), (2 * jt + 1, last)):
                    dest[f][jq, pl.ds(8 * b, 8), :] = x
                    if f == 0 and b < 4:
                        c_k[jq, pl.ds(8 * b, 8), :] = x
                    if f == 1 and b == 4:
                        v48[jq, pl.ds(40, 8), :] = x
    for jq in range(6):
        c_k[jq, pl.ds(32, 8), :] = jnp.where(
            sub < 4, c48[jq, pl.ds(32, 8), :], c48[jq, pl.ds(40, 8), :]
        )

    def c40(jq, kt):
        return c_k[jq] if kt == 2 else c_in[jq, kt]

    def uk(jq, kt):
        return u2[jq] if kt == 2 else u_in[jq, kt]

    top = jnp.maximum(jnp.maximum(peak[0], x32[0]), jnp.maximum(ka[63], kb[63]))
    top = jnp.max(top, keepdims=True)
    step = jnp.broadcast_to(CFL / top, (8, 128))
    step = jnp.concatenate([step] * 5, axis=0)

    def advance(jq, carry):
        jt = tile_j(jq)
        for kt in range(3):
            kn, kp = (kt + 1) % 3, (kt + 2) % 3
            if kt == 2:
                change = sh.change_ij(
                    jq, 2, coef, lambda n: c_k[n], lambda n: u1[n], c48[jq], v48[jq]
                )
            else:
                change = chg[jq, kt]
            c = c40(jq, kt)
            m_dn, m_up = coef[4, jt, kt], coef[5, jt, kt]
            cn, cp = c40(jq, kn), c40(jq, kp)
            up1, up2 = sh.k_up(c, cn, 1, m_up), sh.k_up(c, cn, 2, m_up)
            dn1, dn2 = sh.k_dn(c, cp, 1, m_dn), sh.k_dn(c, cp, 2, m_dn)
            hgt[jq, kt] = dn2 + dn1 + c + up1 + up2
            u = uk(jq, kt)
            u_up, u_dn = sh.k_up(u, uk(jq, kn), 1, m_up), sh.k_dn(u, uk(jq, kp), 1, m_dn)
            change = change + face_change(c, up1, up2, dn1, dn2, u, u_up, u_dn)
            a = jnp.clip(c - step * coef[12, jt, kt] * change, 0.0, 1.0)
            adv[jq, kt] = a
            mob[jq, kt] = 1.0 / (RHO_GAS + (RHO_LIQ - RHO_GAS) * a)
        return carry

    lax.fori_loop(0, 6, advance, 0)

    def weigh(jq, carry):
        jt = tile_j(jq)
        jn, jp = lax.rem(jq + 1, 6), lax.rem(jq + 5, 6)
        odd = jq % 2 == 1
        for kt in range(3):
            kn, kp = (kt + 1) % 3, (kt + 2) % 3
            mi_dn = jnp.where(sh.i_bot1, coef[0, jt, kt], 1.0)
            mi_up = jnp.where(sh.i_top1, coef[1, jt, kt], 1.0)
            at_dn = (lane5 < 16) & jnp.logical_not(odd)
            at_up = (lane5 >= 112) & odd
            mj_dn = jnp.where(at_dn, coef[2, jt, kt], 1.0)
            mj_up = jnp.where(at_up, coef[3, jt, kt], 1.0)
            h = hgt[jq, kt]
            h_up, h_dn = rs(h, -1) * mi_up, rs(h, 1) * mi_dn
            gx, sx = 0.5 * (h_up - h_dn), h_up - 2.0 * h + h_dn
            h_up = sh.j_up(h, hgt[jn, kt], 1) * mj_up
            h_dn = sh.j_dn(h, hgt[jp, kt], 1) * mj_dn
            gy, sy = 0.5 * (h_up - h_dn), h_up - 2.0 * h + h_dn
            gx2, gy2 = gx * gx, gy * gy
            root = lax.rsqrt(1.0 + gx2 + gy2)
            bend = (sx * (1.0 + gy2) + sy * (1.0 + gx2)) * coef[12, jt, kt] * (root * root * root)
            right = (src[jq] if kt == 2 else s_in[jq, kt]) - SIGMA * bend * adv[jq, kt]
            m = mob[jq, kt]
            mk_dn = jnp.where(k16 < 1, coef[4, jt, kt], 1.0)
            mk_up = jnp.where(k16 >= 15, coef[5, jt, kt], 1.0)
            across = (
                rs(m, 1), rs(m, -1),
                sh.j_dn(m, mob[jp, kt], 1), sh.j_up(m, mob[jn, kt], 1),
                sh.k_dn(m, mob[jq, kp], 1), sh.k_up(m, mob[jq, kn], 1),
            )
            masks = (mi_dn, mi_up, mj_dn, mj_up, mk_dn, mk_up)
            edges = (sh.i_bot1, sh.i_top1, at_dn, at_up, k16 < 1, k16 >= 15)
            diag = jnp.zeros_like(m)
            parts = []
            for f in range(6):
                w = (m + masks[f] * across[f]) * jnp.where(edges[f], coef[6 + f, jt, kt], 1.0)
                diag = diag + w
                parts.append(w * masks[f])
            inv = 1.0 / diag
            for f in range(6):
                wts[f, jq, kt] = parts[f] * inv
            rhs[jq, kt] = right * coef[13, jt, kt] * inv
        return carry

    lax.fori_loop(0, 6, weigh, 0)

    for sweep in range(SWEEPS):
        new = p0 if sweep % 2 == 0 else p1
        older = p1 if sweep % 2 == 0 else p0
        last = sweep == SWEEPS - 1

        def old(jq, kt, sweep=sweep, older=older):
            if sweep:
                return older[jq, kt]
            return p_k[jq] if kt == 2 else p_in[jq, kt]

        def relax(jq, carry, old=old, new=new, last=last):
            jn, jp = lax.rem(jq + 1, 6), lax.rem(jq + 5, 6)
            for kt in range(2 if last else 3):
                kn, kp = (kt + 1) % 3, (kt + 2) % 3
                p = old(jq, kt)
                total = wts[0, jq, kt] * rs(p, 1) + wts[1, jq, kt] * rs(p, -1)
                total = total + wts[2, jq, kt] * sh.j_dn(p, old(jp, kt), 1)
                total = total + wts[3, jq, kt] * sh.j_up(p, old(jn, kt), 1)
                total = total + wts[4, jq, kt] * sh.k_dn(p, old(jq, kp), 1)
                total = total + wts[5, jq, kt] * sh.k_up(p, old(jq, kn), 1)
                total = total - rhs[jq, kt]
                if last:
                    out_p[jq, kt] = total[:32]
                    out_adv[jq, kt] = adv[jq, kt][:32]
                else:
                    new[jq, kt] = total
            return carry

        lax.fori_loop(0, 4 if last else 6, relax, 0)

    even = d % 2 == 0
    for h in range(2):
        for n, ref in enumerate((out_adv, out_p)):
            low, high = tile_half(ref, 0, h, tree), tile_half(ref, 7, h, tree)
            send_a[n, :, halves(h)] = jnp.where(even, high, low)
            send_b[n, :, halves(h)] = jnp.where(even, low, high)


def tile_half(ref, t, h, tree):
    row0 = pl.multiple_of(16 * ((t & 1) ^ tree), 16)
    return ref[2 * ((t >> 1) & 1) + h, (t >> 2) & 1, pl.ds(row0, 16), :]


def slots_kernel(adv, prs, bounds, vof, pres):
    d, tree, gi, gj, gk = where_am_i()
    start = bounds[d]
    count = bounds[d + 1] - start
    off = 8 * d - start
    vof[...] = jnp.zeros_like(vof)
    pres[...] = jnp.zeros_like(pres)
    for t in range(8):
        slot = t + off

        @pl.when((slot >= 0) & (slot < count))
        def _(t=t, slot=slot):
            for h in range(2):
                vof[slot, :, halves(h)] = tile_half(adv, t, h, tree)
                pres[slot, :, halves(h)] = tile_half(prs, t, h, tree)


VM = pl.BlockSpec(memory_space=pltpu.VMEM)
SM = pl.BlockSpec(memory_space=pltpu.SMEM)
HB = pl.BlockSpec(memory_space=pltpu.HBM)


def shape(*dims):
    return jax.ShapeDtypeStruct(dims, F32)


def blocks(n):
    return shape(n, 8, 128)


def call(kernel, specs, outs, args, scratch=(), micros=1):
    return pl.pallas_call(
        kernel,
        out_shape=outs,
        in_specs=specs,
        out_specs=jax.tree.map(lambda _: VM, outs),
        scratch_shapes=list(scratch),
        compiler_params=pltpu.CompilerParams(vmem_limit_bytes=40 * 1024 * 1024),
        cost_estimate=pl.CostEstimate(
            flops=micros * 1000000, bytes_accessed=micros * 3000000, transcendentals=0
        ),
    )(*args)


def local(volume, velocity, source, pressure_prev, neighbours, levels, refine, bounds_old, bounds_new):
    d = lax.axis_index("row") * 16 + lax.axis_index("col")
    one = blocks(1)
    ra, rb, ib, ic, peak, old = call(
        first_kernel,
        [HB] * 6,
        (blocks(57), blocks(24), blocks(32), blocks(8), one, shape(6, 10, 16, 256)),
        (volume, velocity, source, pressure_prev, levels, bounds_old),
        [
            pltpu.SMEM((1024,), jnp.int32),
            pltpu.SMEM((129,), jnp.int32),
            pltpu.SemaphoreType.DMA((6,)),
        ],
    )
    x8, x9 = send(peak, flip_pairs(8)), send(peak, flip_pairs(9))
    rb, ic = send(rb, ODD_PAIRS), send(ic, FAR_PAIRS)
    ib, ra = send(ib, axis_pairs(0, 1)), send(ra, EVEN_PAIRS)
    peak = jnp.maximum(jnp.maximum(peak, ra[56:57]), jnp.maximum(x8, x9))
    x64 = send(peak, flip_pairs(64))
    coef = call(
        coefficient_kernel,
        [SM] * 3,
        shape(14, 4, 3, 40, 128),
        (neighbours.reshape(-1), levels, refine),
        [pltpu.SMEM((14 * 64,), F32), pltpu.SMEM((7,), F32)],
        5,
    )
    own, mine, flags = call(
        own_kernel, [VM, SM], (shape(6, 4, 2, 32, 128), blocks(8), blocks(FLAG_COUNT)), (old, bounds_old)
    )
    ext, ia, ib, ja, jb, peak = call(
        block_kernel,
        [VM] * 9 + [HB],
        (shape(6, 4, 2, 32, 128), blocks(32), blocks(32), blocks(43), blocks(43), one),
        (own, mine, flags, ra, rb, ib, ic, peak, x64, coef),
    )
    x16 = send(peak, flip_pairs(16))
    ja, jb = send(ja, axis_pairs(1, 0)), send(jb, axis_pairs(1, 1))
    ka, kb = call(early_k_kernel, [VM] * 3, (blocks(64), blocks(64)), (ext, ia, ib), (), 2)
    ka, kb, peak = call(
        late_k_kernel, [VM] * 6, (blocks(64), blocks(64), one), (ka, kb, ja, jb, peak, x16)
    )
    x32 = send(peak, flip_pairs(32))
    ka, kb = send(ka, axis_pairs(2, 0)), send(kb, axis_pairs(2, 1))
    part, part_tall = (6, 2, 40, 128), (6, 2, 48, 128)
    early = call(
        early_kernel,
        [VM] * 6,
        (shape(*part),) * 5,
        (ext, ia, ib, ja, jb, coef),
        [pltpu.VMEM(part_tall, F32)] * 2 + [pltpu.VMEM(part, F32)],
        4,
    )
    halo, grid = (6, 40, 128), (6, 3, 40, 128)
    adv, prs, sa, sb = call(
        main_kernel,
        [VM] * 10,
        (shape(4, 2, 32, 128),) * 2 + (shape(2, 16, 256),) * 2,
        (*early, ka, kb, peak, x32, coef),
        [pltpu.VMEM((6, 48, 128), F32)] * 2
        + [pltpu.VMEM(halo, F32)] * 5
        + [pltpu.VMEM(grid, F32)] * 6
        + [pltpu.VMEM((6, *grid), F32)],
        8,
    )
    sb, sa = send(sb, ODD_PAIRS), send(sa, EVEN_PAIRS)
    vof, pres = call(slots_kernel, [VM] * 2 + [SM], (shape(10, 16, 256),) * 2, (adv, prs, bounds_new))
    even = d % 2 == 0
    low, high = jnp.where(even, sb, sa), jnp.where(even, sa, sb)
    start, stop = bounds_new[d], bounds_new[d + 1]
    slots = jnp.arange(10, dtype=jnp.int32)
    at_low = ((slots == 0) & (start == 8 * d - 1))[:, None, None]
    at_high = ((slots == 8 * d + 8 - start) & (stop == 8 * d + 9))[:, None, None]
    outs = [
        jnp.where(at_low, low[n][None], jnp.where(at_high, high[n][None], x))
        for n, x in enumerate((vof, pres))
    ]
    return tuple(outs)


def solution(mesh):
    in_specs = (
        P(AXES, None, None),
        P(None, AXES, None, None),
        P(AXES, None, None),
        P(AXES, None, None),
        P(),
        P(),
        P(),
        P(),
        P(),
    )
    out_specs = (P(AXES, None, None), P(AXES, None, None))
    return jax.shard_map(local, mesh=mesh, in_specs=in_specs, out_specs=out_specs, check_vma=False)
```

time: 82.1 us -> 90 us (1.096)
  local copies, waits for them, and re-layouts: 6.99 us -> 19.3 us
  waiting for transfers between devices: 16.8 us -> 11.1 us
  Pallas kernels: 21.7 us -> 22.8 us
    unnamed x23 -> x53, local copies, waits for them, and re-layouts: 6.05 us -> 18.3 us
    ppermute x16 -> x15, waiting for transfers between devices: 16.8 us -> 11.1 us  [send(): return lax.ppermute(x, AXES, pairs)]
    pallas_call x7 -> x9, Pallas kernels: 21.7 us -> 22.8 us  [call(): pl.pallas_call(kernel, out_shape=outs, in_specs=specs, out_specs=jax.tree...]
    ppermute x16 -> x15, starting transfers between devices: 32.2 us -> 32.4 us  [send(): return lax.ppermute(x, AXES, pairs)]
  transfers between devices with their start and end apart: 16 -> 15, of which waited for: 10 -> 4; matrix products, arithmetic and copies ran while one was open for 1% -> 2% of each run, Pallas kernels for 8% -> 10%
where the time goes in v1:
time: 90 us; the launch traced here: 89.3 us
  starting transfers between devices  32.4 us (36%)
  Pallas kernels  22.8 us (25%)
  local copies, waits for them, and re-layouts  19.3 us (21%)
  waiting for transfers between devices  11.1 us (12%)
  between operations  2.8 us (3%)
    ppermute x15, starting transfers between devices, send(): return lax.ppermute(x, AXES, pairs)  32.4 us
    pallas_call x9, Pallas kernels, call(): pl.pallas_call(kernel, out_shape=outs, in_specs=specs, out_specs=jax.tree...  22.8 us
    unnamed x53, local copies, waits for them, and re-layouts  18.3 us
    ppermute x15, waiting for transfers between devices, send(): return lax.ppermute(x, AXES, pairs)  11.1 us
  transfers between devices with their start and end apart: 15, of which 4 were waited for; matrix products, arithmetic and copies ran while one was open for 2% of the time, Pallas kernels for 10%

profile of v1, /device:TPU:1, one launch (start us, length us, event | category | flops | bytes accessed | tf_op | source)
XLA Modules:
  0.0 89.3 jit_solution(6967311518930599721)
XLA Ops:
  0.6 1.0 %copy-done.10 = f32[3,10,16,256]{3,2,1,0:T(8,128)S(1)} copy-done((f32[3,10,16,256]{3,2,1,0:T(8,128)S(1)}, f32[3,10,16,256]{3,2,1,0:T(8,128)}, u32[]{:S(2)}) %copy-start.10) | copy-done | bytes 491544
  5.8 1.8 %shard_map.104 = (f32[57,8,128]{2,1,0:T(8,128)S(1)}, f32[24,8,128]{2,1,0:T(8,128)}, f32[32,8,128]{2,1,0:T(8,128)}, f32[8,8,128]{2,1,0:T(8,128)S(1)}, f32[1,8,128...) custom-call(f32[10,16,256]{2,1,0:T(8,128)S(1)} %copy-done.13, f32[3,10,16,256]{3,2,1,0:T(8,128)S(1)} %copy-done.10, ...), custom_call_target="tpu_custom_call" | custom-call | flops 1000000 | bytes 3000000 | tf_op jit(solution)/shard_map/pallas_call | solution.py:726
  7.6 2.1 %collective-permute-start = (f32[57,8,128]{2,1,0:T(8,128)S(1)}, f32[57,8,128]{2,1,0:T(8,128)S(1)}, u32[]{:S(2)}, u32[]{:S(2)}) collective-permute-start(f32[57,8,128]{2,1,0:T(8,128)S(1)} %get-tuple-element.37), channel_id=1, source_target_pairs={{0,1},{1,0},{2,3},{3,2},{4,5},{5,4},{6,7},{7,6},{8,9},{9,8},{10,11... | collective-permute-start | bytes 700424 | tf_op jit(solution)/shard_map/ppermute | solution.py:50
  9.7 2.9 %collective-permute-start.4 = (f32[1,8,128]{2,1,0:T(8,128)S(1)}, f32[1,8,128]{2,1,0:T(8,128)S(1)}, u32[]{:S(2)}, u32[]{:S(2)}) collective-permute-start(f32[1,8,128]{2,1,0:T(8,128)S(1)} %get-tuple-element.41), channel_id=1, source_target_pairs={{0,8},{1,9},{2,10},{3,11},{4,12},{5,13},{6,14},{7,15},{8,0},{9,1},... | collective-permute-start | bytes 12296 | tf_op jit(solution)/shard_map/ppermute | solution.py:50
  12.6 8.3 %collective-permute-start.1 = (f32[24,8,128]{2,1,0:T(8,128)}, f32[24,8,128]{2,1,0:T(8,128)}, u32[]{:S(2)}, u32[]{:S(2)}) collective-permute-start(f32[24,8,128]{2,1,0:T(8,128)} %get-tuple-element.38), channel_id=1, source_target_pairs={{1,2},{2,1},{3,4},{4,3},{5,6},{6,5},{7,8},{8,7},{9,10},{10,9},{11,... | collective-permute-start | bytes 294920 | tf_op jit(solution)/shard_map/ppermute | solution.py:50
  20.9 3.7 %collective-permute-start.2 = (f32[32,8,128]{2,1,0:T(8,128)}, f32[32,8,128]{2,1,0:T(8,128)}, u32[]{:S(2)}, u32[]{:S(2)}) collective-permute-start(f32[32,8,128]{2,1,0:T(8,128)} %get-tuple-element.39), channel_id=1, source_target_pairs={{0,64},{1,8},{2,66},{3,10},{4,68},{5,12},{6,70},{7,14},{8,1},{9,73... | collective-permute-start | bytes 393224 | tf_op jit(solution)/shard_map/ppermute | solution.py:50
  24.6 1.9 %collective-permute-start.3 = (f32[8,8,128]{2,1,0:T(8,128)S(1)}, f32[8,8,128]{2,1,0:T(8,128)S(1)}, u32[]{:S(2)}, u32[]{:S(2)}) collective-permute-start(f32[8,8,128]{2,1,0:T(8,128)S(1)} %get-tuple-element.40), channel_id=1, source_target_pairs={{1,66},{2,8},{3,68},{4,10},{5,70},{6,12},{7,1},{8,14},{9,3},{10,73... | collective-permute-start | bytes 98312 | tf_op jit(solution)/shard_map/ppermute | solution.py:50
  27.2 3.0 %collective-permute-start.6 = (f32[1,8,128]{2,1,0:T(8,128)S(1)}, f32[1,8,128]{2,1,0:T(8,128)S(1)}, u32[]{:S(2)}, u32[]{:S(2)}) collective-permute-start(f32[1,8,128]{2,1,0:T(8,128)S(1)} %fusion.peak), channel_id=1, source_target_pairs={{0,64},{1,65},{2,66},{3,67},{4,68},{5,69},{6,70},{7,71},{8,72},{9,... | collective-permute-start | bytes 12296 | tf_op jit(solution)/shard_map/ppermute | solution.py:50
  30.2 1.0 %copy.11 = s32[1024,6]{1,0:T(8,128)S(1)} copy(s32[1024,6]{0,1:T(8,128)} %param.13) | data formatting | bytes 49152 | tf_op args[4]
  34.2 5.8 %shard_map.106.coef = f32[14,4,3,40,128]{4,3,2,1,0:T(8,128)S(1)} custom-call(s32[6144]{0:T(1024)S(1)} %reshape.17.neighbours, s32[1024]{0:T(1024)S(1)} %copy-done.21, s32[1024]{0:T(1024)S(1)} %copy-done.22), custom_call_target="tpu_custom_call" | custom-call | flops 5000000 | bytes 15000000 | tf_op jit(solution)/shard_map/pallas_call | solution.py:726
  40.1 1.2 %shard_map.107 = (f32[6,4,2,32,128]{4,3,2,1,0:T(8,128)S(1)}, f32[32,8,128]{2,1,0:T(8,128)S(1)}, f32[32,8,128]{2,1,0:T(8,128)S(1)}, f32[43,8,128]{2,1,0:T(8,128)S...) custom-call(f32[6,4,2,32,128]{4,3,2,1,0:T(8,128)S(1)} %get-tuple-element.34.own, ...), custom_call_target="tpu_custom_call" | custom-call | flops 1000000 | bytes 3000000 | tf_op jit(solution)/shard_map/pallas_call | solution.py:726
  41.4 3.4 %collective-permute-start.8 = (f32[43,8,128]{2,1,0:T(8,128)S(1)}, f32[43,8,128]{2,1,0:T(8,128)S(1)}, u32[]{:S(2)}, u32[]{:S(2)}) collective-permute-start(f32[43,8,128]{2,1,0:T(8,128)S(1)} %get-tuple-element.46), channel_id=1, source_target_pairs={{0,18},{1,19},{2,16},{3,17},{4,22},{5,23},{6,20},{7,21},{8,26},{9,... | collective-permute-start | bytes 528392 | tf_op jit(solution)/shard_map/ppermute | solution.py:50
  46.2 2.4 %collective-permute-done.7.ja = f32[43,8,128]{2,1,0:T(8,128)S(1)} collective-permute-done((f32[43,8,128]{2,1,0:T(8,128)S(1)}, f32[43,8,128]{2,1,0:T(8,128)S(1)}, u32[]{:S(2)}, u32[]{:S(2)}) %collective-permute-start.7) | collective-permute-done | bytes 176160 | tf_op jit(solution)/shard_map/ppermute | solution.py:50
  48.7 4.1 %collective-permute-done.8.jb = f32[43,8,128]{2,1,0:T(8,128)S(1)} collective-permute-done((f32[43,8,128]{2,1,0:T(8,128)S(1)}, f32[43,8,128]{2,1,0:T(8,128)S(1)}, u32[]{:S(2)}, u32[]{:S(2)}) %collective-permute-start.8) | collective-permute-done | bytes 176160 | tf_op jit(solution)/shard_map/ppermute | solution.py:50
  52.8 1.1 %shard_map.110 = (f32[64,8,128]{2,1,0:T(8,128)}, f32[64,8,128]{2,1,0:T(8,128)}, f32[1,8,128]{2,1,0:T(8,128)S(1)}) custom-call(f32[64,8,128]{2,1,0:T(8,128)S(1)} %get-tuple-element.52.ka_in, f32[64,8,128]{2,1,0:T(8,128)S(1)} %get-tuple-element.53.kb_in, f32[43,8,128]{2,1,0:T(8,128)S(1)} %collective-permute-done.7.ja, ...), custom_call_target="tpu_custom_call" | custom-call | flops 1000000 | bytes 3000000 | tf_op jit(solution)/shard_map/pallas_call | solution.py:726
  54.6 1.9 %collective-permute-start.11 = (f32[64,8,128]{2,1,0:T(8,128)}, f32[64,8,128]{2,1,0:T(8,128)}, u32[]{:S(2)}, u32[]{:S(2)}) collective-permute-start(f32[64,8,128]{2,1,0:T(8,128)} %get-tuple-element.56), channel_id=1, source_target_pairs={{0,36},{1,37},{2,38},{3,39},{4,32},{5,33},{6,34},{7,35},{8,44},{9,... | collective-permute-start | bytes 786440 | tf_op jit(solution)/shard_map/ppermute | solution.py:50
  59.7 1.1 %copy-done.1 = f32[6,4,2,32,128]{4,3,2,1,0:T(8,128)S(1)} copy-done((f32[6,4,2,32,128]{4,3,2,1,0:T(8,128)S(1)}, f32[6,4,2,32,128]{4,3,2,1,0:T(8,128)}, u32[]{:S(2)}) %copy-start.1) | copy-done | bytes 786456
  60.9 0.9 %copy-done.3 = f32[43,8,128]{2,1,0:T(8,128)S(1)} copy-done((f32[43,8,128]{2,1,0:T(8,128)S(1)}, f32[43,8,128]{2,1,0:T(8,128)}, u32[]{:S(2)}) %copy-start.3) | copy-done | bytes 176152
  61.8 0.9 %copy-done.5 = f32[43,8,128]{2,1,0:T(8,128)S(1)} copy-done((f32[43,8,128]{2,1,0:T(8,128)S(1)}, f32[43,8,128]{2,1,0:T(8,128)}, u32[]{:S(2)}) %copy-start.5) | copy-done | bytes 176152
  64.5 1.5 %shard_map.108 = (f32[6,2,40,128]{3,2,1,0:T(8,128)S(1)}, f32[6,2,40,128]{3,2,1,0:T(8,128)S(1)}, f32[6,2,40,128]{3,2,1,0:T(8,128)S(1)}, f32[6,2,40,128]{3,2,1,0:T(8,128)S(1)}, f32[6,2,40,128]{3,2,1,0:T(8,128)S(1)}) custom-call(f32[6,4,2,32,128]{4,3,2,1,0:T(8,128)S(1)} %copy-done.1, f32[32,8,128]{2,1,0:T(8,128)S(1)} %copy-done.7, f32[32,8,128]{2,1,0:T(8,128)S(1)} %copy-done.9, ...), custom_call_target="tpu_custom_call" | custom-call | flops 4000000 | bytes 12000000 | tf_op jit(solution)/shard_map/pallas_call | solution.py:726
  66.0 2.9 %collective-permute-done.11.kb = f32[64,8,128]{2,1,0:T(8,128)} collective-permute-done((f32[64,8,128]{2,1,0:T(8,128)}, f32[64,8,128]{2,1,0:T(8,128)}, u32[]{:S(2)}, u32[]{:S(2)}) %collective-permute-start.11) | collective-permute-done | bytes 262176 | tf_op jit(solution)/shard_map/ppermute | solution.py:50
  68.9 9.7 %shard_map.111 = (f32[4,2,32,128]{3,2,1,0:T(8,128)S(1)}, f32[4,2,32,128]{3,2,1,0:T(8,128)S(1)}, f32[2,16,256]{2,1,0:T(8,128)S(1)}, f32[2,16,256]{2,1,0:T(8,128)S(1)}) custom-call(f32[6,2,40,128]{3,2,1,0:T(8,128)S(1)} %get-tuple-element.47.c_in, f32[6,2,40,128]{3,2,1,0:T(8,128)S(1)} %get-tuple-element.48.u_in, f32[6,2,40,128]{3,2,1,0:T(8,128)S(1)} %get-tuple-element.49.s_in, ...), custom_call_target="tpu_custom_call" | custom-call | flops 8000000 | bytes 24000000 | tf_op jit(solution)/shard_map/pallas_call | solution.py:726
  79.9 4.4 %collective-permute-start.13 = (f32[2,16,256]{2,1,0:T(8,128)S(1)}, f32[2,16,256]{2,1,0:T(8,128)S(1)}, u32[]{:S(2)}, u32[]{:S(2)}) collective-permute-start(f32[2,16,256]{2,1,0:T(8,128)S(1)} %get-tuple-element.58), channel_id=1, source_target_pairs={{1,2},{2,1},{3,4},{4,3},{5,6},{6,5},{7,8},{8,7},{9,10},{10,9},{11,... | collective-permute-start | bytes 98312 | tf_op jit(solution)/shard_map/ppermute | solution.py:50
  86.9 1.6 %collective-permute-done.13 = f32[2,16,256]{2,1,0:T(8,128)S(1)} collective-permute-done((f32[2,16,256]{2,1,0:T(8,128)S(1)}, f32[2,16,256]{2,1,0:T(8,128)S(1)}, u32[]{:S(2)}, u32[]{:S(2)}) %collective-permute-start.13) | collective-permute-done | bytes 32800 | tf_op jit(solution)/shard_map/ppermute | solution.py:50
  (75 shorter events, 18.0 us)
Async XLA Ops:
  0.6 1.0 %copy-start.10 = (f32[3,10,16,256]{3,2,1,0:T(8,128)S(1)}, f32[3,10,16,256]{3,2,1,0:T(8,128)}, u32[]{:S(2)}) copy-start(f32[3,10,16,256]{3,2,1,0:T(8,128)} %vel.1) | copy-start | bytes 1474564
  7.6 18.9 %collective-permute-start = (f32[57,8,128]{2,1,0:T(8,128)S(1)}, f32[57,8,128]{2,1,0:T(8,128)S(1)}, u32[]{:S(2)}, u32[]{:S(2)}) collective-permute-start(f32[57,8,128]{2,1,0:T(8,128)S(1)} %get-tuple-element.37), channel_id=1, source_target_pairs={{0,1},{1,0},{2,3},{3,2},{4,5},{5,4},{6,7},{7,6},{8,9},{9,8},{10,11... | collective-permute-start | bytes 700424 | tf_op jit(solution)/shard_map/ppermute | solution.py:50
  9.7 14.9 %collective-permute-start.4 = (f32[1,8,128]{2,1,0:T(8,128)S(1)}, f32[1,8,128]{2,1,0:T(8,128)S(1)}, u32[]{:S(2)}, u32[]{:S(2)}) collective-permute-start(f32[1,8,128]{2,1,0:T(8,128)S(1)} %get-tuple-element.41), channel_id=1, source_target_pairs={{0,8},{1,9},{2,10},{3,11},{4,12},{5,13},{6,14},{7,15},{8,0},{9,1},... | collective-permute-start | bytes 12296 | tf_op jit(solution)/shard_map/ppermute | solution.py:50
  12.6 13.9 %collective-permute-start.5 = (f32[1,8,128]{2,1,0:T(8,128)S(1)}, f32[1,8,128]{2,1,0:T(8,128)S(1)}, u32[]{:S(2)}, u32[]{:S(2)}) collective-permute-start(f32[1,8,128]{2,1,0:T(8,128)S(1)} %get-tuple-element.41), channel_id=1, source_target_pairs={{0,9},{1,8},{2,11},{3,10},{4,13},{5,12},{6,15},{7,14},{8,1},{9,0},... | collective-permute-start | bytes 12296 | tf_op jit(solution)/shard_map/ppermute | solution.py:50
  12.6 27.4 %collective-permute-start.1 = (f32[24,8,128]{2,1,0:T(8,128)}, f32[24,8,128]{2,1,0:T(8,128)}, u32[]{:S(2)}, u32[]{:S(2)}) collective-permute-start(f32[24,8,128]{2,1,0:T(8,128)} %get-tuple-element.38), channel_id=1, source_target_pairs={{1,2},{2,1},{3,4},{4,3},{5,6},{6,5},{7,8},{8,7},{9,10},{10,9},{11,... | collective-permute-start | bytes 294920 | tf_op jit(solution)/shard_map/ppermute | solution.py:50
  20.9 19.2 %collective-permute-start.2 = (f32[32,8,128]{2,1,0:T(8,128)}, f32[32,8,128]{2,1,0:T(8,128)}, u32[]{:S(2)}, u32[]{:S(2)}) collective-permute-start(f32[32,8,128]{2,1,0:T(8,128)} %get-tuple-element.39), channel_id=1, source_target_pairs={{0,64},{1,8},{2,66},{3,10},{4,68},{5,12},{6,70},{7,14},{8,1},{9,73... | collective-permute-start | bytes 393224 | tf_op jit(solution)/shard_map/ppermute | solution.py:50
  24.6 15.5 %collective-permute-start.3 = (f32[8,8,128]{2,1,0:T(8,128)S(1)}, f32[8,8,128]{2,1,0:T(8,128)S(1)}, u32[]{:S(2)}, u32[]{:S(2)}) collective-permute-start(f32[8,8,128]{2,1,0:T(8,128)S(1)} %get-tuple-element.40), channel_id=1, source_target_pairs={{1,66},{2,8},{3,68},{4,10},{5,70},{6,12},{7,1},{8,14},{9,3},{10,73... | collective-permute-start | bytes 98312 | tf_op jit(solution)/shard_map/ppermute | solution.py:50
  27.2 12.9 %collective-permute-start.6 = (f32[1,8,128]{2,1,0:T(8,128)S(1)}, f32[1,8,128]{2,1,0:T(8,128)S(1)}, u32[]{:S(2)}, u32[]{:S(2)}) collective-permute-start(f32[1,8,128]{2,1,0:T(8,128)S(1)} %fusion.peak), channel_id=1, source_target_pairs={{0,64},{1,65},{2,66},{3,67},{4,68},{5,69},{6,70},{7,71},{8,72},{9,... | collective-permute-start | bytes 12296 | tf_op jit(solution)/shard_map/ppermute | solution.py:50
  31.5 8.6 %copy-start.12 = (f32[57,8,128]{2,1,0:T(8,128)S(1)}, f32[57,8,128]{2,1,0:T(8,128)}, u32[]{:S(2)}) copy-start(f32[57,8,128]{2,1,0:T(8,128)} %copy-done.11) | copy-start | bytes 700420
  40.0 17.2 %copy-start.25 = (s32[129]{0:T(256)S(1)}, s32[129]{0:T(256)}, u32[]{:S(2)}) copy-start(s32[129]{0:T(256)} %bounds.3) | copy-start | bytes 1552
  41.3 13.3 %copy-start.6 = (f32[32,8,128]{2,1,0:T(8,128)}, f32[32,8,128]{2,1,0:T(8,128)S(1)}, u32[]{:S(2)}) copy-start(f32[32,8,128]{2,1,0:T(8,128)S(1)} %get-tuple-element.43.ia) | copy-start | bytes 393220
  41.3 13.3 %copy-start.8 = (f32[32,8,128]{2,1,0:T(8,128)}, f32[32,8,128]{2,1,0:T(8,128)S(1)}, u32[]{:S(2)}) copy-start(f32[32,8,128]{2,1,0:T(8,128)S(1)} %get-tuple-element.44.ib) | copy-start | bytes 393220
  41.3 7.4 %collective-permute-start.7 = (f32[43,8,128]{2,1,0:T(8,128)S(1)}, f32[43,8,128]{2,1,0:T(8,128)S(1)}, u32[]{:S(2)}, u32[]{:S(2)}) collective-permute-start(f32[43,8,128]{2,1,0:T(8,128)S(1)} %get-tuple-element.45), channel_id=1, source_target_pairs={{0,2},{1,3},{2,0},{3,1},{4,6},{5,7},{6,4},{7,5},{8,10},{9,11},{10,... | collective-permute-start | bytes 528392 | tf_op jit(solution)/shard_map/ppermute | solution.py:50
  41.4 11.5 %collective-permute-start.8 = (f32[43,8,128]{2,1,0:T(8,128)S(1)}, f32[43,8,128]{2,1,0:T(8,128)S(1)}, u32[]{:S(2)}, u32[]{:S(2)}) collective-permute-start(f32[43,8,128]{2,1,0:T(8,128)S(1)} %get-tuple-element.46), channel_id=1, source_target_pairs={{0,18},{1,19},{2,16},{3,17},{4,22},{5,23},{6,20},{7,21},{8,26},{9,... | collective-permute-start | bytes 528392 | tf_op jit(solution)/shard_map/ppermute | solution.py:50
  44.7 1.5 %collective-permute-start.9 = (f32[1,8,128]{2,1,0:T(8,128)S(1)}, f32[1,8,128]{2,1,0:T(8,128)S(1)}, u32[]{:S(2)}, u32[]{:S(2)}) collective-permute-start(f32[1,8,128]{2,1,0:T(8,128)S(1)} %get-tuple-element.54.peak), channel_id=1, source_target_pairs={{0,16},{1,17},{2,18},{3,19},{4,20},{5,21},{6,22},{7,23},{8,24},{9,... | collective-permute-start | bytes 12296 | tf_op jit(solution)/shard_map/ppermute | solution.py:50
  52.8 1.1 %copy-start.4 = (f32[43,8,128]{2,1,0:T(8,128)}, f32[43,8,128]{2,1,0:T(8,128)S(1)}, u32[]{:S(2)}) copy-start(f32[43,8,128]{2,1,0:T(8,128)S(1)} %collective-permute-done.8.jb) | copy-start | bytes 528388
  54.6 11.4 %collective-permute-start.10 = (f32[64,8,128]{2,1,0:T(8,128)}, f32[64,8,128]{2,1,0:T(8,128)}, u32[]{:S(2)}, u32[]{:S(2)}) collective-permute-start(f32[64,8,128]{2,1,0:T(8,128)} %get-tuple-element.55), channel_id=1, source_target_pairs={{0,4},{1,5},{2,6},{3,7},{4,0},{5,1},{6,2},{7,3},{8,12},{9,13},{10,... | collective-permute-start | bytes 786440 | tf_op jit(solution)/shard_map/ppermute | solution.py:50
  54.6 14.3 %collective-permute-start.11 = (f32[64,8,128]{2,1,0:T(8,128)}, f32[64,8,128]{2,1,0:T(8,128)}, u32[]{:S(2)}, u32[]{:S(2)}) collective-permute-start(f32[64,8,128]{2,1,0:T(8,128)} %get-tuple-element.56), channel_id=1, source_target_pairs={{0,36},{1,37},{2,38},{3,39},{4,32},{5,33},{6,34},{7,35},{8,44},{9,... | collective-permute-start | bytes 786440 | tf_op jit(solution)/shard_map/ppermute | solution.py:50
  56.5 9.5 %collective-permute-start.12 = (f32[1,8,128]{2,1,0:T(8,128)S(1)}, f32[1,8,128]{2,1,0:T(8,128)S(1)}, u32[]{:S(2)}, u32[]{:S(2)}) collective-permute-start(f32[1,8,128]{2,1,0:T(8,128)S(1)} %get-tuple-element.57.peak), channel_id=1, source_target_pairs={{0,32},{1,33},{2,34},{3,35},{4,36},{5,37},{6,38},{7,39},{8,40},{9,... | collective-permute-start | bytes 12296 | tf_op jit(solution)/shard_map/ppermute | solution.py:50
  59.7 1.1 %copy-start.1 = (f32[6,4,2,32,128]{4,3,2,1,0:T(8,128)S(1)}, f32[6,4,2,32,128]{4,3,2,1,0:T(8,128)}, u32[]{:S(2)}) copy-start(f32[6,4,2,32,128]{4,3,2,1,0:T(8,128)} %copy-done) | copy-start | bytes 2359300
  60.9 0.9 %copy-start.3 = (f32[43,8,128]{2,1,0:T(8,128)S(1)}, f32[43,8,128]{2,1,0:T(8,128)}, u32[]{:S(2)}) copy-start(f32[43,8,128]{2,1,0:T(8,128)} %copy-done.2) | copy-start | bytes 528388
  61.8 0.9 %copy-start.5 = (f32[43,8,128]{2,1,0:T(8,128)S(1)}, f32[43,8,128]{2,1,0:T(8,128)}, u32[]{:S(2)}) copy-start(f32[43,8,128]{2,1,0:T(8,128)} %copy-done.4) | copy-start | bytes 528388
  79.9 8.5 %collective-permute-start.13 = (f32[2,16,256]{2,1,0:T(8,128)S(1)}, f32[2,16,256]{2,1,0:T(8,128)S(1)}, u32[]{:S(2)}, u32[]{:S(2)}) collective-permute-start(f32[2,16,256]{2,1,0:T(8,128)S(1)} %get-tuple-element.58), channel_id=1, source_target_pairs={{1,2},{2,1},{3,4},{4,3},{5,6},{6,5},{7,8},{8,7},{9,10},{10,9},{11,... | collective-permute-start | bytes 98312 | tf_op jit(solution)/shard_map/ppermute | solution.py:50
  84.3 4.1 %collective-permute-start.14 = (f32[2,16,256]{2,1,0:T(8,128)S(1)}, f32[2,16,256]{2,1,0:T(8,128)S(1)}, u32[]{:S(2)}, u32[]{:S(2)}) collective-permute-start(f32[2,16,256]{2,1,0:T(8,128)S(1)} %get-tuple-element.59), channel_id=1, source_target_pairs={{0,1},{1,0},{2,3},{3,2},{4,5},{5,4},{6,7},{7,6},{8,9},{9,8},{10,11... | collective-permute-start | bytes 98312 | tf_op jit(solution)/shard_map/ppermute | solution.py:50
  (17 other events, 13.4 us)

commit v2 on v1

--- a/solution.py
+++ b/solution.py
@@ -43,7 +43,6 @@
 
 EVEN_PAIRS = flip_pairs(1)
 ODD_PAIRS = [(d, d + 1 if d % 2 else d - 1) for d in range(1, DEVS - 1)]
-FAR_PAIRS = [(d, dict(axis_pairs(0, 1))[e]) for d, e in ODD_PAIRS]
 
 
 def send(x, pairs):
@@ -97,26 +96,10 @@
     )
 
 
-def first_kernel(
-    vol, vel, src, prev, levels_in, bounds_in, ra, rb, ib, ic, peak, old, levels, bounds, sems
-):
-    copies = [
-        pltpu.make_async_copy(bounds_in, bounds, sems.at[0]),
-        pltpu.make_async_copy(levels_in, levels, sems.at[1]),
-        pltpu.make_async_copy(vol, old.at[0], sems.at[2]),
-        pltpu.make_async_copy(vel, old.at[pl.ds(1, 3)], sems.at[3]),
-        pltpu.make_async_copy(src, old.at[4], sems.at[4]),
-        pltpu.make_async_copy(prev, old.at[5], sems.at[5]),
-    ]
-    for copy in copies:
-        copy.start()
+def first_kernel(old, facts, ra, rb, peak):
     d, tree, gi, gj, gk = where_am_i()
     sub, lane = iotas()
-    for copy in copies:
-        copy.wait()
-    start = bounds[d]
-    count = bounds[d + 1] - start
-    off = 8 * d - start
+    off, count = facts[0], facts[1]
     even = d % 2 == 0
     slot_a = jnp.where(even, 8 + off, 0)
     slot_b = jnp.where(even, 0, 8 + off)
@@ -126,32 +109,17 @@
                 ra[f * 4 + r * 2 + h] = old_slice(old, f, slot_a, 8 * r, h)
                 rb[f * 4 + r * 2 + h] = old_slice(old, f, slot_b, 8 * r, h)
     high = gi % 2 == 0
+    row0 = jnp.where(high, 8, 0)
     bit = jnp.where(even, 1, 0)
     for q in range(4):
         for h in range(2):
             slot = jnp.clip(bit + 2 * q + off, 0, 9)
-            row0 = jnp.where(high, 8, 0)
             groups = slab_groups(lambda f: old_slice(old, f, slot, row0, h), high, sub)
             for g in range(4):
                 ra[24 + (g * 4 + q) * 2 + h] = groups[g]
-            slot = jnp.clip(1 - bit + 2 * q + off, 0, 9)
-            groups = slab_groups(
-                lambda f: old_slice(old, f, slot, 8 - row0, h), jnp.logical_not(high), sub
-            )
-            for g in range(4):
-                ib[(g * 4 + q) * 2 + h] = groups[g]
-    other = jnp.where(even, d - 1, d + 1)
-    gi_other = where_is(other)[1]
-    high = gi_other % 2 == 1
-    row0 = jnp.where(high, 8, 0)
-    for h in range(2):
-        groups = slab_groups(lambda f: old_slice(old, f, slot_b, row0, h), high, sub)
-        for g in range(4):
-            ic[g * 2 + h] = groups[g]
     top = jnp.zeros((8, 128), F32)
     for s in range(10):
-        level = levels[jnp.minimum(start + s, 1023)]
-        inv = jnp.where(s < count, jnp.left_shift(1, level), 0).astype(F32)
+        inv = jnp.where(s < count, jnp.left_shift(1, facts[2 + s]), 0).astype(F32)
         part = jnp.zeros((8, 128), F32)
         for r in range(2):
             for h in range(2):
@@ -165,7 +133,7 @@
 FLAG_COUNT = 6
 
 
-def own_kernel(old, bounds, ext, mine, flags):
+def own_kernel(old, bounds, ext, mine, flags, ib):
     d, tree, gi, gj, gk = where_am_i()
     sub, lane = iotas()
     off = 8 * d - bounds[d]
@@ -182,35 +150,50 @@
     high = gi % 2 == 1
     row0 = jnp.where(high, 8, 0)
     slot_a = jnp.where(even, 8 + off, 0)
+    bit = jnp.where(even, 0, 1)
     for h in range(2):
         groups = slab_groups(lambda f: old_slice(old, f, slot_a, row0, h), high, sub)
         for g in range(4):
             mine[g * 2 + h] = groups[g]
-    near_gi = (gi + jnp.where(gi % 2 == 1, 1, 7)) % 8
-    upper = near_gi >= 4
-    li = jnp.where(upper, 7 - near_gi, near_gi)
-    e = (d & 54) | (li & 1) | ((li >> 1) << 3) | jnp.where(upper, 64, 0)
-    e_even = e % 2 == 0
-    odd, e_odd = jnp.logical_not(even), jnp.logical_not(e_even)
+        for q in range(4):
+            slot = jnp.clip(bit + 2 * q + off, 0, 9)
+            groups = slab_groups(lambda f: old_slice(old, f, slot, row0, h), high, sub)
+            for g in range(4):
+                ib[(g * 4 + q) * 2 + h] = groups[g]
+    odd = jnp.logical_not(even)
+    first, last = bounds[d] == 8 * d + 1, bounds[d + 1] == 8 * d + 7
     values = (
-        bounds[d] == 8 * d + 1,
-        bounds[d + 1] == 8 * d + 7,
+        first,
+        last,
         even & (bounds[d + 1] == 8 * d + 9),
         odd & (bounds[d] == 8 * d - 1),
-        e_even & (bounds[e] == 8 * e + 1),
-        e_odd & (bounds[e + 1] == 8 * e + 7),
+        even & first,
+        odd & last,
     )
     for n, value in enumerate(values):
         flags[n] = jnp.full((8, 128), jnp.where(value, 1.0, 0.0), F32)
 
 
-def block_kernel(
-    own, mine, flags, ra, rb, ib_in, ic, peak, x64, coef, ext, ia, ib, ja, jb, peak_out
-):
+def second_kernel(ib_in, flags, rb, ra, peak, x8, x9, ib, peak_out):
     d, tree, gi, gj, gk = where_am_i()
     sub, lane = iotas()
+    high = gi % 2 == 1
+    block = jnp.where(high, 2, 0)
+    for q in range(4):
+        for h in range(2):
+            if q in (0, 3):
+                groups = slab_groups(lambda f: rb[f * 4 + block + h], high, sub)
+                flag = flags[4 if q == 0 else 5] > 0.5
+            for g in range(4):
+                n = (g * 4 + q) * 2 + h
+                ib[n] = jnp.where(flag, groups[g], ib_in[n]) if q in (0, 3) else ib_in[n]
+    peak_out[0] = jnp.maximum(jnp.maximum(peak[0], ra[56]), jnp.maximum(x8[0], x9[0]))
+
+
+def block_kernel(own, mine, flags, ra, rb, ext, ia):
+    d, tree, gi, gj, gk = where_am_i()
     even = d % 2 == 0
-    flag = [flags[n] > 0.5 for n in range(FLAG_COUNT)]
+    flag = [flags[n] > 0.5 for n in range(4)]
     ext[...] = own[...]
     for t, missing in ((0, flag[0]), (7, flag[1])):
         bj, bk = (t >> 1) & 1, (t >> 2) & 1
@@ -229,20 +212,12 @@
         for h in range(2):
             for g in range(4):
                 n = (g * 4 + q) * 2 + h
-                x, y = ra[24 + n], ib_in[n]
+                x = ra[24 + n]
                 if q == 0:
                     x = jnp.where(flag[2], mine[g * 2 + h], x)
-                    y = jnp.where(flag[4], ic[g * 2 + h], y)
                 if q == 3:
                     x = jnp.where(flag[3], mine[g * 2 + h], x)
-                    y = jnp.where(flag[5], ic[g * 2 + h], y)
                 ia[n] = x
-                ib[n] = y
-    top = jnp.maximum(peak[0], x64[0])
-    pack_j(ext, ia, ib, ja, jb, gi, gj, sub, lane)
-    ja[42] = top
-    jb[42] = top
-    peak_out[0] = top
 
 
 def make_block(ext, ia, ib, gi, sub):
@@ -266,26 +241,54 @@
     return rows, pair
 
 
-def pack_j(ext, ia, ib, ja, jb, gi, gj, sub, lane):
+J_BLOCKS = 37
+
+
+def j_place(f, kt, b):
+    if f == 0:
+        return kt * 6 + b
+    if f == 5:
+        return 32 + b
+    return (12 if f in (2, 4) else 22) + kt * 5 + b
+
+
+def third_kernel(ext, ia, ib, peak, x64, ja, jb, peak_out):
+    d, tree, gi, gj, gk = where_am_i()
+    sub, lane = iotas()
     rows, _ = make_block(ext, ia, ib, gi, sub)
     even = gj % 2 == 0
 
-    def pack(jq, kt, g, b):
-        if g == 0:
-            return rows(0, jq, kt, b)
-        if g == 1:
-            return rows(2, jq, kt, b)
-        fa, fb = ((1, 3), (5, 4))[g - 2]
-        nat = lane < 64 if jq == 0 else lane >= 64
-        return jnp.where(nat, rows(fa, jq, kt, b), rl(rows(fb, jq, kt, b), 64))
-
-    for g in range(4):
+    def put(f, kt, b, get):
+        lo, hi = get(0), get(3)
+        ja[j_place(f, kt, b)] = jnp.where(even, hi, lo)
+        jb[j_place(f, kt, b)] = jnp.where(even, lo, hi)
+
+    for b in range(6):
         for kt in range(2):
-            for b in range(6 if g == 0 else 5):
-                n = kt * 6 + b if g == 0 else 12 + ((g - 1) * 2 + kt) * 5 + b
-                lo, hi = pack(0, kt, g, b), pack(3, kt, g, b)
-                ja[n] = jnp.where(even, hi, lo)
-                jb[n] = jnp.where(even, lo, hi)
+            put(0, kt, b, lambda jq: rows(0, jq, kt, b))
+    for b in range(5):
+        for kt in range(2):
+            def five(jq):
+                nat = lane < 80 if jq == 0 else lane >= 48
+                turn = 80 if jq == 0 else -80
+                return jnp.where(nat, rows(2, jq, kt, b), rl(rows(4, jq, kt, b), turn))
+
+            def four(jq):
+                nat = lane < 64 if jq == 0 else lane >= 64
+                return jnp.where(nat, rows(1, jq, kt, b), rl(rows(3, jq, kt, b), 64))
+
+            put(2, kt, b, five)
+            put(1, kt, b, four)
+
+        def both(jq):
+            nat = lane < 64 if jq == 0 else lane >= 64
+            return jnp.where(nat, rows(5, jq, 0, b), rl(rows(5, jq, 1, b), 64))
+
+        put(5, 0, b, both)
+    top = jnp.maximum(peak[0], x64[0])
+    ja[J_BLOCKS] = top
+    jb[J_BLOCKS] = top
+    peak_out[0] = top
 
 
 def make_wide(rows, ja, jb, gj):
@@ -294,76 +297,75 @@
     def wide(f, jq, kt, b):
         if jq < 4:
             return rows(f, jq, kt, b)
-        if f == 0:
-            n = kt * 6 + b
-        else:
-            n = 12 + ((1, 1, 0, 1, 2, 2)[f] * 2 + kt) * 5 + b
+        n = j_place(f, kt, b)
         if jq == 4:
             x = jnp.where(first_high, ja[n], jb[n])
         else:
             x = jnp.where(first_high, jb[n], ja[n])
-        return rl(x, 64) if f in (3, 4) else x
+        if f == 4:
+            return rl(x, -80 if jq == 4 else 80)
+        return rl(x, 64) if f == 3 or (f == 5 and kt == 1) else x
 
     return wide
 
 
-def k_place(g, jt, b):
-    return jt * 6 + b if g == 0 else 18 + ((g - 1) * 3 + jt) * 5 + b
-
-
-def pack_k(wide, jt, ka, kb, gk, lane):
+K_BLOCKS = 43
+
+
+def k_place(kind, jt, b):
+    if kind == 0:
+        return jt * 6 + b
+    if jt == 2:
+        return 38 + b
+    return (18 if kind < 3 else 28) + jt * 5 + b
+
+
+def pack_k(get, ka, kb, gk, lane):
     even = gk % 2 == 0
     near = lane % 16 < 8
-    small = lane % 8 < 4
-
-    def squeeze(f, kt, b):
-        first, last = wide(f, 2 * jt, kt, b), wide(f, 2 * jt + 1, kt, b)
+    k8 = lane % 8
+
+    def put(n, lo, hi):
+        ka[n] = jnp.where(even, hi, lo)
+        kb[n] = jnp.where(even, lo, hi)
+
+    def squeeze(first, last, kt):
         if kt == 0:
             return jnp.where(near, first, rl(last, 8))
         return jnp.where(near, rl(first, -8), last)
 
-    def pack(kt, g, b):
-        if g == 0:
-            return squeeze(0, kt, b)
-        if g == 1:
-            return squeeze(3, kt, b)
-        fa, fb = ((1, 2), (5, 4))[g - 2]
-        one, two = squeeze(fa, kt, b), squeeze(fb, kt, b)
-        if kt == 0:
-            return jnp.where(small, one, rl(two, 4))
-        return jnp.where(small, rl(two, -4), one)
-
-    for g in range(4):
-        for b in range(6 if g == 0 else 5):
-            n = k_place(g, jt, b)
-            lo, hi = pack(0, g, b), pack(1, g, b)
-            ka[n] = jnp.where(even, hi, lo)
-            kb[n] = jnp.where(even, lo, hi)
-
-
-def early_k_kernel(ext, ia, ib, ka, kb):
-    d, tree, gi, gj, gk = where_am_i()
-    sub, lane = iotas()
-    rows, _ = make_block(ext, ia, ib, gi, sub)
+    def join(kind, value, kt):
+        if kind == 1:
+            nat, turn = (k8 < 5, 5) if kt == 0 else (k8 >= 3, -5)
+        else:
+            nat, turn = (k8 < 4, 4) if kt == 0 else (k8 >= 4, -4)
+        return jnp.where(nat, value(kind), rl(value(kind + 1), turn))
+
+    for jt in range(3):
+        for b in range(6):
+            sides = [squeeze(get(0, 2 * jt, kt, b), get(0, 2 * jt + 1, kt, b), kt) for kt in range(2)]
+            put(k_place(0, jt, b), *sides)
     for jt in range(2):
-        pack_k(rows, jt, ka, kb, gk, lane)
-
-
-def late_k_kernel(ka_in, kb_in, ja, jb, peak, x16, ka, kb, peak_out):
-    d, tree, gi, gj, gk = where_am_i()
-    sub, lane = iotas()
-    wide = make_wide(None, ja, jb, gj)
-    for jt in range(2):
-        for g in range(4):
-            for b in range(6 if g == 0 else 5):
-                n = k_place(g, jt, b)
-                ka[n] = ka_in[n]
-                kb[n] = kb_in[n]
-    pack_k(wide, 2, ka, kb, gk, lane)
-    top = jnp.maximum(jnp.maximum(peak[0], x16[0]), jnp.maximum(ja[42], jb[42]))
-    ka[63] = top
-    kb[63] = top
-    peak_out[0] = top
+        for kind in (1, 3):
+            for b in range(5):
+                sides = [
+                    join(
+                        kind,
+                        lambda n: squeeze(get(n, 2 * jt, kt, b), get(n, 2 * jt + 1, kt, b), kt),
+                        kt,
+                    )
+                    for kt in range(2)
+                ]
+                put(k_place(kind, jt, b), *sides)
+    for b in range(5):
+        sides = []
+        for kt in range(2):
+            both = [
+                join(kind, lambda n: jnp.where(lane < 64, get(n, 4, kt, b), get(n, 5, kt, b)), kt)
+                for kind in (1, 3)
+            ]
+            sides.append(squeeze(*both, kt))
+        put(k_place(1, 2, b), *sides)
 
 
 def coefficient_kernel(neighbours, levels, refine, out, table, ratio):
@@ -408,12 +410,17 @@
             v = [jnp.full((8, 128), table[base + ip * 16 + kp], F32) for kp in range(4)]
             vals[ip] = (v[0], v[1], jnp.where(lane % 16 < 8, v[2], v[3]))
         for kt in range(3):
-            mixed = jnp.where(sub < 4, vals[2][kt], vals[3][kt])
-            for b, v in enumerate((vals[0][kt], vals[0][kt], vals[1][kt], vals[1][kt], mixed)):
-                out[item, jp, kt, pl.ds(8 * b, 8), :] = v
+            out[item, jp, kt, 0] = vals[0][kt]
+            out[item, jp, kt, 1] = vals[1][kt]
+            out[item, jp, kt, 2] = jnp.where(sub < 4, vals[2][kt], vals[3][kt])
         return carry
 
     lax.fori_loop(0, 56, expand, 0)
+
+
+def coefficient(coef, item, jt, kt):
+    a, b, c = (coef[item, jt, kt, n] for n in range(3))
+    return jnp.concatenate([a, a, b, b, c], axis=0)
 
 
 def minmod(a, b):
@@ -470,8 +477,8 @@
         odd = jq % 2 == 1
         lane5 = self.lane5
         c = c40(jq)
-        m_dn = jnp.where(odd, 1.0, coef[2, jt, kt])
-        m_up = jnp.where(odd, coef[3, jt, kt], 1.0)
+        m_dn = jnp.where(odd, 1.0, coefficient(coef, 2, jt, kt))
+        m_up = jnp.where(odd, coefficient(coef, 3, jt, kt), 1.0)
         up_m1 = jnp.where(lane5 >= 112, m_up, 1.0)
         up_m2 = jnp.where(lane5 >= 96, m_up, 1.0)
         dn_m1 = jnp.where(lane5 < 16, m_dn, 1.0)
@@ -483,7 +490,7 @@
             self.j_dn(c, cp, 1) * dn_m1, self.j_dn(c, cp, 2) * dn_m2,
             u, self.j_up(u, u1(jn), 1) * up_m1, self.j_dn(u, u1(jp), 1) * dn_m1,
         )
-        m_dn, m_up = coef[0, jt, kt], coef[1, jt, kt]
+        m_dn, m_up = coefficient(coef, 0, jt, kt), coefficient(coef, 1, jt, kt)
         up_m1, up_m2 = jnp.where(self.i_top1, m_up, 1.0), jnp.where(self.i_top2, m_up, 1.0)
         dn_m1, dn_m2 = jnp.where(self.i_bot1, m_dn, 1.0), jnp.where(self.i_bot2, m_dn, 1.0)
         wrap = self.wrap
@@ -498,7 +505,11 @@
     return jnp.where(jq < 4, jq >> 1, jq - 2)
 
 
-def early_kernel(ext, ia, ib, ja, jb, coef, c40, u2, src, prs, chg, c48, v48, u1):
+def early_kernel(
+    ext, ia, ib, ja, jb, peak, x16, coef,
+    c40, u2, src, prs, chg, ka, kb, peak_out,
+    c48, v48, u1,
+):
     d, tree, gi, gj, gk = where_am_i()
     sh = Shifts()
     sub = sh.sub
@@ -531,40 +542,67 @@
         return carry
 
     lax.fori_loop(0, 6, step, 0)
+    kinds = (c48, u2, src, chg, prs)
+    pack_k(
+        lambda kind, jq, kt, b: kinds[kind][jq, kt, pl.ds(8 * b, 8), :], ka, kb, gk, sh.lane
+    )
+    top = jnp.maximum(
+        jnp.maximum(peak[0], x16[0]), jnp.maximum(ja[J_BLOCKS], jb[J_BLOCKS])
+    )
+    ka[K_BLOCKS] = top
+    kb[K_BLOCKS] = top
+    peak_out[0] = top
 
 
 def main_kernel(
-    c_in, u_in, s_in, p_in, chg, ka, kb, peak, x32, coef,
+    c_in, u_in, s_in, p_in, chg_in, ka, kb, peak, x32, coef,
     out_adv, out_p, send_a, send_b,
-    c48, v48, c_k, u1, u2, src, p_k, p0, p1, adv, mob, hgt, rhs, wts,
+    c_k, u2, src, p_k, chg_k, p0, p1, adv, mob, hgt, rhs, wts,
 ):
     d, tree, gi, gj, gk = where_am_i()
     sh = Shifts()
     sub, lane, lane5, k16 = sh.sub, sh.lane, sh.lane5, sh.k16
     near = lane % 16 < 8
     k_even = gk % 2 == 0
-    dest = (c48, v48, u1, u2, src, p_k)
-    for f in range(6):
-        for b in range(6 if f == 0 else 5):
+
+    def sides(kind, jt, b):
+        a, e = ka[k_place(kind, jt, b)], kb[k_place(kind, jt, b)]
+        low, high = jnp.where(k_even, a, e), jnp.where(k_even, e, a)
+        if jt == 2 and kind == 3:
+            low, high = rl(low, -8), rl(high, 0)
+        elif jt == 2 and kind == 1:
+            low, high = low, rl(high, 8)
+        return low, high
+
+    for b in range(6):
+        for jt in range(3):
+            low, high = sides(0, jt, b)
+            halves_of = (
+                jnp.where(near, low, rl(high, 8)), jnp.where(near, rl(low, -8), high)
+            )
+            for jq, x in zip((2 * jt, 2 * jt + 1), halves_of):
+                if b < 4:
+                    c_k[jq, pl.ds(8 * b, 8), :] = x
+                elif b == 4:
+                    c_k[jq, pl.ds(32, 8), :] = x
+                else:
+                    c_k[jq, pl.ds(32, 8), :] = jnp.where(sub < 4, c_k[jq, pl.ds(32, 8), :], x)
+    dest = {1: u2, 2: src, 3: chg_k, 4: p_k}
+    for b in range(5):
+        for kind in (1, 3):
+            turn = 5 if kind == 1 else 4
             for jt in range(3):
-                n = k_place((0, 2, 2, 1, 3, 3)[f], jt, b)
-                a, e = ka[n], kb[n]
-                low_pack = jnp.where(k_even, a, e)
-                high_pack = jnp.where(k_even, e, a)
-                if f in (2, 4):
-                    low_pack, high_pack = rl(low_pack, -4), rl(high_pack, 4)
-                first = jnp.where(near, low_pack, rl(high_pack, 8))
-                last = jnp.where(near, rl(low_pack, -8), high_pack)
-                for jq, x in ((2 * jt, first), (2 * jt + 1, last)):
-                    dest[f][jq, pl.ds(8 * b, 8), :] = x
-                    if f == 0 and b < 4:
-                        c_k[jq, pl.ds(8 * b, 8), :] = x
-                    if f == 1 and b == 4:
-                        v48[jq, pl.ds(40, 8), :] = x
-    for jq in range(6):
-        c_k[jq, pl.ds(32, 8), :] = jnp.where(
-            sub < 4, c48[jq, pl.ds(32, 8), :], c48[jq, pl.ds(40, 8), :]
-        )
+                low, high = sides(kind, jt, b)
+                for n in range(2):
+                    if n == 1:
+                        low, high = rl(low, -turn), rl(high, turn)
+                    if jt == 2:
+                        first = last = jnp.where(near, low, high)
+                    else:
+                        first = jnp.where(near, low, rl(high, 8))
+                        last = jnp.where(near, rl(low, -8), high)
+                    dest[kind + n][2 * jt, pl.ds(8 * b, 8), :] = first
+                    dest[kind + n][2 * jt + 1, pl.ds(8 * b, 8), :] = last
 
     def c40(jq, kt):
         return c_k[jq] if kt == 2 else c_in[jq, kt]
@@ -572,7 +610,9 @@
     def uk(jq, kt):
         return u2[jq] if kt == 2 else u_in[jq, kt]
 
-    top = jnp.maximum(jnp.maximum(peak[0], x32[0]), jnp.maximum(ka[63], kb[63]))
+    top = jnp.maximum(
+        jnp.maximum(peak[0], x32[0]), jnp.maximum(ka[K_BLOCKS], kb[K_BLOCKS])
+    )
     top = jnp.max(top, keepdims=True)
     step = jnp.broadcast_to(CFL / top, (8, 128))
     step = jnp.concatenate([step] * 5, axis=0)
@@ -581,14 +621,9 @@
         jt = tile_j(jq)
         for kt in range(3):
             kn, kp = (kt + 1) % 3, (kt + 2) % 3
-            if kt == 2:
-                change = sh.change_ij(
-                    jq, 2, coef, lambda n: c_k[n], lambda n: u1[n], c48[jq], v48[jq]
-                )
-            else:
-                change = chg[jq, kt]
+            change = chg_k[jq] if kt == 2 else chg_in[jq, kt]
             c = c40(jq, kt)
-            m_dn, m_up = coef[4, jt, kt], coef[5, jt, kt]
+            m_dn, m_up = coefficient(coef, 4, jt, kt), coefficient(coef, 5, jt, kt)
             cn, cp = c40(jq, kn), c40(jq, kp)
             up1, up2 = sh.k_up(c, cn, 1, m_up), sh.k_up(c, cn, 2, m_up)
             dn1, dn2 = sh.k_dn(c, cp, 1, m_dn), sh.k_dn(c, cp, 2, m_dn)
@@ -596,7 +631,7 @@
             u = uk(jq, kt)
             u_up, u_dn = sh.k_up(u, uk(jq, kn), 1, m_up), sh.k_dn(u, uk(jq, kp), 1, m_dn)
             change = change + face_change(c, up1, up2, dn1, dn2, u, u_up, u_dn)
-            a = jnp.clip(c - step * coef[12, jt, kt] * change, 0.0, 1.0)
+            a = jnp.clip(c - step * coefficient(coef, 12, jt, kt) * change, 0.0, 1.0)
             adv[jq, kt] = a
             mob[jq, kt] = 1.0 / (RHO_GAS + (RHO_LIQ - RHO_GAS) * a)
         return carry
@@ -609,12 +644,12 @@
         odd = jq % 2 == 1
         for kt in range(3):
             kn, kp = (kt + 1) % 3, (kt + 2) % 3
-            mi_dn = jnp.where(sh.i_bot1, coef[0, jt, kt], 1.0)
-            mi_up = jnp.where(sh.i_top1, coef[1, jt, kt], 1.0)
+            mi_dn = jnp.where(sh.i_bot1, coefficient(coef, 0, jt, kt), 1.0)
+            mi_up = jnp.where(sh.i_top1, coefficient(coef, 1, jt, kt), 1.0)
             at_dn = (lane5 < 16) & jnp.logical_not(odd)
             at_up = (lane5 >= 112) & odd
-            mj_dn = jnp.where(at_dn, coef[2, jt, kt], 1.0)
-            mj_up = jnp.where(at_up, coef[3, jt, kt], 1.0)
+            mj_dn = jnp.where(at_dn, coefficient(coef, 2, jt, kt), 1.0)
+            mj_up = jnp.where(at_up, coefficient(coef, 3, jt, kt), 1.0)
             h = hgt[jq, kt]
             h_up, h_dn = rs(h, -1) * mi_up, rs(h, 1) * mi_dn
             gx, sx = 0.5 * (h_up - h_dn), h_up - 2.0 * h + h_dn
@@ -623,11 +658,11 @@
             gy, sy = 0.5 * (h_up - h_dn), h_up - 2.0 * h + h_dn
             gx2, gy2 = gx * gx, gy * gy
             root = lax.rsqrt(1.0 + gx2 + gy2)
-            bend = (sx * (1.0 + gy2) + sy * (1.0 + gx2)) * coef[12, jt, kt] * (root * root * root)
+            bend = (sx * (1.0 + gy2) + sy * (1.0 + gx2)) * coefficient(coef, 12, jt, kt) * (root * root * root)
             right = (src[jq] if kt == 2 else s_in[jq, kt]) - SIGMA * bend * adv[jq, kt]
             m = mob[jq, kt]
-            mk_dn = jnp.where(k16 < 1, coef[4, jt, kt], 1.0)
-            mk_up = jnp.where(k16 >= 15, coef[5, jt, kt], 1.0)
+            mk_dn = jnp.where(k16 < 1, coefficient(coef, 4, jt, kt), 1.0)
+            mk_up = jnp.where(k16 >= 15, coefficient(coef, 5, jt, kt), 1.0)
             across = (
                 rs(m, 1), rs(m, -1),
                 sh.j_dn(m, mob[jp, kt], 1), sh.j_up(m, mob[jn, kt], 1),
@@ -638,13 +673,13 @@
             diag = jnp.zeros_like(m)
             parts = []
             for f in range(6):
-                w = (m + masks[f] * across[f]) * jnp.where(edges[f], coef[6 + f, jt, kt], 1.0)
+                w = (m + masks[f] * across[f]) * jnp.where(edges[f], coefficient(coef, 6 + f, jt, kt), 1.0)
                 diag = diag + w
                 parts.append(w * masks[f])
             inv = 1.0 / diag
             for f in range(6):
                 wts[f, jq, kt] = parts[f] * inv
-            rhs[jq, kt] = right * coef[13, jt, kt] * inv
+            rhs[jq, kt] = right * coefficient(coef, 13, jt, kt) * inv
         return carry
 
     lax.fori_loop(0, 6, weigh, 0)
@@ -711,7 +746,6 @@
 
 VM = pl.BlockSpec(memory_space=pltpu.VMEM)
 SM = pl.BlockSpec(memory_space=pltpu.SMEM)
-HB = pl.BlockSpec(memory_space=pltpu.HBM)
 
 
 def shape(*dims):
@@ -722,14 +756,14 @@
     return shape(n, 8, 128)
 
 
-def call(kernel, specs, outs, args, scratch=(), micros=1):
+def call(kernel, specs, outs, args, scratch=(), micros=1, mib=8):
     return pl.pallas_call(
         kernel,
         out_shape=outs,
         in_specs=specs,
         out_specs=jax.tree.map(lambda _: VM, outs),
         scratch_shapes=list(scratch),
-        compiler_params=pltpu.CompilerParams(vmem_limit_bytes=40 * 1024 * 1024),
+        compiler_params=pltpu.CompilerParams(vmem_limit_bytes=mib * 1024 * 1024),
         cost_estimate=pl.CostEstimate(
             flops=micros * 1000000, bytes_accessed=micros * 3000000, transcendentals=0
         ),
@@ -739,67 +773,69 @@
 def local(volume, velocity, source, pressure_prev, neighbours, levels, refine, bounds_old, bounds_new):
     d = lax.axis_index("row") * 16 + lax.axis_index("col")
     one = blocks(1)
-    ra, rb, ib, ic, peak, old = call(
-        first_kernel,
-        [HB] * 6,
-        (blocks(57), blocks(24), blocks(32), blocks(8), one, shape(6, 10, 16, 256)),
-        (volume, velocity, source, pressure_prev, levels, bounds_old),
-        [
-            pltpu.SMEM((1024,), jnp.int32),
-            pltpu.SMEM((129,), jnp.int32),
-            pltpu.SemaphoreType.DMA((6,)),
-        ],
-    )
+    old = jnp.concatenate([volume[None], velocity, source[None], pressure_prev[None]], axis=0)
+    start = bounds_old[d]
+    own_levels = lax.dynamic_slice_in_dim(jnp.pad(levels, (0, 16)), start, 14, 0)
+    facts = jnp.concatenate([jnp.stack([8 * d - start, bounds_old[d + 1] - start]), own_levels])
+    ra, rb, peak = call(first_kernel, [VM, SM], (blocks(57), blocks(24), one), (old, facts))
     x8, x9 = send(peak, flip_pairs(8)), send(peak, flip_pairs(9))
-    rb, ic = send(rb, ODD_PAIRS), send(ic, FAR_PAIRS)
-    ib, ra = send(ib, axis_pairs(0, 1)), send(ra, EVEN_PAIRS)
-    peak = jnp.maximum(jnp.maximum(peak, ra[56:57]), jnp.maximum(x8, x9))
+    rb, ra = send(rb, ODD_PAIRS), send(ra, EVEN_PAIRS)
+    own, mine, flags, ib = call(
+        own_kernel,
+        [VM, SM],
+        (shape(6, 4, 2, 32, 128), blocks(8), blocks(FLAG_COUNT), blocks(32)),
+        (old, bounds_old),
+    )
+    ib, peak = call(
+        second_kernel, [VM] * 7, (blocks(32), one), (ib, flags, rb, ra, peak, x8, x9)
+    )
     x64 = send(peak, flip_pairs(64))
+    ib = send(ib, axis_pairs(0, 1))
+    ext, ia = call(
+        block_kernel,
+        [VM] * 5,
+        (shape(6, 4, 2, 32, 128), blocks(32)),
+        (own, mine, flags, ra, rb),
+    )
+    ja, jb, peak = call(
+        third_kernel,
+        [VM] * 5,
+        (blocks(J_BLOCKS + 1), blocks(J_BLOCKS + 1), one),
+        (ext, ia, ib, peak, x64),
+    )
+    x16 = send(peak, flip_pairs(16))
+    ja, jb = send(ja, axis_pairs(1, 0)), send(jb, axis_pairs(1, 1))
     coef = call(
         coefficient_kernel,
         [SM] * 3,
-        shape(14, 4, 3, 40, 128),
+        shape(14, 4, 3, 3, 8, 128),
         (neighbours.reshape(-1), levels, refine),
         [pltpu.SMEM((14 * 64,), F32), pltpu.SMEM((7,), F32)],
         5,
     )
-    own, mine, flags = call(
-        own_kernel, [VM, SM], (shape(6, 4, 2, 32, 128), blocks(8), blocks(FLAG_COUNT)), (old, bounds_old)
-    )
-    ext, ia, ib, ja, jb, peak = call(
-        block_kernel,
-        [VM] * 9 + [HB],
-        (shape(6, 4, 2, 32, 128), blocks(32), blocks(32), blocks(43), blocks(43), one),
-        (own, mine, flags, ra, rb, ib, ic, peak, x64, coef),
-    )
-    x16 = send(peak, flip_pairs(16))
-    ja, jb = send(ja, axis_pairs(1, 0)), send(jb, axis_pairs(1, 1))
-    ka, kb = call(early_k_kernel, [VM] * 3, (blocks(64), blocks(64)), (ext, ia, ib), (), 2)
-    ka, kb, peak = call(
-        late_k_kernel, [VM] * 6, (blocks(64), blocks(64), one), (ka, kb, ja, jb, peak, x16)
+    part, part_tall = (6, 2, 40, 128), (6, 2, 48, 128)
+    *early, ka, kb, peak = call(
+        early_kernel,
+        [VM] * 8,
+        (shape(*part),) * 5 + (blocks(K_BLOCKS + 1),) * 2 + (one,),
+        (ext, ia, ib, ja, jb, peak, x16, coef),
+        [pltpu.VMEM(part_tall, F32)] * 2 + [pltpu.VMEM(part, F32)],
+        2,
+        12,
     )
     x32 = send(peak, flip_pairs(32))
     ka, kb = send(ka, axis_pairs(2, 0)), send(kb, axis_pairs(2, 1))
-    part, part_tall = (6, 2, 40, 128), (6, 2, 48, 128)
-    early = call(
-        early_kernel,
-        [VM] * 6,
-        (shape(*part),) * 5,
-        (ext, ia, ib, ja, jb, coef),
-        [pltpu.VMEM(part_tall, F32)] * 2 + [pltpu.VMEM(part, F32)],
-        4,
-    )
     halo, grid = (6, 40, 128), (6, 3, 40, 128)
     adv, prs, sa, sb = call(
         main_kernel,
         [VM] * 10,
         (shape(4, 2, 32, 128),) * 2 + (shape(2, 16, 256),) * 2,
         (*early, ka, kb, peak, x32, coef),
-        [pltpu.VMEM((6, 48, 128), F32)] * 2
-        + [pltpu.VMEM(halo, F32)] * 5
+        [pltpu.VMEM(halo, F32)] * 5
         + [pltpu.VMEM(grid, F32)] * 6
         + [pltpu.VMEM((6, *grid), F32)],
         8,
+        16,
     )
     sb, sa = send(sb, ODD_PAIRS), send(sa, EVEN_PAIRS)
     vof, pres = call(slots_kernel, [VM] * 2 + [SM], (shape(10, 16, 256),) * 2, (adv, prs, bounds_new))

time: 90 us -> 86.8 us (0.964)
  starting transfers between devices: 32.4 us -> 26.9 us
  between operations: 2.8 us -> 6.57 us
  local copies, waits for them, and re-layouts: 19.3 us -> 15.6 us
  waiting for transfers between devices: 11.1 us -> 14.3 us
  Pallas kernels: 22.8 us -> 20.5 us
  other arithmetic: 0.86 us -> 2.26 us
    ppermute x15 -> x14, starting transfers between devices: 32.4 us -> 26.9 us  [send(): return lax.ppermute(x, AXES, pairs)]
    unnamed x53 -> x43, local copies, waits for them, and re-layouts: 18.3 us -> 13.1 us
    ppermute x15 -> x14, waiting for transfers between devices: 11.1 us -> 14.3 us  [send(): return lax.ppermute(x, AXES, pairs)]
    pallas_call x9, Pallas kernels: 22.8 us -> 20.5 us  [call(): pl.pallas_call(kernel, out_shape=outs, in_specs=specs, out_specs=jax.tree...]
    concatenate x0 -> x2, other arithmetic: none -> 1.41 us  [the longest x1 1.33 us: local(): jnp.concatenate([volume[None], velocity, source[None], pressure_prev[None...]
  transfers between devices with their start and end apart: 15 -> 14, of which waited for: 4 -> 6; matrix products, arithmetic and copies ran while one was open for 2% -> 1% of each run, Pallas kernels for 10% -> 8%
where the time goes in v2:
time: 86.8 us; the launch traced here: 86.1 us
  starting transfers between devices  26.9 us (31%)
  Pallas kernels  20.5 us (24%)
  local copies, waits for them, and re-layouts  15.6 us (18%)
  waiting for transfers between devices  14.3 us (16%)
  between operations  6.57 us (8%)
  other arithmetic  2.26 us (3%)
    ppermute x14, starting transfers between devices, send(): return lax.ppermute(x, AXES, pairs)  26.9 us
    pallas_call x9, Pallas kernels, call(): pl.pallas_call(kernel, out_shape=outs, in_specs=specs, out_specs=jax.tree...  20.5 us
    ppermute x14, waiting for transfers between devices, send(): return lax.ppermute(x, AXES, pairs)  14.3 us
    unnamed x43, local copies, waits for them, and re-layouts  13.1 us
  transfers between devices with their start and end apart: 14, of which 6 were waited for; matrix products, arithmetic and copies ran while one was open for 1% of the time, Pallas kernels for 8%

profile of v2, /device:TPU:1, one launch (start us, length us, event | category | flops | bytes accessed | tf_op | source)
XLA Modules:
  0.0 86.1 jit_solution(15727993394294551218)
XLA Ops:
  0.6 1.4 %fusion = (s32[1]{0:T(128)}, s32[1]{0:T(128)}, s32[1]{0:T(128)}, s32[1]{0:T(128)}) fusion(s32[129]{0:T(256)} %bounds.3, s32[]{:T(128)S(6)} %select_n.43, s32[]{:T(128)S(6)} %select_n.46, s32[129]{0:T(256)} %bounds.2), kind=kLoop, calls=%fused_computation.13 | loop fusion | bytes 40 | tf_op jit(solution)/shard_map/dynamic_slice | solution.py:844
  6.8 1.3 %pad_maximum_fusion.old = f32[6,10,16,256]{3,2,1,0:T(8,128)S(1)} fusion(f32[1,10,16,256]{3,2,1,0:T(8,128)} %bitcast.17, f32[1,10,16,256]{3,2,1,0:T(8,128)} %bitcast.18, f32[3,10,16,256]{3,2,1,0:T(8,128)} %param.10, f32[1,10,16,256]{3,2,1,0:T(8,128)} %bitcast.19), kind=kLoop, calls=%fused_computation | loop fusion | flops 737280 | bytes 1966080 | tf_op jit(solution)/shard_map/concatenate | solution.py:776
  8.8 2.1 %collective-permute-start = (f32[57,8,128]{2,1,0:T(8,128)S(1)}, f32[57,8,128]{2,1,0:T(8,128)S(1)}, u32[]{:S(2)}, u32[]{:S(2)}) collective-permute-start(f32[57,8,128]{2,1,0:T(8,128)S(1)} %get-tuple-element.33), channel_id=1, source_target_pairs={{0,1},{1,0},{2,3},{3,2},{4,5},{5,4},{6,7},{7,6},{8,9},{9,8},{10,11... | collective-permute-start | bytes 700424 | tf_op jit(solution)/shard_map/ppermute | solution.py:49
  10.9 7.0 %collective-permute-start.1 = (f32[24,8,128]{2,1,0:T(8,128)S(1)}, f32[24,8,128]{2,1,0:T(8,128)S(1)}, u32[]{:S(2)}, u32[]{:S(2)}) collective-permute-start(f32[24,8,128]{2,1,0:T(8,128)S(1)} %get-tuple-element.34), channel_id=1, source_target_pairs={{1,2},{2,1},{3,4},{4,3},{5,6},{6,5},{7,8},{8,7},{9,10},{10,9},{11,... | collective-permute-start | bytes 294920 | tf_op jit(solution)/shard_map/ppermute | solution.py:49
  18.8 4.1 %collective-permute-done.3.x9 = f32[1,8,128]{2,1,0:T(8,128)S(1)} collective-permute-done((f32[1,8,128]{2,1,0:T(8,128)S(1)}, f32[1,8,128]{2,1,0:T(8,128)S(1)}, u32[]{:S(2)}, u32[]{:S(2)}) %collective-permute-start.3) | collective-permute-done | bytes 4128 | tf_op jit(solution)/shard_map/ppermute | solution.py:49
  22.9 3.7 %collective-permute-start.4 = (f32[32,8,128]{2,1,0:T(8,128)S(1)}, f32[32,8,128]{2,1,0:T(8,128)S(1)}, u32[]{:S(2)}, u32[]{:S(2)}) collective-permute-start(f32[32,8,128]{2,1,0:T(8,128)S(1)} %get-tuple-element.39), channel_id=1, source_target_pairs={{0,64},{1,8},{2,66},{3,10},{4,68},{5,12},{6,70},{7,14},{8,1},{9,73... | collective-permute-start | bytes 393224 | tf_op jit(solution)/shard_map/ppermute | solution.py:49
  26.8 4.0 %collective-permute-done.5.x64 = f32[1,8,128]{2,1,0:T(8,128)S(1)} collective-permute-done((f32[1,8,128]{2,1,0:T(8,128)S(1)}, f32[1,8,128]{2,1,0:T(8,128)S(1)}, u32[]{:S(2)}, u32[]{:S(2)}) %collective-permute-start.5) | collective-permute-done | bytes 4128 | tf_op jit(solution)/shard_map/ppermute | solution.py:49
  31.6 1.2 %collective-permute-start.6 = (f32[38,8,128]{2,1,0:T(8,128)}, f32[38,8,128]{2,1,0:T(8,128)S(1)}, u32[]{:S(2)}, u32[]{:S(2)}) collective-permute-start(f32[38,8,128]{2,1,0:T(8,128)} %get-tuple-element.41), channel_id=1, source_target_pairs={{0,2},{1,3},{2,0},{3,1},{4,6},{5,7},{6,4},{7,5},{8,10},{9,11},{10,... | collective-permute-start | bytes 466952 | tf_op jit(solution)/shard_map/ppermute | solution.py:49
  32.9 4.4 %collective-permute-start.7 = (f32[38,8,128]{2,1,0:T(8,128)}, f32[38,8,128]{2,1,0:T(8,128)S(1)}, u32[]{:S(2)}, u32[]{:S(2)}) collective-permute-start(f32[38,8,128]{2,1,0:T(8,128)} %get-tuple-element.42), channel_id=1, source_target_pairs={{0,18},{1,19},{2,16},{3,17},{4,22},{5,23},{6,20},{7,21},{8,26},{9,... | collective-permute-start | bytes 466952 | tf_op jit(solution)/shard_map/ppermute | solution.py:49
  37.9 5.8 %shard_map.109.coef = f32[14,4,3,3,8,128]{5,4,3,2,1,0:T(8,128)S(1)} custom-call(s32[6144]{0:T(1024)S(1)} %reshape.17.neighbours, s32[1024]{0:T(1024)S(1)} %copy-done.16, s32[1024]{0:T(1024)S(1)} %copy-done.17), custom_call_target="tpu_custom_call" | custom-call | flops 5000000 | bytes 15000000 | tf_op jit(solution)/shard_map/pallas_call | solution.py:760
  44.4 0.9 %copy-done.11 = f32[38,8,128]{2,1,0:T(8,128)S(1)} copy-done((f32[38,8,128]{2,1,0:T(8,128)S(1)}, f32[38,8,128]{2,1,0:T(8,128)}, u32[]{:S(2)}) %copy-start.11) | copy-done | bytes 155672
  45.3 3.7 %shard_map.110 = (f32[6,2,40,128]{3,2,1,0:T(8,128)S(1)}, f32[6,2,40,128]{3,2,1,0:T(8,128)S(1)}, f32[6,2,40,128]{3,2,1,0:T(8,128)S(1)}, f32[6,2,40,128]{3,2,1,0:T...) custom-call(f32[6,4,2,32,128]{4,3,2,1,0:T(8,128)S(1)} %get-tuple-ele, ...), custom_call_target="tpu_custom_call" | custom-call | flops 2000000 | bytes 6000000 | tf_op jit(solution)/shard_map/pallas_call | solution.py:760
  52.3 1.5 %collective-permute-start.10 = (f32[44,8,128]{2,1,0:T(8,128)}, f32[44,8,128]{2,1,0:T(8,128)S(1)}, u32[]{:S(2)}, u32[]{:S(2)}) collective-permute-start(f32[44,8,128]{2,1,0:T(8,128)} %get-tuple-element.50), channel_id=1, source_target_pairs={{0,36},{1,37},{2,38},{3,39},{4,32},{5,33},{6,34},{7,35},{8,44},{9,... | collective-permute-start | bytes 540680 | tf_op jit(solution)/shard_map/ppermute | solution.py:49
  56.4 0.8 collective-permute-done.11.x32
  57.4 4.3 %collective-permute-done.10.kb = f32[44,8,128]{2,1,0:T(8,128)S(1)} collective-permute-done((f32[44,8,128]{2,1,0:T(8,128)}, f32[44,8,128]{2,1,0:T(8,128)S(1)}, u32[]{:S(2)}, u32[]{:S(2)}) %collective-permute-start.10) | collective-permute-done | bytes 180256 | tf_op jit(solution)/shard_map/ppermute | solution.py:49
  62.4 0.9 %copy-done.1 = f32[6,2,40,128]{3,2,1,0:T(8,128)S(1)} copy-done((f32[6,2,40,128]{3,2,1,0:T(8,128)S(1)}, f32[6,2,40,128]{3,2,1,0:T(8,128)}, u32[]{:S(2)}) %copy-start.1) | copy-done | bytes 245784
  63.3 0.9 %copy-done.3 = f32[6,2,40,128]{3,2,1,0:T(8,128)S(1)} copy-done((f32[6,2,40,128]{3,2,1,0:T(8,128)S(1)}, f32[6,2,40,128]{3,2,1,0:T(8,128)}, u32[]{:S(2)}) %copy-start.3) | copy-done | bytes 245784
  64.3 0.9 %copy-done.5 = f32[6,2,40,128]{3,2,1,0:T(8,128)S(1)} copy-done((f32[6,2,40,128]{3,2,1,0:T(8,128)S(1)}, f32[6,2,40,128]{3,2,1,0:T(8,128)}, u32[]{:S(2)}) %copy-start.5) | copy-done | bytes 245784
  65.2 0.9 %copy-done.7 = f32[6,2,40,128]{3,2,1,0:T(8,128)S(1)} copy-done((f32[6,2,40,128]{3,2,1,0:T(8,128)S(1)}, f32[6,2,40,128]{3,2,1,0:T(8,128)}, u32[]{:S(2)}) %copy-start.7) | copy-done | bytes 245784
  66.2 0.9 %copy-done.9 = f32[44,8,128]{2,1,0:T(8,128)S(1)} copy-done((f32[44,8,128]{2,1,0:T(8,128)S(1)}, f32[44,8,128]{2,1,0:T(8,128)}, u32[]{:S(2)}) %copy-start.9) | copy-done | bytes 180248
  67.1 8.1 %shard_map.111 = (f32[4,2,32,128]{3,2,1,0:T(8,128)S(1)}, f32[4,2,32,128]{3,2,1,0:T(8,128)S(1)}, f32[2,16,256]{2,1,0:T(8,128)S(1)}, f32[2,16,256]{2,1,0:T(8,128)}) custom-call(f32[6,2,40,128]{3,2,1,0:T(8,128)S(1)} %get-tuple-element.44.c_in, f32[6,2,40,128]{3,2,1,0:T(8,128)S(1)} %copy-done.1, f32[6,2,40,128]{3,2,1,0:T(8,128)S(1)} %copy-done.3, ...), custom_call_target="tpu_custom_call" | custom-call | flops 8000000 | bytes 24000000 | tf_op jit(solution)/shard_map/pallas_call | solution.py:760
  76.5 5.3 %collective-permute-start.12 = (f32[2,16,256]{2,1,0:T(8,128)}, f32[2,16,256]{2,1,0:T(8,128)S(1)}, u32[]{:S(2)}, u32[]{:S(2)}) collective-permute-start(f32[2,16,256]{2,1,0:T(8,128)} %get-tuple-element.52), channel_id=1, source_target_pairs={{1,2},{2,1},{3,4},{4,3},{5,6},{6,5},{7,8},{8,7},{9,10},{10,9},{11,... | collective-permute-start | bytes 98312 | tf_op jit(solution)/shard_map/ppermute | solution.py:49
  82.0 0.9 %copy-done.13 = f32[4,2,32,128]{3,2,1,0:T(8,128)S(1)} copy-done((f32[4,2,32,128]{3,2,1,0:T(8,128)S(1)}, f32[4,2,32,128]{3,2,1,0:T(8,128)}, u32[]{:S(2)}) %copy-start.13) | copy-done | bytes 131096
  82.9 0.9 %copy-done.15 = f32[4,2,32,128]{3,2,1,0:T(8,128)S(1)} copy-done((f32[4,2,32,128]{3,2,1,0:T(8,128)S(1)}, f32[4,2,32,128]{3,2,1,0:T(8,128)}, u32[]{:S(2)}) %copy-start.15) | copy-done | bytes 131096
  (67 shorter events, 13.3 us)
Async XLA Ops:
  0.6 17.5 %copy-start.18 = (s32[129]{0:T(256)S(1)}, s32[129]{0:T(256)}, u32[]{:S(2)}) copy-start(s32[129]{0:T(256)} %bounds.2) | copy-start | bytes 1552
  8.8 28.6 %copy-start.20 = (s32[1024,6]{0,1:T(8,128)S(1)}, s32[1024,6]{0,1:T(8,128)}, u32[]{:S(2)}) copy-start(s32[1024,6]{0,1:T(8,128)} %param.13) | copy-start | bytes 73732
  8.8 14.1 %collective-permute-start = (f32[57,8,128]{2,1,0:T(8,128)S(1)}, f32[57,8,128]{2,1,0:T(8,128)S(1)}, u32[]{:S(2)}, u32[]{:S(2)}) collective-permute-start(f32[57,8,128]{2,1,0:T(8,128)S(1)} %get-tuple-element.33), channel_id=1, source_target_pairs={{0,1},{1,0},{2,3},{3,2},{4,5},{5,4},{6,7},{7,6},{8,9},{9,8},{10,11... | collective-permute-start | bytes 700424 | tf_op jit(solution)/shard_map/ppermute | solution.py:49
  10.9 12.0 %collective-permute-start.1 = (f32[24,8,128]{2,1,0:T(8,128)S(1)}, f32[24,8,128]{2,1,0:T(8,128)S(1)}, u32[]{:S(2)}, u32[]{:S(2)}) collective-permute-start(f32[24,8,128]{2,1,0:T(8,128)S(1)} %get-tuple-element.34), channel_id=1, source_target_pairs={{1,2},{2,1},{3,4},{4,3},{5,6},{6,5},{7,8},{8,7},{9,10},{10,9},{11,... | collective-permute-start | bytes 294920 | tf_op jit(solution)/shard_map/ppermute | solution.py:49
  17.9 4.9 %collective-permute-start.3 = (f32[1,8,128]{2,1,0:T(8,128)S(1)}, f32[1,8,128]{2,1,0:T(8,128)S(1)}, u32[]{:S(2)}, u32[]{:S(2)}) collective-permute-start(f32[1,8,128]{2,1,0:T(8,128)S(1)} %get-tuple-element.38.peak), channel_id=1, source_target_pairs={{0,9},{1,8},{2,11},{3,10},{4,13},{5,12},{6,15},{7,14},{8,1},{9,0},... | collective-permute-start | bytes 12296 | tf_op jit(solution)/shard_map/ppermute | solution.py:49
  18.0 4.9 %collective-permute-start.2 = (f32[1,8,128]{2,1,0:T(8,128)S(1)}, f32[1,8,128]{2,1,0:T(8,128)S(1)}, u32[]{:S(2)}, u32[]{:S(2)}) collective-permute-start(f32[1,8,128]{2,1,0:T(8,128)S(1)} %get-tuple-element.38.peak), channel_id=1, source_target_pairs={{0,8},{1,9},{2,10},{3,11},{4,12},{5,13},{6,14},{7,15},{8,0},{9,1},... | collective-permute-start | bytes 12296 | tf_op jit(solution)/shard_map/ppermute | solution.py:49
  18.8 19.2 %copy-start.16 = (s32[1024]{0:T(1024)S(1)}, s32[1024]{0:T(1024)}, u32[]{:S(2)}) copy-start(s32[1024]{0:T(1024)} %levels.1) | copy-start | bytes 12292
  18.8 19.2 %copy-start.17 = (s32[1024]{0:T(1024)S(1)}, s32[1024]{0:T(1024)}, u32[]{:S(2)}) copy-start(s32[1024]{0:T(1024)} %refine.1) | copy-start | bytes 12292
  22.9 7.9 %collective-permute-start.4 = (f32[32,8,128]{2,1,0:T(8,128)S(1)}, f32[32,8,128]{2,1,0:T(8,128)S(1)}, u32[]{:S(2)}, u32[]{:S(2)}) collective-permute-start(f32[32,8,128]{2,1,0:T(8,128)S(1)} %get-tuple-element.39), channel_id=1, source_target_pairs={{0,64},{1,8},{2,66},{3,10},{4,68},{5,12},{6,70},{7,14},{8,1},{9,73... | collective-permute-start | bytes 393224 | tf_op jit(solution)/shard_map/ppermute | solution.py:49
  26.6 4.2 %collective-permute-start.5 = (f32[1,8,128]{2,1,0:T(8,128)S(1)}, f32[1,8,128]{2,1,0:T(8,128)S(1)}, u32[]{:S(2)}, u32[]{:S(2)}) collective-permute-start(f32[1,8,128]{2,1,0:T(8,128)S(1)} %get-tuple-element.40.peak), channel_id=1, source_target_pairs={{0,64},{1,65},{2,66},{3,67},{4,68},{5,69},{6,70},{7,71},{8,72},{9,... | collective-permute-start | bytes 12296 | tf_op jit(solution)/shard_map/ppermute | solution.py:49
  31.6 12.1 %collective-permute-start.6 = (f32[38,8,128]{2,1,0:T(8,128)}, f32[38,8,128]{2,1,0:T(8,128)S(1)}, u32[]{:S(2)}, u32[]{:S(2)}) collective-permute-start(f32[38,8,128]{2,1,0:T(8,128)} %get-tuple-element.41), channel_id=1, source_target_pairs={{0,2},{1,3},{2,0},{3,1},{4,6},{5,7},{6,4},{7,5},{8,10},{9,11},{10,... | collective-permute-start | bytes 466952 | tf_op jit(solution)/shard_map/ppermute | solution.py:49
  32.9 10.8 %collective-permute-start.7 = (f32[38,8,128]{2,1,0:T(8,128)}, f32[38,8,128]{2,1,0:T(8,128)S(1)}, u32[]{:S(2)}, u32[]{:S(2)}) collective-permute-start(f32[38,8,128]{2,1,0:T(8,128)} %get-tuple-element.42), channel_id=1, source_target_pairs={{0,18},{1,19},{2,16},{3,17},{4,22},{5,23},{6,20},{7,21},{8,26},{9,... | collective-permute-start | bytes 466952 | tf_op jit(solution)/shard_map/ppermute | solution.py:49
  37.3 6.4 %collective-permute-start.8 = (f32[1,8,128]{2,1,0:T(8,128)S(1)}, f32[1,8,128]{2,1,0:T(8,128)S(1)}, u32[]{:S(2)}, u32[]{:S(2)}) collective-permute-start(f32[1,8,128]{2,1,0:T(8,128)S(1)} %get-tuple-element.43.peak), channel_id=1, source_target_pairs={{0,16},{1,17},{2,18},{3,19},{4,20},{5,21},{6,22},{7,23},{8,24},{9,... | collective-permute-start | bytes 12296 | tf_op jit(solution)/shard_map/ppermute | solution.py:49
  51.8 30.1 %copy-start.19 = (s32[129]{0:T(256)S(1)}, s32[129]{0:T(256)}, u32[]{:S(2)}) copy-start(s32[129]{0:T(256)} %bounds.3) | copy-start | bytes 1552
  51.9 5.6 %collective-permute-start.9 = (f32[44,8,128]{2,1,0:T(8,128)}, f32[44,8,128]{2,1,0:T(8,128)S(1)}, u32[]{:S(2)}, u32[]{:S(2)}) collective-permute-start(f32[44,8,128]{2,1,0:T(8,128)} %get-tuple-element.49), channel_id=1, source_target_pairs={{0,4},{1,5},{2,6},{3,7},{4,0},{5,1},{6,2},{7,3},{8,12},{9,13},{10,... | collective-permute-start | bytes 540680 | tf_op jit(solution)/shard_map/ppermute | solution.py:49
  52.3 9.4 %collective-permute-start.10 = (f32[44,8,128]{2,1,0:T(8,128)}, f32[44,8,128]{2,1,0:T(8,128)S(1)}, u32[]{:S(2)}, u32[]{:S(2)}) collective-permute-start(f32[44,8,128]{2,1,0:T(8,128)} %get-tuple-element.50), channel_id=1, source_target_pairs={{0,36},{1,37},{2,38},{3,39},{4,32},{5,33},{6,34},{7,35},{8,44},{9,... | collective-permute-start | bytes 540680 | tf_op jit(solution)/shard_map/ppermute | solution.py:49
  54.4 2.8 %collective-permute-start.11 = (f32[1,8,128]{2,1,0:T(8,128)S(1)}, f32[1,8,128]{2,1,0:T(8,128)S(1)}, u32[]{:S(2)}, u32[]{:S(2)}) collective-permute-start(f32[1,8,128]{2,1,0:T(8,128)S(1)} %get-tuple-element.51.peak), channel_id=1, source_target_pairs={{0,32},{1,33},{2,34},{3,35},{4,36},{5,37},{6,38},{7,39},{8,40},{9,... | collective-permute-start | bytes 12296 | tf_op jit(solution)/shard_map/ppermute | solution.py:49
  62.4 0.9 %copy-start.1 = (f32[6,2,40,128]{3,2,1,0:T(8,128)S(1)}, f32[6,2,40,128]{3,2,1,0:T(8,128)}, u32[]{:S(2)}) copy-start(f32[6,2,40,128]{3,2,1,0:T(8,128)} %copy-done) | copy-start | bytes 737284
  63.3 0.9 %copy-start.3 = (f32[6,2,40,128]{3,2,1,0:T(8,128)S(1)}, f32[6,2,40,128]{3,2,1,0:T(8,128)}, u32[]{:S(2)}) copy-start(f32[6,2,40,128]{3,2,1,0:T(8,128)} %copy-done.2) | copy-start | bytes 737284
  64.3 0.9 %copy-start.5 = (f32[6,2,40,128]{3,2,1,0:T(8,128)S(1)}, f32[6,2,40,128]{3,2,1,0:T(8,128)}, u32[]{:S(2)}) copy-start(f32[6,2,40,128]{3,2,1,0:T(8,128)} %copy-done.4) | copy-start | bytes 737284
  65.2 0.9 %copy-start.7 = (f32[6,2,40,128]{3,2,1,0:T(8,128)S(1)}, f32[6,2,40,128]{3,2,1,0:T(8,128)}, u32[]{:S(2)}) copy-start(f32[6,2,40,128]{3,2,1,0:T(8,128)} %copy-done.6) | copy-start | bytes 737284
  66.2 0.9 %copy-start.9 = (f32[44,8,128]{2,1,0:T(8,128)S(1)}, f32[44,8,128]{2,1,0:T(8,128)}, u32[]{:S(2)}) copy-start(f32[44,8,128]{2,1,0:T(8,128)} %copy-done.8) | copy-start | bytes 540676
  76.5 8.8 %collective-permute-start.12 = (f32[2,16,256]{2,1,0:T(8,128)}, f32[2,16,256]{2,1,0:T(8,128)S(1)}, u32[]{:S(2)}, u32[]{:S(2)}) collective-permute-start(f32[2,16,256]{2,1,0:T(8,128)} %get-tuple-element.52), channel_id=1, source_target_pairs={{1,2},{2,1},{3,4},{4,3},{5,6},{6,5},{7,8},{8,7},{9,10},{10,9},{11,... | collective-permute-start | bytes 98312 | tf_op jit(solution)/shard_map/ppermute | solution.py:49
  81.8 3.4 %collective-permute-start.13 = (f32[2,16,256]{2,1,0:T(8,128)S(1)}, f32[2,16,256]{2,1,0:T(8,128)S(1)}, u32[]{:S(2)}, u32[]{:S(2)}) collective-permute-start(f32[2,16,256]{2,1,0:T(8,128)S(1)} %get-tuple-element.53), channel_id=1, source_target_pairs={{0,1},{1,0},{2,3},{3,2},{4,5},{5,4},{6,7},{7,6},{8,9},{9,8},{10,11... | collective-permute-start | bytes 98312 | tf_op jit(solution)/shard_map/ppermute | solution.py:49
  (11 other events, 8.2 us)

commit v3 on v2

--- a/solution.py
+++ b/solution.py
@@ -96,10 +96,12 @@
     )
 
 
-def first_kernel(old, facts, ra, rb, peak):
+def first_kernel(old, levels, bounds, ra, rb, peak):
     d, tree, gi, gj, gk = where_am_i()
     sub, lane = iotas()
-    off, count = facts[0], facts[1]
+    start = bounds[d]
+    count = bounds[d + 1] - start
+    off = 8 * d - start
     even = d % 2 == 0
     slot_a = jnp.where(even, 8 + off, 0)
     slot_b = jnp.where(even, 0, 8 + off)
@@ -119,7 +121,8 @@
                 ra[24 + (g * 4 + q) * 2 + h] = groups[g]
     top = jnp.zeros((8, 128), F32)
     for s in range(10):
-        inv = jnp.where(s < count, jnp.left_shift(1, facts[2 + s]), 0).astype(F32)
+        level = levels[jnp.minimum(start + s, 1023)]
+        inv = jnp.where(s < count, jnp.left_shift(1, level), 0).astype(F32)
         part = jnp.zeros((8, 128), F32)
         for r in range(2):
             for h in range(2):
@@ -309,63 +312,63 @@
     return wide
 
 
-K_BLOCKS = 43
+K_BLOCKS = 38
 
 
 def k_place(kind, jt, b):
-    if kind == 0:
-        return jt * 6 + b
     if jt == 2:
-        return 38 + b
-    return (18 if kind < 3 else 28) + jt * 5 + b
-
-
-def pack_k(get, ka, kb, gk, lane):
-    even = gk % 2 == 0
-    near = lane % 16 < 8
-    k8 = lane % 8
-
-    def put(n, lo, hi):
-        ka[n] = jnp.where(even, hi, lo)
-        kb[n] = jnp.where(even, lo, hi)
-
-    def squeeze(first, last, kt):
+        return 30 + b
+    return (0, 10, 10, 20, 20)[kind] + jt * 5 + b
+
+
+class KPack:
+    def __init__(self, gk, lane):
+        self.even = gk % 2 == 0
+        self.near = lane % 16 < 8
+        self.k8 = lane % 8
+
+    def put(self, ka, kb, n, lo, hi):
+        ka[n] = jnp.where(self.even, hi, lo)
+        kb[n] = jnp.where(self.even, lo, hi)
+
+    def squeeze(self, first, last, kt):
         if kt == 0:
-            return jnp.where(near, first, rl(last, 8))
-        return jnp.where(near, rl(first, -8), last)
-
-    def join(kind, value, kt):
+            return jnp.where(self.near, first, rl(last, 8))
+        return jnp.where(self.near, rl(first, -8), last)
+
+    def join(self, kind, value, kt):
+        if kind == 0:
+            return value(0)
         if kind == 1:
-            nat, turn = (k8 < 5, 5) if kt == 0 else (k8 >= 3, -5)
+            nat, turn = (self.k8 < 5, 5) if kt == 0 else (self.k8 >= 3, -5)
         else:
-            nat, turn = (k8 < 4, 4) if kt == 0 else (k8 >= 4, -4)
+            nat, turn = (self.k8 < 4, 4) if kt == 0 else (self.k8 >= 4, -4)
         return jnp.where(nat, value(kind), rl(value(kind + 1), turn))
 
-    for jt in range(3):
-        for b in range(6):
-            sides = [squeeze(get(0, 2 * jt, kt, b), get(0, 2 * jt + 1, kt, b), kt) for kt in range(2)]
-            put(k_place(0, jt, b), *sides)
-    for jt in range(2):
-        for kind in (1, 3):
-            for b in range(5):
-                sides = [
-                    join(
-                        kind,
-                        lambda n: squeeze(get(n, 2 * jt, kt, b), get(n, 2 * jt + 1, kt, b), kt),
-                        kt,
-                    )
-                    for kt in range(2)
-                ]
-                put(k_place(kind, jt, b), *sides)
-    for b in range(5):
-        sides = []
-        for kt in range(2):
-            both = [
-                join(kind, lambda n: jnp.where(lane < 64, get(n, 4, kt, b), get(n, 5, kt, b)), kt)
-                for kind in (1, 3)
-            ]
-            sides.append(squeeze(*both, kt))
-        put(k_place(1, 2, b), *sides)
+    def block(self, kinds, get, ka, kb):
+        for jt in range(2):
+            for kind in kinds:
+                for b in range(5):
+                    sides = []
+                    for kt in range(2):
+
+                        def value(n):
+                            one, two = get(n, 2 * jt, kt, b), get(n, 2 * jt + 1, kt, b)
+                            return self.squeeze(one, two, kt)
+
+                        sides.append(self.join(kind, value, kt))
+                    self.put(ka, kb, k_place(kind, jt, b), *sides)
+
+    def halo(self, get, ka, kb):
+        for n in range(8):
+            sides = []
+            for kt in range(2):
+                packs = []
+                for m in (n, min(n + 8, 14)):
+                    kind, b = (0, 1, 3)[m // 5], m % 5
+                    packs.append(self.join(kind, lambda f: get(f, kt, b), kt))
+                sides.append(self.squeeze(*packs, kt))
+            self.put(ka, kb, 30 + n, *sides)
 
 
 def coefficient_kernel(neighbours, levels, refine, out, table, ratio):
@@ -400,22 +403,35 @@
         table[13 * 64 + pos] = jnp.left_shift(1, 6 - 2 * depth).astype(F32) * (2.0 / 64.0)
         return carry
 
-    lax.fori_loop(0, 64, one, 0)
+    lax.fori_loop(0, 64, one, 0, unroll=4)
 
     def expand(step, carry):
-        item, jp = step >> 2, step & 3
-        base = item * 64 + jp * 4
-        vals = {}
-        for ip in range(4):
-            v = [jnp.full((8, 128), table[base + ip * 16 + kp], F32) for kp in range(4)]
-            vals[ip] = (v[0], v[1], jnp.where(lane % 16 < 8, v[2], v[3]))
-        for kt in range(3):
-            out[item, jp, kt, 0] = vals[0][kt]
-            out[item, jp, kt, 1] = vals[1][kt]
-            out[item, jp, kt, 2] = jnp.where(sub < 4, vals[2][kt], vals[3][kt])
+        base = step * 64
+
+        def tiles(jp):
+            vals = []
+            for ip in range(4):
+                n = base + ip * 16 + jp * 4
+                v = [jnp.full((8, 128), table[n + kp], F32) for kp in range(4)]
+                vals.append((v[0], v[1], jnp.where(lane % 16 < 8, v[2], v[3])))
+            return [
+                [vals[0][kt], vals[1][kt], jnp.where(sub < 4, vals[2][kt], vals[3][kt])]
+                for kt in range(3)
+            ]
+
+        high, low = tiles(2), tiles(3)
+        sets = (
+            tiles(0),
+            tiles(1),
+            [[jnp.where(lane < 64, high[k][n], low[k][n]) for n in range(3)] for k in range(3)],
+        )
+        for jt in range(3):
+            for kt in range(3):
+                for n in range(3):
+                    out[step, jt, kt, n] = sets[jt][kt][n]
         return carry
 
-    lax.fori_loop(0, 56, expand, 0)
+    lax.fori_loop(0, 14, expand, 0)
 
 
 def coefficient(coef, item, jt, kt):
@@ -471,81 +487,120 @@
     def j_dn(self, x, prv, n):
         return rl(jnp.where(self.lane5 >= 128 - 16 * n, prv, x), 16 * n)
 
-    def change_ij(self, jq, kt, coef, c40, u1, c48, v48):
-        jt = tile_j(jq)
-        jn, jp = lax.rem(jq + 1, 6), lax.rem(jq + 5, 6)
-        odd = jq % 2 == 1
+    def change_j(self, c, cn, cp, u, un, up, m_dn, m_up):
         lane5 = self.lane5
-        c = c40(jq)
-        m_dn = jnp.where(odd, 1.0, coefficient(coef, 2, jt, kt))
-        m_up = jnp.where(odd, coefficient(coef, 3, jt, kt), 1.0)
-        up_m1 = jnp.where(lane5 >= 112, m_up, 1.0)
-        up_m2 = jnp.where(lane5 >= 96, m_up, 1.0)
-        dn_m1 = jnp.where(lane5 < 16, m_dn, 1.0)
-        dn_m2 = jnp.where(lane5 < 32, m_dn, 1.0)
-        cn, cp = c40(jn), c40(jp)
-        u = u1(jq)
-        change = face_change(
-            c, self.j_up(c, cn, 1) * up_m1, self.j_up(c, cn, 2) * up_m2,
-            self.j_dn(c, cp, 1) * dn_m1, self.j_dn(c, cp, 2) * dn_m2,
-            u, self.j_up(u, u1(jn), 1) * up_m1, self.j_dn(u, u1(jp), 1) * dn_m1,
+
+        def masked(x, m, at):
+            return x if m is None else x * jnp.where(at, m, 1.0)
+
+        return face_change(
+            c,
+            masked(self.j_up(c, cn, 1), m_up, lane5 >= 112),
+            masked(self.j_up(c, cn, 2), m_up, lane5 >= 96),
+            masked(self.j_dn(c, cp, 1), m_dn, lane5 < 16),
+            masked(self.j_dn(c, cp, 2), m_dn, lane5 < 32),
+            u,
+            masked(self.j_up(u, un, 1), m_up, lane5 >= 112),
+            masked(self.j_dn(u, up, 1), m_dn, lane5 < 16),
         )
-        m_dn, m_up = coefficient(coef, 0, jt, kt), coefficient(coef, 1, jt, kt)
+
+    def change_i(self, c48, v48, m_dn, m_up):
         up_m1, up_m2 = jnp.where(self.i_top1, m_up, 1.0), jnp.where(self.i_top2, m_up, 1.0)
         dn_m1, dn_m2 = jnp.where(self.i_bot1, m_dn, 1.0), jnp.where(self.i_bot2, m_dn, 1.0)
         wrap = self.wrap
-        return change + face_change(
-            c, wrap(rs(c48, -1)) * up_m1, wrap(rs(c48, -2)) * up_m2,
+        return face_change(
+            wrap(c48), wrap(rs(c48, -1)) * up_m1, wrap(rs(c48, -2)) * up_m2,
             wrap(rs(c48, 1)) * dn_m1, wrap(rs(c48, 2)) * dn_m2,
             wrap(v48), wrap(rs(v48, -1)) * up_m1, wrap(rs(v48, 1)) * dn_m1,
         )
 
 
-def tile_j(jq):
-    return jnp.where(jq < 4, jq >> 1, jq - 2)
-
-
-def early_kernel(
-    ext, ia, ib, ja, jb, peak, x16, coef,
+def inner_kernel(ext, ia, ib, coef, c40, u2, src, prs, u1, chg, ka, kb):
+    d, tree, gi, gj, gk = where_am_i()
+    sh = Shifts()
+    rows, pair = make_block(ext, ia, ib, gi, sh.sub)
+    dest = {0: c40, 2: u1, 3: u2, 4: src, 5: prs}
+    for jq in range(4):
+        for kt in range(2):
+            jt = jq // 2
+            c48 = jnp.concatenate([rows(0, jq, kt, b) for b in range(6)], axis=0)
+            v48 = jnp.concatenate(
+                [rows(1, jq, kt, b) for b in range(4)] + list(pair(1, jq, kt)), axis=0
+            )
+            for f, ref in dest.items():
+                if f == 0:
+                    ref[jq, kt] = sh.wrap(c48)
+                else:
+                    ref[jq, kt] = jnp.concatenate([rows(f, jq, kt, b) for b in range(5)], axis=0)
+            m_dn, m_up = coefficient(coef, 0, jt, kt), coefficient(coef, 1, jt, kt)
+            chg[jq, kt] = sh.change_i(c48, v48, m_dn, m_up)
+    for jq in (1, 2):
+        for kt in range(2):
+            m_dn = coefficient(coef, 2, jq // 2, kt) if jq == 2 else None
+            m_up = coefficient(coef, 3, jq // 2, kt) if jq == 1 else None
+            chg[jq, kt] = chg[jq, kt] + sh.change_j(
+                c40[jq, kt], c40[jq + 1, kt], c40[jq - 1, kt],
+                u1[jq, kt], u1[jq + 1, kt], u1[jq - 1, kt], m_dn, m_up,
+            )
+    kinds = (c40, u2, src)
+    KPack(gk, sh.lane).block(
+        (0, 1), lambda kind, jq, kt, b: kinds[kind][jq, kt, pl.ds(8 * b, 8), :], ka, kb
+    )
+
+
+def outer_kernel(
+    ja, jb, peak, x16, coef, c_in, u2_in, src_in, prs_in, u1_in, chg_in, ka_in, kb_in,
     c40, u2, src, prs, chg, ka, kb, peak_out,
-    c48, v48, u1,
 ):
     d, tree, gi, gj, gk = where_am_i()
     sh = Shifts()
-    sub = sh.sub
-    rows, pair = make_block(ext, ia, ib, gi, sub)
-    wide = make_wide(rows, ja, jb, gj)
-    dest = (c48, v48, u1, u2, src, prs)
-    for f in range(6):
-        for jq in range(6):
-            for kt in range(2):
-                for b in range(6 if f == 0 else 5):
-                    x = wide(f, jq, kt, b)
-                    if f == 1 and b == 4:
-                        hi, lo = pair(1, jq, kt) if jq < 4 else (x, x)
-                        v48[jq, kt, pl.ds(32, 8), :] = hi
-                        v48[jq, kt, pl.ds(40, 8), :] = lo
-                    else:
-                        dest[f][jq, kt, pl.ds(8 * b, 8), :] = x
-                    if f == 0 and b < 4:
-                        c40[jq, kt, pl.ds(8 * b, 8), :] = x
-                if f == 0:
-                    c40[jq, kt, pl.ds(32, 8), :] = jnp.where(
-                        sub < 4, c48[jq, kt, pl.ds(32, 8), :], c48[jq, kt, pl.ds(40, 8), :]
-                    )
-
-    def step(jq, carry):
+    wide = make_wide(None, ja, jb, gj)
+    low5 = sh.lane5 < 64
+    for jq in range(4):
         for kt in range(2):
-            chg[jq, kt] = sh.change_ij(
-                jq, kt, coef, lambda n: c40[n, kt], lambda n: u1[n, kt], c48[jq, kt], v48[jq, kt]
-            )
-        return carry
-
-    lax.fori_loop(0, 6, step, 0)
-    kinds = (c48, u2, src, chg, prs)
-    pack_k(
-        lambda kind, jq, kt, b: kinds[kind][jq, kt, pl.ds(8 * b, 8), :], ka, kb, gk, sh.lane
-    )
+            c40[jq, kt], u2[jq, kt] = c_in[jq, kt], u2_in[jq, kt]
+            src[jq, kt], prs[jq, kt] = src_in[jq, kt], prs_in[jq, kt]
+            if jq in (1, 2):
+                chg[jq, kt] = chg_in[jq, kt]
+    for n in range(20):
+        ka[n], kb[n] = ka_in[n], kb_in[n]
+
+    def whole(f, jq, kt, count=5):
+        return jnp.concatenate([wide(f, jq, kt, b) for b in range(count)], axis=0)
+
+    for kt in range(2):
+        for f, ref in ((3, u2), (4, src), (5, prs)):
+            ref[4, kt] = jnp.where(low5, whole(f, 4, kt), whole(f, 5, kt))
+        c48 = [whole(0, jq, kt, 6) for jq in (4, 5)]
+        c_high, c_low = sh.wrap(c48[0]), sh.wrap(c48[1])
+        c40[4, kt] = jnp.where(low5, c_high, c_low)
+        u_high, u_low = whole(2, 4, kt), whole(2, 5, kt)
+        m_dn, m_up = coefficient(coef, 0, 2, kt), coefficient(coef, 1, 2, kt)
+        side = []
+        for n in range(2):
+            v40 = whole(1, 4 + n, kt)
+            v48 = jnp.concatenate([v40, v40[32:]], axis=0)
+            side.append(sh.change_i(c48[n], v48, m_dn, m_up))
+        m_dn, m_up = coefficient(coef, 2, 2, kt), coefficient(coef, 3, 2, kt)
+        side[0] = side[0] + sh.change_j(
+            c_high, c_low, c_in[3, kt], u_high, u_low, u1_in[3, kt], m_dn, None
+        )
+        side[1] = side[1] + sh.change_j(
+            c_low, c_in[0, kt], c_high, u_low, u1_in[0, kt], u_high, None, m_up
+        )
+        chg[4, kt] = jnp.where(low5, side[0], side[1])
+        chg[0, kt] = chg_in[0, kt] + sh.change_j(
+            c_in[0, kt], c_in[1, kt], c_low, u1_in[0, kt], u1_in[1, kt], u_low,
+            coefficient(coef, 2, 0, kt), None,
+        )
+        chg[3, kt] = chg_in[3, kt] + sh.change_j(
+            c_in[3, kt], c_high, c_in[2, kt], u1_in[3, kt], u_high, u1_in[2, kt],
+            None, coefficient(coef, 3, 1, kt),
+        )
+    kinds = (c40, u2, src, chg, prs)
+    pack = KPack(gk, sh.lane)
+    pack.block((3,), lambda kind, jq, kt, b: kinds[kind][jq, kt, pl.ds(8 * b, 8), :], ka, kb)
+    pack.halo(lambda kind, kt, b: kinds[kind][4, kt, pl.ds(8 * b, 8), :], ka, kb)
     top = jnp.maximum(
         jnp.maximum(peak[0], x16[0]), jnp.maximum(ja[J_BLOCKS], jb[J_BLOCKS])
     )
@@ -564,45 +619,33 @@
     sub, lane, lane5, k16 = sh.sub, sh.lane, sh.lane5, sh.k16
     near = lane % 16 < 8
     k_even = gk % 2 == 0
-
-    def sides(kind, jt, b):
-        a, e = ka[k_place(kind, jt, b)], kb[k_place(kind, jt, b)]
-        low, high = jnp.where(k_even, a, e), jnp.where(k_even, e, a)
-        if jt == 2 and kind == 3:
-            low, high = rl(low, -8), rl(high, 0)
-        elif jt == 2 and kind == 1:
-            low, high = low, rl(high, 8)
-        return low, high
-
-    for b in range(6):
-        for jt in range(3):
-            low, high = sides(0, jt, b)
-            halves_of = (
-                jnp.where(near, low, rl(high, 8)), jnp.where(near, rl(low, -8), high)
-            )
-            for jq, x in zip((2 * jt, 2 * jt + 1), halves_of):
-                if b < 4:
-                    c_k[jq, pl.ds(8 * b, 8), :] = x
-                elif b == 4:
-                    c_k[jq, pl.ds(32, 8), :] = x
-                else:
-                    c_k[jq, pl.ds(32, 8), :] = jnp.where(sub < 4, c_k[jq, pl.ds(32, 8), :], x)
-    dest = {1: u2, 2: src, 3: chg_k, 4: p_k}
-    for b in range(5):
-        for kind in (1, 3):
-            turn = 5 if kind == 1 else 4
-            for jt in range(3):
-                low, high = sides(kind, jt, b)
-                for n in range(2):
+    dest = (c_k, u2, src, chg_k, p_k)
+
+    def both_sides(n):
+        a, e = ka[n], kb[n]
+        return jnp.where(k_even, a, e), jnp.where(k_even, e, a)
+
+    for kind in (0, 1, 3):
+        turn = (0, 5, 0, 4)[kind]
+        for b in range(5):
+            rows = pl.ds(8 * b, 8)
+            for n in range(1 if kind == 0 else 2):
+                ref = dest[kind + n]
+                for jt in range(2):
+                    low, high = both_sides(k_place(kind, jt, b))
                     if n == 1:
                         low, high = rl(low, -turn), rl(high, turn)
-                    if jt == 2:
-                        first = last = jnp.where(near, low, high)
-                    else:
-                        first = jnp.where(near, low, rl(high, 8))
-                        last = jnp.where(near, rl(low, -8), high)
-                    dest[kind + n][2 * jt, pl.ds(8 * b, 8), :] = first
-                    dest[kind + n][2 * jt + 1, pl.ds(8 * b, 8), :] = last
+                    ref[2 * jt, rows, :] = jnp.where(near, low, rl(high, 8))
+                    ref[2 * jt + 1, rows, :] = jnp.where(near, rl(low, -8), high)
+                m = (0, 1, 0, 2)[kind] * 5 + b
+                low, high = both_sides(30 + m % 8)
+                if m < 8:
+                    high = rl(high, 8)
+                else:
+                    low = rl(low, -8)
+                if n == 1:
+                    low, high = rl(low, -turn), rl(high, turn)
+                ref[4, rows, :] = jnp.where(near, low, high)
 
     def c40(jq, kt):
         return c_k[jq] if kt == 2 else c_in[jq, kt]
@@ -618,7 +661,7 @@
     step = jnp.concatenate([step] * 5, axis=0)
 
     def advance(jq, carry):
-        jt = tile_j(jq)
+        jt = jq >> 1
         for kt in range(3):
             kn, kp = (kt + 1) % 3, (kt + 2) % 3
             change = chg_k[jq] if kt == 2 else chg_in[jq, kt]
@@ -636,18 +679,18 @@
             mob[jq, kt] = 1.0 / (RHO_GAS + (RHO_LIQ - RHO_GAS) * a)
         return carry
 
-    lax.fori_loop(0, 6, advance, 0)
+    lax.fori_loop(0, 5, advance, 0)
 
     def weigh(jq, carry):
-        jt = tile_j(jq)
-        jn, jp = lax.rem(jq + 1, 6), lax.rem(jq + 5, 6)
-        odd = jq % 2 == 1
+        jt = jq >> 1
+        jn, jp = lax.rem(jq + 1, 5), lax.rem(jq + 4, 5)
+        begins, ends = jq % 2 == 0, (jq % 2 == 1) | (jq == 4)
         for kt in range(3):
             kn, kp = (kt + 1) % 3, (kt + 2) % 3
             mi_dn = jnp.where(sh.i_bot1, coefficient(coef, 0, jt, kt), 1.0)
             mi_up = jnp.where(sh.i_top1, coefficient(coef, 1, jt, kt), 1.0)
-            at_dn = (lane5 < 16) & jnp.logical_not(odd)
-            at_up = (lane5 >= 112) & odd
+            at_dn = (lane5 < 16) & begins
+            at_up = (lane5 >= 112) & ends
             mj_dn = jnp.where(at_dn, coefficient(coef, 2, jt, kt), 1.0)
             mj_up = jnp.where(at_up, coefficient(coef, 3, jt, kt), 1.0)
             h = hgt[jq, kt]
@@ -682,7 +725,7 @@
             rhs[jq, kt] = right * coefficient(coef, 13, jt, kt) * inv
         return carry
 
-    lax.fori_loop(0, 6, weigh, 0)
+    lax.fori_loop(0, 5, weigh, 0)
 
     for sweep in range(SWEEPS):
         new = p0 if sweep % 2 == 0 else p1
@@ -695,7 +738,7 @@
             return p_k[jq] if kt == 2 else p_in[jq, kt]
 
         def relax(jq, carry, old=old, new=new, last=last):
-            jn, jp = lax.rem(jq + 1, 6), lax.rem(jq + 5, 6)
+            jn, jp = lax.rem(jq + 1, 5), lax.rem(jq + 4, 5)
             for kt in range(2 if last else 3):
                 kn, kp = (kt + 1) % 3, (kt + 2) % 3
                 p = old(jq, kt)
@@ -712,7 +755,7 @@
                     new[jq, kt] = total
             return carry
 
-        lax.fori_loop(0, 4 if last else 6, relax, 0)
+        lax.fori_loop(0, 4 if last else 5, relax, 0)
 
     even = d % 2 == 0
     for h in range(2):
@@ -765,7 +808,7 @@
         scratch_shapes=list(scratch),
         compiler_params=pltpu.CompilerParams(vmem_limit_bytes=mib * 1024 * 1024),
         cost_estimate=pl.CostEstimate(
-            flops=micros * 1000000, bytes_accessed=micros * 3000000, transcendentals=0
+            flops=micros * 100000, bytes_accessed=micros * 100000, transcendentals=0
         ),
     )(*args)
 
@@ -774,10 +817,9 @@
     d = lax.axis_index("row") * 16 + lax.axis_index("col")
     one = blocks(1)
     old = jnp.concatenate([volume[None], velocity, source[None], pressure_prev[None]], axis=0)
-    start = bounds_old[d]
-    own_levels = lax.dynamic_slice_in_dim(jnp.pad(levels, (0, 16)), start, 14, 0)
-    facts = jnp.concatenate([jnp.stack([8 * d - start, bounds_old[d + 1] - start]), own_levels])
-    ra, rb, peak = call(first_kernel, [VM, SM], (blocks(57), blocks(24), one), (old, facts))
+    ra, rb, peak = call(
+        first_kernel, [VM, SM, SM], (blocks(57), blocks(24), one), (old, levels, bounds_old)
+    )
     x8, x9 = send(peak, flip_pairs(8)), send(peak, flip_pairs(9))
     rb, ra = send(rb, ODD_PAIRS), send(ra, EVEN_PAIRS)
     own, mine, flags, ib = call(
@@ -808,24 +850,30 @@
     coef = call(
         coefficient_kernel,
         [SM] * 3,
-        shape(14, 4, 3, 3, 8, 128),
+        shape(14, 3, 3, 3, 8, 128),
         (neighbours.reshape(-1), levels, refine),
         [pltpu.SMEM((14 * 64,), F32), pltpu.SMEM((7,), F32)],
         5,
     )
-    part, part_tall = (6, 2, 40, 128), (6, 2, 48, 128)
+    inner = call(
+        inner_kernel,
+        [VM] * 4,
+        (shape(4, 2, 40, 128),) * 6 + (blocks(20),) * 2,
+        (ext, ia, ib, coef),
+        (),
+        2,
+    )
     *early, ka, kb, peak = call(
-        early_kernel,
-        [VM] * 8,
-        (shape(*part),) * 5 + (blocks(K_BLOCKS + 1),) * 2 + (one,),
-        (ext, ia, ib, ja, jb, peak, x16, coef),
-        [pltpu.VMEM(part_tall, F32)] * 2 + [pltpu.VMEM(part, F32)],
-        2,
-        12,
+        outer_kernel,
+        [VM] * 13,
+        (shape(5, 2, 40, 128),) * 5 + (blocks(K_BLOCKS + 1),) * 2 + (one,),
+        (ja, jb, peak, x16, coef, *inner),
+        (),
+        1,
     )
     x32 = send(peak, flip_pairs(32))
     ka, kb = send(ka, axis_pairs(2, 0)), send(kb, axis_pairs(2, 1))
-    halo, grid = (6, 40, 128), (6, 3, 40, 128)
+    halo, grid = (5, 40, 128), (5, 3, 40, 128)
     adv, prs, sa, sb = call(
         main_kernel,
         [VM] * 10,

time: 86.8 us -> 64.4 us (0.74)
  local copies, waits for them, and re-layouts: 15.6 us -> 1.18 us
  Pallas kernels: 20.5 us -> 15.8 us
  between operations: 6.57 us -> 2.83 us
  starting transfers between devices: 26.9 us -> 27.9 us
    unnamed x43 -> x11, local copies, waits for them, and re-layouts: 13.1 us -> 0.24 us
    pallas_call x9 -> x10, Pallas kernels: 20.5 us -> 15.8 us  [call(): pl.pallas_call(kernel, out_shape=outs, in_specs=specs, out_specs=jax.tree...]
    ppermute x14, starting transfers between devices: 26.9 us -> 27.9 us  [send(): return lax.ppermute(x, AXES, pairs)]
  transfers between devices with their start and end apart: 14 -> 14, of which waited for: 6 -> 6; matrix products, arithmetic and copies ran while one was open for 1% -> 2% of each run, Pallas kernels for 8% -> 11%
where the time goes in v3:
time: 64.4 us; the launch traced here: 64.2 us
  starting transfers between devices  27.9 us (43%)
  Pallas kernels  15.8 us (25%)
  waiting for transfers between devices  14.3 us (22%)
  between operations  2.83 us (4%)
  other arithmetic  2.18 us (3%)
  local copies, waits for them, and re-layouts  1.18 us (2%)
    ppermute x14, starting transfers between devices, send(): return lax.ppermute(x, AXES, pairs)  27.9 us
    pallas_call x10, Pallas kernels, call(): pl.pallas_call(kernel, out_shape=outs, in_specs=specs, out_specs=jax.tree...  15.8 us
    ppermute x14, waiting for transfers between devices, send(): return lax.ppermute(x, AXES, pairs)  14.3 us
    concatenate x1, other arithmetic, local(): jnp.concatenate([volume[None], velocity, source[None], pressure_prev[None...  1.34 us
  transfers between devices with their start and end apart: 14, of which 6 were waited for; matrix products, arithmetic and copies ran while one was open for 2% of the time, Pallas kernels for 11%

profile of v3, /device:TPU:1, one launch (start us, length us, event | category | flops | bytes accessed | tf_op | source)
XLA Modules:
  0.0 64.2 jit_solution(16548248279300055097)
XLA Ops:
  0.7 1.3 %pad_maximum_fusion.old = f32[6,10,16,256]{3,2,1,0:T(8,128)S(1)} fusion(f32[1,10,16,256]{3,2,1,0:T(8,128)} %bitcast.13, f32[1,10,16,256]{3,2,1,0:T(8,128)} %bitcast.14, f32[3,10,16,256]{3,2,1,0:T(8,128)} %param.10, f32[1,10,16,256]{3,2,1,0:T(8,128)} %bitcast.15), kind=kLoop, calls=%fused_computation | loop fusion | flops 737280 | bytes 1966080 | tf_op jit(solution)/shard_map/concatenate | solution.py:819
  2.0 0.7 %shard_map.105 = (f32[57,8,128]{2,1,0:T(8,128)S(1)}, f32[24,8,128]{2,1,0:T(8,128)S(1)}, f32[1,8,128]{2,1,0:T(8,128)S(1)}) custom-call(f32[6,10,16,256]{3,2,1,0:T(8,128)S(1)} %pad_maximum_fusion.old, s32[1024]{0:T(1024)S(1)} %copy-done, s32[129]{0:T(256)S(1)} %copy-done.2), custom_call_target="tpu_custom_call" | custom-call | flops 100000 | bytes 100000 | tf_op jit(solution)/shard_map/pallas_call | solution.py:803
  2.7 2.1 %collective-permute-start = (f32[57,8,128]{2,1,0:T(8,128)S(1)}, f32[57,8,128]{2,1,0:T(8,128)S(1)}, u32[]{:S(2)}, u32[]{:S(2)}) collective-permute-start(f32[57,8,128]{2,1,0:T(8,128)S(1)} %get-tuple-element.41), channel_id=1, source_target_pairs={{0,1},{1,0},{2,3},{3,2},{4,5},{5,4},{6,7},{7,6},{8,9},{9,8},{10,11... | collective-permute-start | bytes 700424 | tf_op jit(solution)/shard_map/ppermute | solution.py:49
  4.8 7.0 %collective-permute-start.1 = (f32[24,8,128]{2,1,0:T(8,128)S(1)}, f32[24,8,128]{2,1,0:T(8,128)S(1)}, u32[]{:S(2)}, u32[]{:S(2)}) collective-permute-start(f32[24,8,128]{2,1,0:T(8,128)S(1)} %get-tuple-element.42), channel_id=1, source_target_pairs={{1,2},{2,1},{3,4},{4,3},{5,6},{6,5},{7,8},{8,7},{9,10},{10,9},{11,... | collective-permute-start | bytes 294920 | tf_op jit(solution)/shard_map/ppermute | solution.py:49
  12.0 0.7 %shard_map.104 = (f32[6,4,2,32,128]{4,3,2,1,0:T(8,128)S(1)}, f32[8,8,128]{2,1,0:T(8,128)S(1)}, f32[6,8,128]{2,1,0:T(8,128)S(1)}, f32[32,8,128]{2,1,0:T(8,128)S(1)}) custom-call(f32[6,10,16,256]{3,2,1,0:T(8,128)S(1)} %pad_maximum_fusion.old, s32[129]{0:T(256)S(1)} %copy-done.2), custom_call_target="tpu_custom_call" | custom-call | flops 100000 | bytes 100000 | tf_op jit(solution)/shard_map/pallas_call | solution.py:803
  12.7 3.5 %collective-permute-done.2.x8 = f32[1,8,128]{2,1,0:T(8,128)S(1)} collective-permute-done((f32[1,8,128]{2,1,0:T(8,128)S(1)}, f32[1,8,128]{2,1,0:T(8,128)S(1)}, u32[]{:S(2)}, u32[]{:S(2)}) %collective-permute-start.2) | collective-permute-done | bytes 4128 | tf_op jit(solution)/shard_map/ppermute | solution.py:49
  16.2 0.7 %collective-permute-done.3.x9 = f32[1,8,128]{2,1,0:T(8,128)S(1)} collective-permute-done((f32[1,8,128]{2,1,0:T(8,128)S(1)}, f32[1,8,128]{2,1,0:T(8,128)S(1)}, u32[]{:S(2)}, u32[]{:S(2)}) %collective-permute-start.3) | collective-permute-done | bytes 4128 | tf_op jit(solution)/shard_map/ppermute | solution.py:49
  16.9 3.7 %collective-permute-start.4 = (f32[32,8,128]{2,1,0:T(8,128)S(1)}, f32[32,8,128]{2,1,0:T(8,128)S(1)}, u32[]{:S(2)}, u32[]{:S(2)}) collective-permute-start(f32[32,8,128]{2,1,0:T(8,128)S(1)} %get-tuple-element.47), channel_id=1, source_target_pairs={{0,64},{1,8},{2,66},{3,10},{4,68},{5,12},{6,70},{7,14},{8,1},{9,73... | collective-permute-start | bytes 393224 | tf_op jit(solution)/shard_map/ppermute | solution.py:49
  20.8 4.1 %collective-permute-done.5.x64 = f32[1,8,128]{2,1,0:T(8,128)S(1)} collective-permute-done((f32[1,8,128]{2,1,0:T(8,128)S(1)}, f32[1,8,128]{2,1,0:T(8,128)S(1)}, u32[]{:S(2)}, u32[]{:S(2)}) %collective-permute-start.5) | collective-permute-done | bytes 4128 | tf_op jit(solution)/shard_map/ppermute | solution.py:49
  25.2 6.2 %collective-permute-start.7 = (f32[38,8,128]{2,1,0:T(8,128)S(1)}, f32[38,8,128]{2,1,0:T(8,128)S(1)}, u32[]{:S(2)}, u32[]{:S(2)}) collective-permute-start(f32[38,8,128]{2,1,0:T(8,128)S(1)} %get-tuple-element.50), channel_id=1, source_target_pairs={{0,18},{1,19},{2,16},{3,17},{4,22},{5,23},{6,20},{7,21},{8,26},{9,... | collective-permute-start | bytes 466952 | tf_op jit(solution)/shard_map/ppermute | solution.py:49
  32.0 5.1 %shard_map.109.coef = f32[14,3,3,3,8,128]{5,4,3,2,1,0:T(8,128)S(1)} custom-call(s32[6144]{0:T(1024)S(1)} %reshape.17.neighbours, s32[1024]{0:T(1024)S(1)} %copy-done, s32[1024]{0:T(1024)S(1)} %copy-done.1), custom_call_target="tpu_custom_call" | custom-call | flops 500000 | bytes 500000 | tf_op jit(solution)/shard_map/pallas_call | solution.py:803
  37.1 0.7 %shard_map.110 = (f32[4,2,40,128]{3,2,1,0:T(8,128)S(1)}, f32[4,2,40,128]{3,2,1,0:T(8,128)S(1)}, f32[4,2,40,128]{3,2,1,0:T(8,128)S(1)}, f32[4,2,40,128]{3,2,1,0:T...) custom-call(f32[6,4,2,32,128]{4,3,2,1,0:T(8,128)S(1)} %get-tuple-ele, ...), custom_call_target="tpu_custom_call" | custom-call | flops 200000 | bytes 200000 | tf_op jit(solution)/shard_map/pallas_call | solution.py:803
  37.9 1.4 %shard_map.111 = (f32[5,2,40,128]{3,2,1,0:T(8,128)S(1)}, f32[5,2,40,128]{3,2,1,0:T(8,128)S(1)}, f32[5,2,40,128]{3,2,1,0:T(8,128)S(1)}, f32[5,2,40,128]{3,2,1,0:T...) custom-call(f32[38,8,128]{2,1,0:T(8,128)S(1)} %collective-permute-do, ...), custom_call_target="tpu_custom_call" | custom-call | flops 100000 | bytes 100000 | tf_op jit(solution)/shard_map/pallas_call | solution.py:803
  39.3 1.2 %collective-permute-start.10 = (f32[39,8,128]{2,1,0:T(8,128)S(1)}, f32[39,8,128]{2,1,0:T(8,128)S(1)}, u32[]{:S(2)}, u32[]{:S(2)}) collective-permute-start(f32[39,8,128]{2,1,0:T(8,128)S(1)} %get-tuple-element.66), channel_id=1, source_target_pairs={{0,36},{1,37},{2,38},{3,39},{4,32},{5,33},{6,34},{7,35},{8,44},{9,... | collective-permute-start | bytes 479240 | tf_op jit(solution)/shard_map/ppermute | solution.py:49
  40.5 0.8 %collective-permute-start.9 = (f32[39,8,128]{2,1,0:T(8,128)S(1)}, f32[39,8,128]{2,1,0:T(8,128)S(1)}, u32[]{:S(2)}, u32[]{:S(2)}) collective-permute-start(f32[39,8,128]{2,1,0:T(8,128)S(1)} %get-tuple-element.65), channel_id=1, source_target_pairs={{0,4},{1,5},{2,6},{3,7},{4,0},{5,1},{6,2},{7,3},{8,12},{9,13},{10,... | collective-permute-start | bytes 479240 | tf_op jit(solution)/shard_map/ppermute | solution.py:49
  41.3 0.7 %collective-permute-start.11 = (f32[1,8,128]{2,1,0:T(8,128)S(1)}, f32[1,8,128]{2,1,0:T(8,128)S(1)}, u32[]{:S(2)}, u32[]{:S(2)}) collective-permute-start(f32[1,8,128]{2,1,0:T(8,128)S(1)} %get-tuple-element.67.peak), channel_id=1, source_target_pairs={{0,32},{1,33},{2,34},{3,35},{4,36},{5,37},{6,38},{7,39},{8,40},{9,... | collective-permute-start | bytes 12296 | tf_op jit(solution)/shard_map/ppermute | solution.py:49
  42.0 0.6 fusion
  44.5 0.9 %collective-permute-done.10.kb = f32[39,8,128]{2,1,0:T(8,128)S(1)} collective-permute-done((f32[39,8,128]{2,1,0:T(8,128)S(1)}, f32[39,8,128]{2,1,0:T(8,128)S(1)}, u32[]{:S(2)}, u32[]{:S(2)}) %collective-permute-start.10) | collective-permute-done | bytes 159776 | tf_op jit(solution)/shard_map/ppermute | solution.py:49
  45.4 3.0 %collective-permute-done.9.ka = f32[39,8,128]{2,1,0:T(8,128)S(1)} collective-permute-done((f32[39,8,128]{2,1,0:T(8,128)S(1)}, f32[39,8,128]{2,1,0:T(8,128)S(1)}, u32[]{:S(2)}, u32[]{:S(2)}) %collective-permute-start.9) | collective-permute-done | bytes 159776 | tf_op jit(solution)/shard_map/ppermute | solution.py:49
  48.4 6.4 %shard_map.112 = (f32[4,2,32,128]{3,2,1,0:T(8,128)S(1)}, f32[4,2,32,128]{3,2,1,0:T(8,128)S(1)}, f32[2,16,256]{2,1,0:T(8,128)S(1)}, f32[2,16,256]{2,1,0:T(8,128)S(1)}) custom-call(f32[5,2,40,128]{3,2,1,0:T(8,128)S(1)} %get-tuple-element.60.c_in, f32[5,2,40,128]{3,2,1,0:T(8,128)S(1)} %get-tuple-element.61.u_in, f32[5,2,40,128]{3,2,1,0:T(8,128)S(1)} %get-tuple-element.62.s_in, ...), custom_call_target="tpu_custom_call" | custom-call | flops 800000 | bytes 800000 | tf_op jit(solution)/shard_map/pallas_call | solution.py:803
  54.8 5.6 %collective-permute-start.12 = (f32[2,16,256]{2,1,0:T(8,128)S(1)}, f32[2,16,256]{2,1,0:T(8,128)S(1)}, u32[]{:S(2)}, u32[]{:S(2)}) collective-permute-start(f32[2,16,256]{2,1,0:T(8,128)S(1)} %get-tuple-element.68), channel_id=1, source_target_pairs={{1,2},{2,1},{3,4},{4,3},{5,6},{6,5},{7,8},{8,7},{9,10},{10,9},{11,... | collective-permute-start | bytes 98312 | tf_op jit(solution)/shard_map/ppermute | solution.py:49
  60.6 0.6 shard_map.113
  61.2 2.2 %collective-permute-done.12 = f32[2,16,256]{2,1,0:T(8,128)S(1)} collective-permute-done((f32[2,16,256]{2,1,0:T(8,128)S(1)}, f32[2,16,256]{2,1,0:T(8,128)S(1)}, u32[]{:S(2)}, u32[]{:S(2)}) %collective-permute-start.12) | collective-permute-done | bytes 32800 | tf_op jit(solution)/shard_map/ppermute | solution.py:49
  63.4 0.8 %select_select_fusion = (f32[10,16,256]{2,1,0:T(8,128)}, f32[10,16,256]{2,1,0:T(8,128)}) fusion(f32[10,16,256]{2,1,0:T(8,128)S(1)} %get-tuple-element.73, f32[16,256]{1,0:T(8,128)S(1)} %get-tuple-element.78, f32[16,256]{1,0:T(8,128)S(1)} %get-tuple-element.85, pred[10]{0:T(512)(128)(4,1)S(1)} %get-tuple-element.86, pred[10]{0:T(512)(128)(4,1)S(1)} %get-tuple-element.87, ...), kind=kLoop, calls=%fused_computation.1 | loop fusion | flops 163840 | bytes 720916 | tf_op jit(solution)/shard_map/jit(_where)/select_n | solution.py:897
  (32 shorter events, 1.5 us)
Async XLA Ops:
  0.6 1.4 %copy-start.2 = (s32[129]{0:T(256)S(1)}, s32[129]{0:T(256)}, u32[]{:S(2)}) copy-start(s32[129]{0:T(256)} %bounds.4) | copy-start | bytes 1552
  0.6 1.4 %copy-start = (s32[1024]{0:T(1024)S(1)}, s32[1024]{0:T(1024)}, u32[]{:S(2)}) copy-start(s32[1024]{0:T(1024)} %levels.3) | copy-start | bytes 12292
  2.7 14.2 %collective-permute-start = (f32[57,8,128]{2,1,0:T(8,128)S(1)}, f32[57,8,128]{2,1,0:T(8,128)S(1)}, u32[]{:S(2)}, u32[]{:S(2)}) collective-permute-start(f32[57,8,128]{2,1,0:T(8,128)S(1)} %get-tuple-element.41), channel_id=1, source_target_pairs={{0,1},{1,0},{2,3},{3,2},{4,5},{5,4},{6,7},{7,6},{8,9},{9,8},{10,11... | collective-permute-start | bytes 700424 | tf_op jit(solution)/shard_map/ppermute | solution.py:49
  4.8 12.0 %collective-permute-start.1 = (f32[24,8,128]{2,1,0:T(8,128)S(1)}, f32[24,8,128]{2,1,0:T(8,128)S(1)}, u32[]{:S(2)}, u32[]{:S(2)}) collective-permute-start(f32[24,8,128]{2,1,0:T(8,128)S(1)} %get-tuple-element.42), channel_id=1, source_target_pairs={{1,2},{2,1},{3,4},{4,3},{5,6},{6,5},{7,8},{8,7},{9,10},{10,9},{11,... | collective-permute-start | bytes 294920 | tf_op jit(solution)/shard_map/ppermute | solution.py:49
  11.8 4.4 %collective-permute-start.2 = (f32[1,8,128]{2,1,0:T(8,128)S(1)}, f32[1,8,128]{2,1,0:T(8,128)S(1)}, u32[]{:S(2)}, u32[]{:S(2)}) collective-permute-start(f32[1,8,128]{2,1,0:T(8,128)S(1)} %get-tuple-element.46.peak), channel_id=1, source_target_pairs={{0,8},{1,9},{2,10},{3,11},{4,12},{5,13},{6,14},{7,15},{8,0},{9,1},... | collective-permute-start | bytes 12296 | tf_op jit(solution)/shard_map/ppermute | solution.py:49
  11.9 4.9 %collective-permute-start.3 = (f32[1,8,128]{2,1,0:T(8,128)S(1)}, f32[1,8,128]{2,1,0:T(8,128)S(1)}, u32[]{:S(2)}, u32[]{:S(2)}) collective-permute-start(f32[1,8,128]{2,1,0:T(8,128)S(1)} %get-tuple-element.46.peak), channel_id=1, source_target_pairs={{0,9},{1,8},{2,11},{3,10},{4,13},{5,12},{6,15},{7,14},{8,1},{9,0},... | collective-permute-start | bytes 12296 | tf_op jit(solution)/shard_map/ppermute | solution.py:49
  12.7 18.7 %copy-start.4 = (s32[1024,6]{0,1:T(8,128)S(1)}, s32[1024,6]{0,1:T(8,128)}, u32[]{:S(2)}) copy-start(s32[1024,6]{0,1:T(8,128)} %param.13) | copy-start | bytes 73732
  16.9 7.9 %collective-permute-start.4 = (f32[32,8,128]{2,1,0:T(8,128)S(1)}, f32[32,8,128]{2,1,0:T(8,128)S(1)}, u32[]{:S(2)}, u32[]{:S(2)}) collective-permute-start(f32[32,8,128]{2,1,0:T(8,128)S(1)} %get-tuple-element.47), channel_id=1, source_target_pairs={{0,64},{1,8},{2,66},{3,10},{4,68},{5,12},{6,70},{7,14},{8,1},{9,73... | collective-permute-start | bytes 393224 | tf_op jit(solution)/shard_map/ppermute | solution.py:49
  20.6 4.3 %collective-permute-start.5 = (f32[1,8,128]{2,1,0:T(8,128)S(1)}, f32[1,8,128]{2,1,0:T(8,128)S(1)}, u32[]{:S(2)}, u32[]{:S(2)}) collective-permute-start(f32[1,8,128]{2,1,0:T(8,128)S(1)} %get-tuple-element.48.peak), channel_id=1, source_target_pairs={{0,64},{1,65},{2,66},{3,67},{4,68},{5,69},{6,70},{7,71},{8,72},{9,... | collective-permute-start | bytes 12296 | tf_op jit(solution)/shard_map/ppermute | solution.py:49
  20.7 11.3 %copy-start.1 = (s32[1024]{0:T(1024)S(1)}, s32[1024]{0:T(1024)}, u32[]{:S(2)}) copy-start(s32[1024]{0:T(1024)} %refine.1) | copy-start | bytes 12292
  25.0 12.9 %collective-permute-start.6 = (f32[38,8,128]{2,1,0:T(8,128)S(1)}, f32[38,8,128]{2,1,0:T(8,128)S(1)}, u32[]{:S(2)}, u32[]{:S(2)}) collective-permute-start(f32[38,8,128]{2,1,0:T(8,128)S(1)} %get-tuple-element.49), channel_id=1, source_target_pairs={{0,2},{1,3},{2,0},{3,1},{4,6},{5,7},{6,4},{7,5},{8,10},{9,11},{10,... | collective-permute-start | bytes 466952 | tf_op jit(solution)/shard_map/ppermute | solution.py:49
  25.2 12.6 %collective-permute-start.7 = (f32[38,8,128]{2,1,0:T(8,128)S(1)}, f32[38,8,128]{2,1,0:T(8,128)S(1)}, u32[]{:S(2)}, u32[]{:S(2)}) collective-permute-start(f32[38,8,128]{2,1,0:T(8,128)S(1)} %get-tuple-element.50), channel_id=1, source_target_pairs={{0,18},{1,19},{2,16},{3,17},{4,22},{5,23},{6,20},{7,21},{8,26},{9,... | collective-permute-start | bytes 466952 | tf_op jit(solution)/shard_map/ppermute | solution.py:49
  31.4 6.4 %collective-permute-start.8 = (f32[1,8,128]{2,1,0:T(8,128)S(1)}, f32[1,8,128]{2,1,0:T(8,128)S(1)}, u32[]{:S(2)}, u32[]{:S(2)}) collective-permute-start(f32[1,8,128]{2,1,0:T(8,128)S(1)} %get-tuple-element.51.peak), channel_id=1, source_target_pairs={{0,16},{1,17},{2,18},{3,19},{4,20},{5,21},{6,22},{7,23},{8,24},{9,... | collective-permute-start | bytes 12296 | tf_op jit(solution)/shard_map/ppermute | solution.py:49
  37.8 4.2 %copy-start.3 = (s32[129]{0:T(256)S(1)}, s32[129]{0:T(256)}, u32[]{:S(2)}) copy-start(s32[129]{0:T(256)} %bounds.5) | copy-start | bytes 1552
  39.3 6.1 %collective-permute-start.10 = (f32[39,8,128]{2,1,0:T(8,128)S(1)}, f32[39,8,128]{2,1,0:T(8,128)S(1)}, u32[]{:S(2)}, u32[]{:S(2)}) collective-permute-start(f32[39,8,128]{2,1,0:T(8,128)S(1)} %get-tuple-element.66), channel_id=1, source_target_pairs={{0,36},{1,37},{2,38},{3,39},{4,32},{5,33},{6,34},{7,35},{8,44},{9,... | collective-permute-start | bytes 479240 | tf_op jit(solution)/shard_map/ppermute | solution.py:49
  40.5 7.9 %collective-permute-start.9 = (f32[39,8,128]{2,1,0:T(8,128)S(1)}, f32[39,8,128]{2,1,0:T(8,128)S(1)}, u32[]{:S(2)}, u32[]{:S(2)}) collective-permute-start(f32[39,8,128]{2,1,0:T(8,128)S(1)} %get-tuple-element.65), channel_id=1, source_target_pairs={{0,4},{1,5},{2,6},{3,7},{4,0},{5,1},{6,2},{7,3},{8,12},{9,13},{10,... | collective-permute-start | bytes 479240 | tf_op jit(solution)/shard_map/ppermute | solution.py:49
  41.3 3.3 %collective-permute-start.11 = (f32[1,8,128]{2,1,0:T(8,128)S(1)}, f32[1,8,128]{2,1,0:T(8,128)S(1)}, u32[]{:S(2)}, u32[]{:S(2)}) collective-permute-start(f32[1,8,128]{2,1,0:T(8,128)S(1)} %get-tuple-element.67.peak), channel_id=1, source_target_pairs={{0,32},{1,33},{2,34},{3,35},{4,36},{5,37},{6,38},{7,39},{8,40},{9,... | collective-permute-start | bytes 12296 | tf_op jit(solution)/shard_map/ppermute | solution.py:49
  54.8 8.6 %collective-permute-start.12 = (f32[2,16,256]{2,1,0:T(8,128)S(1)}, f32[2,16,256]{2,1,0:T(8,128)S(1)}, u32[]{:S(2)}, u32[]{:S(2)}) collective-permute-start(f32[2,16,256]{2,1,0:T(8,128)S(1)} %get-tuple-element.68), channel_id=1, source_target_pairs={{1,2},{2,1},{3,4},{4,3},{5,6},{6,5},{7,8},{8,7},{9,10},{10,9},{11,... | collective-permute-start | bytes 98312 | tf_op jit(solution)/shard_map/ppermute | solution.py:49
  60.5 2.9 %collective-permute-start.13 = (f32[2,16,256]{2,1,0:T(8,128)S(1)}, f32[2,16,256]{2,1,0:T(8,128)S(1)}, u32[]{:S(2)}, u32[]{:S(2)}) collective-permute-start(f32[2,16,256]{2,1,0:T(8,128)S(1)} %get-tuple-element.69), channel_id=1, source_target_pairs={{0,1},{1,0},{2,3},{3,2},{4,5},{5,4},{6,7},{7,6},{8,9},{9,8},{10,11... | collective-permute-start | bytes 98312 | tf_op jit(solution)/shard_map/ppermute | solution.py:49

commit v4 on v3

--- a/solution.py
+++ b/solution.py
@@ -177,7 +177,7 @@
         flags[n] = jnp.full((8, 128), jnp.where(value, 1.0, 0.0), F32)
 
 
-def second_kernel(ib_in, flags, rb, ra, peak, x8, x9, ib, peak_out):
+def second_kernel(ib_in, flags, rb, ra, peak, x8, x9, coef, ib, peak_out):
     d, tree, gi, gj, gk = where_am_i()
     sub, lane = iotas()
     high = gi % 2 == 1
@@ -371,11 +371,9 @@
             self.put(ka, kb, 30 + n, *sides)
 
 
-def coefficient_kernel(neighbours, levels, refine, out, table, ratio):
+def coefficient_kernel(neighbours, levels, refine, out, table):
     d, tree, gi, gj, gk = where_am_i()
     sub, lane = iotas()
-    for n in range(7):
-        ratio[n] = 2.0 / (1.0 + 2.0 ** (n - 3))
 
     def one(pos, carry):
         ip, jp, kp = pos >> 4, (pos >> 2) & 3, pos & 3
@@ -392,46 +390,52 @@
         code = jnp.where(inside, code, 0)
         level = levels[code]
         depth = level + refine[code]
-        for f in range(6):
-            p = neighbours[code * 6 + f]
-            opened = inside & (p >= 0)
-            safe = jnp.maximum(p, 0)
-            other = levels[safe] + refine[safe]
-            table[f * 64 + pos] = jnp.where(opened, 1.0, 0.0)
-            table[(6 + f) * 64 + pos] = jnp.where(opened, ratio[depth - other + 3], 1.0)
-        table[12 * 64 + pos] = jnp.left_shift(1, level).astype(F32)
-        table[13 * 64 + pos] = jnp.left_shift(1, 6 - 2 * depth).astype(F32) * (2.0 / 64.0)
+        for axis in range(3):
+            opened = inside & (neighbours[code * 6 + 2 * axis + 1] >= 0)
+            table[axis * 64 + pos] = jnp.where(opened, 1.0, 0.0)
+        table[3 * 64 + pos] = jnp.left_shift(1, level).astype(F32)
+        table[4 * 64 + pos] = jnp.left_shift(1, 3 - depth).astype(F32)
         return carry
 
     lax.fori_loop(0, 64, one, 0, unroll=4)
-
-    def expand(step, carry):
-        base = step * 64
-
-        def tiles(jp):
+    turns = {0: (0, 1, 2, 3), -1: (3, 0, 1, 3), 1: (1, 2, 2, 0)}
+
+    def spread(item, axis=0, step=0):
+        maps = [turns[step if a == axis else 0] for a in range(3)]
+        made = []
+        for jp in range(4):
             vals = []
             for ip in range(4):
-                n = base + ip * 16 + jp * 4
-                v = [jnp.full((8, 128), table[n + kp], F32) for kp in range(4)]
+                n = item * 64 + maps[0][ip] * 16 + maps[1][jp] * 4
+                v = [jnp.full((8, 128), table[n + maps[2][kp]], F32) for kp in range(4)]
                 vals.append((v[0], v[1], jnp.where(lane % 16 < 8, v[2], v[3])))
-            return [
-                [vals[0][kt], vals[1][kt], jnp.where(sub < 4, vals[2][kt], vals[3][kt])]
-                for kt in range(3)
-            ]
-
-        high, low = tiles(2), tiles(3)
-        sets = (
-            tiles(0),
-            tiles(1),
-            [[jnp.where(lane < 64, high[k][n], low[k][n]) for n in range(3)] for k in range(3)],
-        )
-        for jt in range(3):
-            for kt in range(3):
-                for n in range(3):
-                    out[step, jt, kt, n] = sets[jt][kt][n]
-        return carry
-
-    lax.fori_loop(0, 14, expand, 0)
+            made.append(
+                [
+                    (vals[0][kt], vals[1][kt], jnp.where(sub < 4, vals[2][kt], vals[3][kt]))
+                    for kt in range(3)
+                ]
+            )
+        last = [
+            [jnp.where(lane < 64, made[2][kt][n], made[3][kt][n]) for n in range(3)]
+            for kt in range(3)
+        ]
+        return made[0], made[1], last
+
+    places = [(jt, kt, n) for jt in range(3) for kt in range(3) for n in range(3)]
+    size, inverse = spread(4), spread(3)
+    for jt, kt, n in places:
+        e = size[jt][kt][n]
+        out[12, jt, kt, n] = inverse[jt][kt][n]
+        out[13, jt, kt, n] = e * e * (1.0 / 32.0)
+    for axis in range(3):
+        for side, step in ((0, -1), (1, 1)):
+            opened = spread(axis, axis, -1) if side == 0 else spread(axis)
+            other = spread(4, axis, step)
+            for jt, kt, n in places:
+                e, m = size[jt][kt][n], opened[jt][kt][n]
+                ratio = (2.0 * e) / (e + other[jt][kt][n])
+                out[2 * axis + side, jt, kt, n] = m
+                out[6 + 2 * axis + side, jt, kt, n] = jnp.where(m > 0.5, ratio, 1.0)
 
 
 def coefficient(coef, item, jt, kt):
@@ -660,8 +664,8 @@
     step = jnp.broadcast_to(CFL / top, (8, 128))
     step = jnp.concatenate([step] * 5, axis=0)
 
-    def advance(jq, carry):
-        jt = jq >> 1
+    for jq in range(5):
+        jt = jq // 2
         for kt in range(3):
             kn, kp = (kt + 1) % 3, (kt + 2) % 3
             change = chg_k[jq] if kt == 2 else chg_in[jq, kt]
@@ -677,68 +681,67 @@
             a = jnp.clip(c - step * coefficient(coef, 12, jt, kt) * change, 0.0, 1.0)
             adv[jq, kt] = a
             mob[jq, kt] = 1.0 / (RHO_GAS + (RHO_LIQ - RHO_GAS) * a)
-        return carry
-
-    lax.fori_loop(0, 5, advance, 0)
-
-    def weigh(jq, carry):
-        jt = jq >> 1
-        jn, jp = lax.rem(jq + 1, 5), lax.rem(jq + 4, 5)
-        begins, ends = jq % 2 == 0, (jq % 2 == 1) | (jq == 4)
+
+    k_bot, k_top, j_bot, j_top = k16 < 1, k16 >= 15, lane5 < 16, lane5 >= 112
+    for jq in range(5):
+        jt, jn, jp = jq // 2, (jq + 1) % 5, (jq + 4) % 5
+        edges = (
+            sh.i_bot1, sh.i_top1,
+            j_bot if jq % 2 == 0 else None, j_top if jq in (1, 3, 4) else None,
+            k_bot, k_top,
+        )
         for kt in range(3):
             kn, kp = (kt + 1) % 3, (kt + 2) % 3
-            mi_dn = jnp.where(sh.i_bot1, coefficient(coef, 0, jt, kt), 1.0)
-            mi_up = jnp.where(sh.i_top1, coefficient(coef, 1, jt, kt), 1.0)
-            at_dn = (lane5 < 16) & begins
-            at_up = (lane5 >= 112) & ends
-            mj_dn = jnp.where(at_dn, coefficient(coef, 2, jt, kt), 1.0)
-            mj_up = jnp.where(at_up, coefficient(coef, 3, jt, kt), 1.0)
+            opened = [None if e is None else coefficient(coef, f, jt, kt) for f, e in enumerate(edges)]
+
+            def masked(x, f):
+                return x if edges[f] is None else x * jnp.where(edges[f], opened[f], 1.0)
+
             h = hgt[jq, kt]
-            h_up, h_dn = rs(h, -1) * mi_up, rs(h, 1) * mi_dn
+            h_up, h_dn = masked(rs(h, -1), 1), masked(rs(h, 1), 0)
             gx, sx = 0.5 * (h_up - h_dn), h_up - 2.0 * h + h_dn
-            h_up = sh.j_up(h, hgt[jn, kt], 1) * mj_up
-            h_dn = sh.j_dn(h, hgt[jp, kt], 1) * mj_dn
+            h_up = masked(sh.j_up(h, hgt[jn, kt], 1), 3)
+            h_dn = masked(sh.j_dn(h, hgt[jp, kt], 1), 2)
             gy, sy = 0.5 * (h_up - h_dn), h_up - 2.0 * h + h_dn
             gx2, gy2 = gx * gx, gy * gy
             root = lax.rsqrt(1.0 + gx2 + gy2)
-            bend = (sx * (1.0 + gy2) + sy * (1.0 + gx2)) * coefficient(coef, 12, jt, kt) * (root * root * root)
+            bend = (sx * (1.0 + gy2) + sy * (1.0 + gx2)) * coefficient(coef, 12, jt, kt)
+            bend = bend * (root * root * root)
             right = (src[jq] if kt == 2 else s_in[jq, kt]) - SIGMA * bend * adv[jq, kt]
             m = mob[jq, kt]
-            mk_dn = jnp.where(k16 < 1, coefficient(coef, 4, jt, kt), 1.0)
-            mk_up = jnp.where(k16 >= 15, coefficient(coef, 5, jt, kt), 1.0)
             across = (
                 rs(m, 1), rs(m, -1),
                 sh.j_dn(m, mob[jp, kt], 1), sh.j_up(m, mob[jn, kt], 1),
                 sh.k_dn(m, mob[jq, kp], 1), sh.k_up(m, mob[jq, kn], 1),
             )
-            masks = (mi_dn, mi_up, mj_dn, mj_up, mk_dn, mk_up)
-            edges = (sh.i_bot1, sh.i_top1, at_dn, at_up, k16 < 1, k16 >= 15)
+            closed = jnp.zeros_like(m)
             diag = jnp.zeros_like(m)
             parts = []
             for f in range(6):
-                w = (m + masks[f] * across[f]) * jnp.where(edges[f], coefficient(coef, 6 + f, jt, kt), 1.0)
-                diag = diag + w
-                parts.append(w * masks[f])
-            inv = 1.0 / diag
+                part = m + across[f]
+                if edges[f] is not None:
+                    ratio = coefficient(coef, 6 + f, jt, kt)
+                    part = part * jnp.where(edges[f], ratio * opened[f], 1.0)
+                    closed = closed + jnp.where(edges[f], 1.0 - opened[f], 0.0)
+                diag = diag + part
+                parts.append(part)
+            inv = 1.0 / (diag + closed * m)
             for f in range(6):
                 wts[f, jq, kt] = parts[f] * inv
             rhs[jq, kt] = right * coefficient(coef, 13, jt, kt) * inv
-        return carry
-
-    lax.fori_loop(0, 5, weigh, 0)
 
     for sweep in range(SWEEPS):
         new = p0 if sweep % 2 == 0 else p1
         older = p1 if sweep % 2 == 0 else p0
         last = sweep == SWEEPS - 1
 
-        def old(jq, kt, sweep=sweep, older=older):
+        def old(jq, kt):
             if sweep:
                 return older[jq, kt]
             return p_k[jq] if kt == 2 else p_in[jq, kt]
 
-        def relax(jq, carry, old=old, new=new, last=last):
-            jn, jp = lax.rem(jq + 1, 5), lax.rem(jq + 4, 5)
+        for jq in range(4 if last else 5):
+            jn, jp = (jq + 1) % 5, (jq + 4) % 5
             for kt in range(2 if last else 3):
                 kn, kp = (kt + 1) % 3, (kt + 2) % 3
                 p = old(jq, kt)
@@ -753,9 +756,6 @@
                     out_adv[jq, kt] = adv[jq, kt][:32]
                 else:
                     new[jq, kt] = total
-            return carry
-
-        lax.fori_loop(0, 4 if last else 5, relax, 0)
 
     even = d % 2 == 0
     for h in range(2):
@@ -828,8 +828,19 @@
         (shape(6, 4, 2, 32, 128), blocks(8), blocks(FLAG_COUNT), blocks(32)),
         (old, bounds_old),
     )
+    coef = call(
+        coefficient_kernel,
+        [SM] * 3,
+        shape(14, 3, 3, 3, 8, 128),
+        (neighbours.reshape(-1), levels, refine),
+        [pltpu.SMEM((5 * 64,), F32)],
+        5,
+    )
     ib, peak = call(
-        second_kernel, [VM] * 7, (blocks(32), one), (ib, flags, rb, ra, peak, x8, x9)
+        second_kernel,
+        [VM] * 7 + [pl.BlockSpec(memory_space=pl.ANY)],
+        (blocks(32), one),
+        (ib, flags, rb, ra, peak, x8, x9, coef),
     )
     x64 = send(peak, flip_pairs(64))
     ib = send(ib, axis_pairs(0, 1))
@@ -847,14 +858,6 @@
     )
     x16 = send(peak, flip_pairs(16))
     ja, jb = send(ja, axis_pairs(1, 0)), send(jb, axis_pairs(1, 1))
-    coef = call(
-        coefficient_kernel,
-        [SM] * 3,
-        shape(14, 3, 3, 3, 8, 128),
-        (neighbours.reshape(-1), levels, refine),
-        [pltpu.SMEM((14 * 64,), F32), pltpu.SMEM((7,), F32)],
-        5,
-    )
     inner = call(
         inner_kernel,
         [VM] * 4,

time: 64.4 us -> 62.7 us (0.974)
  Pallas kernels: 15.8 us -> 12.2 us
  waiting for transfers between devices: 14.3 us -> 16.8 us
    pallas_call x10, Pallas kernels: 15.8 us -> 12.2 us  [call(): pl.pallas_call(kernel, out_shape=outs, in_specs=specs, out_specs=jax.tree...]
    ppermute x14, waiting for transfers between devices: 14.3 us -> 16.8 us  [send(): return lax.ppermute(x, AXES, pairs)]
  transfers between devices with their start and end apart: 14 -> 14, of which waited for: 6 -> 7; matrix products, arithmetic and copies ran while one was open for 2% -> 2% of each run, Pallas kernels for 11% -> 9%
where the time goes in v4:
time: 62.7 us; the launch traced here: 62.5 us
  starting transfers between devices  27.3 us (44%)
  waiting for transfers between devices  16.8 us (27%)
  Pallas kernels  12.2 us (19%)
  between operations  2.8 us (4%)
  other arithmetic  2.18 us (3%)
  local copies, waits for them, and re-layouts  1.18 us (2%)
    ppermute x14, starting transfers between devices, send(): return lax.ppermute(x, AXES, pairs)  27.3 us
    ppermute x14, waiting for transfers between devices, send(): return lax.ppermute(x, AXES, pairs)  16.8 us
    pallas_call x10, Pallas kernels, call(): pl.pallas_call(kernel, out_shape=outs, in_specs=specs, out_specs=jax.tree...  12.2 us
    concatenate x1, other arithmetic, local(): jnp.concatenate([volume[None], velocity, source[None], pressure_prev[None...  1.34 us
  transfers between devices with their start and end apart: 14, of which 7 were waited for; matrix products, arithmetic and copies ran while one was open for 2% of the time, Pallas kernels for 9%

profile of v4, /device:TPU:1, one launch (start us, length us, event | category | flops | bytes accessed | tf_op | source)
XLA Modules:
  0.0 62.5 jit_solution(4855922486062932389)
XLA Ops:
  0.7 1.3 %pad_maximum_fusion.old = f32[6,10,16,256]{3,2,1,0:T(8,128)S(1)} fusion(f32[1,10,16,256]{3,2,1,0:T(8,128)} %bitcast.13, f32[1,10,16,256]{3,2,1,0:T(8,128)} %bitcast.14, f32[3,10,16,256]{3,2,1,0:T(8,128)} %param.10, f32[1,10,16,256]{3,2,1,0:T(8,128)} %bitcast.15), kind=kLoop, calls=%fused_computation | loop fusion | flops 737280 | bytes 1966080 | tf_op jit(solution)/shard_map/concatenate | solution.py:819
  2.0 0.7 %shard_map.105 = (f32[57,8,128]{2,1,0:T(8,128)S(1)}, f32[24,8,128]{2,1,0:T(8,128)S(1)}, f32[1,8,128]{2,1,0:T(8,128)S(1)}) custom-call(f32[6,10,16,256]{3,2,1,0:T(8,128)S(1)} %pad_maximum_fusion.old, s32[1024]{0:T(1024)S(1)} %copy-done, s32[129]{0:T(256)S(1)} %copy-done.2), custom_call_target="tpu_custom_call" | custom-call | flops 100000 | bytes 100000 | tf_op jit(solution)/shard_map/pallas_call | solution.py:803
  2.7 2.1 %collective-permute-start = (f32[57,8,128]{2,1,0:T(8,128)S(1)}, f32[57,8,128]{2,1,0:T(8,128)S(1)}, u32[]{:S(2)}, u32[]{:S(2)}) collective-permute-start(f32[57,8,128]{2,1,0:T(8,128)S(1)} %get-tuple-element.41), channel_id=1, source_target_pairs={{0,1},{1,0},{2,3},{3,2},{4,5},{5,4},{6,7},{7,6},{8,9},{9,8},{10,11... | collective-permute-start | bytes 700424 | tf_op jit(solution)/shard_map/ppermute | solution.py:49
  4.9 7.0 %collective-permute-start.1 = (f32[24,8,128]{2,1,0:T(8,128)S(1)}, f32[24,8,128]{2,1,0:T(8,128)S(1)}, u32[]{:S(2)}, u32[]{:S(2)}) collective-permute-start(f32[24,8,128]{2,1,0:T(8,128)S(1)} %get-tuple-element.42), channel_id=1, source_target_pairs={{1,2},{2,1},{3,4},{4,3},{5,6},{6,5},{7,8},{8,7},{9,10},{10,9},{11,... | collective-permute-start | bytes 294920 | tf_op jit(solution)/shard_map/ppermute | solution.py:49
  12.1 0.7 %shard_map.104 = (f32[6,4,2,32,128]{4,3,2,1,0:T(8,128)S(1)}, f32[8,8,128]{2,1,0:T(8,128)S(1)}, f32[6,8,128]{2,1,0:T(8,128)S(1)}, f32[32,8,128]{2,1,0:T(8,128)S(1)}) custom-call(f32[6,10,16,256]{3,2,1,0:T(8,128)S(1)} %pad_maximum_fusion.old, s32[129]{0:T(256)S(1)} %copy-done.2), custom_call_target="tpu_custom_call" | custom-call | flops 100000 | bytes 100000 | tf_op jit(solution)/shard_map/pallas_call | solution.py:803
  13.3 3.2 %shard_map.107.coef = f32[14,3,3,3,8,128]{5,4,3,2,1,0:T(8,128)S(1)} custom-call(s32[6144]{0:T(1024)S(1)} %reshape.17.neighbours, s32[1024]{0:T(1024)S(1)} %copy-done, s32[1024]{0:T(1024)S(1)} %copy-done.1), custom_call_target="tpu_custom_call" | custom-call | flops 500000 | bytes 500000 | tf_op jit(solution)/shard_map/pallas_call | solution.py:803
  16.9 3.7 %collective-permute-start.4 = (f32[32,8,128]{2,1,0:T(8,128)S(1)}, f32[32,8,128]{2,1,0:T(8,128)S(1)}, u32[]{:S(2)}, u32[]{:S(2)}) collective-permute-start(f32[32,8,128]{2,1,0:T(8,128)S(1)} %get-tuple-element.47), channel_id=1, source_target_pairs={{0,64},{1,8},{2,66},{3,10},{4,68},{5,12},{6,70},{7,14},{8,1},{9,73... | collective-permute-start | bytes 393224 | tf_op jit(solution)/shard_map/ppermute | solution.py:49
  20.8 4.1 %collective-permute-done.5.x64 = f32[1,8,128]{2,1,0:T(8,128)S(1)} collective-permute-done((f32[1,8,128]{2,1,0:T(8,128)S(1)}, f32[1,8,128]{2,1,0:T(8,128)S(1)}, u32[]{:S(2)}, u32[]{:S(2)}) %collective-permute-start.5) | collective-permute-done | bytes 4128 | tf_op jit(solution)/shard_map/ppermute | solution.py:49
  25.0 2.1 %collective-permute-start.6 = (f32[38,8,128]{2,1,0:T(8,128)S(1)}, f32[38,8,128]{2,1,0:T(8,128)S(1)}, u32[]{:S(2)}, u32[]{:S(2)}) collective-permute-start(f32[38,8,128]{2,1,0:T(8,128)S(1)} %get-tuple-element.49), channel_id=1, source_target_pairs={{0,2},{1,3},{2,0},{3,1},{4,6},{5,7},{6,4},{7,5},{8,10},{9,11},{10,... | collective-permute-start | bytes 466952 | tf_op jit(solution)/shard_map/ppermute | solution.py:49
  27.1 4.3 %collective-permute-start.7 = (f32[38,8,128]{2,1,0:T(8,128)S(1)}, f32[38,8,128]{2,1,0:T(8,128)S(1)}, u32[]{:S(2)}, u32[]{:S(2)}) collective-permute-start(f32[38,8,128]{2,1,0:T(8,128)S(1)} %get-tuple-element.50), channel_id=1, source_target_pairs={{0,18},{1,19},{2,16},{3,17},{4,22},{5,23},{6,20},{7,21},{8,26},{9,... | collective-permute-start | bytes 466952 | tf_op jit(solution)/shard_map/ppermute | solution.py:49
  31.5 0.7 %shard_map.110 = (f32[4,2,40,128]{3,2,1,0:T(8,128)S(1)}, f32[4,2,40,128]{3,2,1,0:T(8,128)S(1)}, f32[4,2,40,128]{3,2,1,0:T(8,128)S(1)}, f32[4,2,40,128]{3,2,1,0:T...) custom-call(f32[6,4,2,32,128]{4,3,2,1,0:T(8,128)S(1)} %get-tuple-ele, ...), custom_call_target="tpu_custom_call" | custom-call | flops 200000 | bytes 200000 | tf_op jit(solution)/shard_map/pallas_call | solution.py:803
  32.6 5.2 %collective-permute-done.7.jb = f32[38,8,128]{2,1,0:T(8,128)S(1)} collective-permute-done((f32[38,8,128]{2,1,0:T(8,128)S(1)}, f32[38,8,128]{2,1,0:T(8,128)S(1)}, u32[]{:S(2)}, u32[]{:S(2)}) %collective-permute-start.7) | collective-permute-done | bytes 155680 | tf_op jit(solution)/shard_map/ppermute | solution.py:49
  37.8 1.4 %shard_map.111 = (f32[5,2,40,128]{3,2,1,0:T(8,128)S(1)}, f32[5,2,40,128]{3,2,1,0:T(8,128)S(1)}, f32[5,2,40,128]{3,2,1,0:T(8,128)S(1)}, f32[5,2,40,128]{3,2,1,0:T...) custom-call(f32[38,8,128]{2,1,0:T(8,128)S(1)} %collective-permute-do, ...), custom_call_target="tpu_custom_call" | custom-call | flops 100000 | bytes 100000 | tf_op jit(solution)/shard_map/pallas_call | solution.py:803
  39.2 1.0 %collective-permute-start.10 = (f32[39,8,128]{2,1,0:T(8,128)S(1)}, f32[39,8,128]{2,1,0:T(8,128)S(1)}, u32[]{:S(2)}, u32[]{:S(2)}) collective-permute-start(f32[39,8,128]{2,1,0:T(8,128)S(1)} %get-tuple-element.66), channel_id=1, source_target_pairs={{0,36},{1,37},{2,38},{3,39},{4,32},{5,33},{6,34},{7,35},{8,44},{9,... | collective-permute-start | bytes 479240 | tf_op jit(solution)/shard_map/ppermute | solution.py:49
  40.1 1.0 %collective-permute-start.9 = (f32[39,8,128]{2,1,0:T(8,128)S(1)}, f32[39,8,128]{2,1,0:T(8,128)S(1)}, u32[]{:S(2)}, u32[]{:S(2)}) collective-permute-start(f32[39,8,128]{2,1,0:T(8,128)S(1)} %get-tuple-element.65), channel_id=1, source_target_pairs={{0,4},{1,5},{2,6},{3,7},{4,0},{5,1},{6,2},{7,3},{8,12},{9,13},{10,... | collective-permute-start | bytes 479240 | tf_op jit(solution)/shard_map/ppermute | solution.py:49
  41.2 0.7 %collective-permute-start.11 = (f32[1,8,128]{2,1,0:T(8,128)S(1)}, f32[1,8,128]{2,1,0:T(8,128)S(1)}, u32[]{:S(2)}, u32[]{:S(2)}) collective-permute-start(f32[1,8,128]{2,1,0:T(8,128)S(1)} %get-tuple-element.67.peak), channel_id=1, source_target_pairs={{0,32},{1,33},{2,34},{3,35},{4,36},{5,37},{6,38},{7,39},{8,40},{9,... | collective-permute-start | bytes 12296 | tf_op jit(solution)/shard_map/ppermute | solution.py:49
  41.9 0.6 fusion
  44.4 1.0 %collective-permute-done.10.kb = f32[39,8,128]{2,1,0:T(8,128)S(1)} collective-permute-done((f32[39,8,128]{2,1,0:T(8,128)S(1)}, f32[39,8,128]{2,1,0:T(8,128)S(1)}, u32[]{:S(2)}, u32[]{:S(2)}) %collective-permute-start.10) | collective-permute-done | bytes 159776 | tf_op jit(solution)/shard_map/ppermute | solution.py:49
  45.4 3.0 %collective-permute-done.9.ka = f32[39,8,128]{2,1,0:T(8,128)S(1)} collective-permute-done((f32[39,8,128]{2,1,0:T(8,128)S(1)}, f32[39,8,128]{2,1,0:T(8,128)S(1)}, u32[]{:S(2)}, u32[]{:S(2)}) %collective-permute-start.9) | collective-permute-done | bytes 159776 | tf_op jit(solution)/shard_map/ppermute | solution.py:49
  48.4 4.6 %shard_map.112 = (f32[4,2,32,128]{3,2,1,0:T(8,128)S(1)}, f32[4,2,32,128]{3,2,1,0:T(8,128)S(1)}, f32[2,16,256]{2,1,0:T(8,128)S(1)}, f32[2,16,256]{2,1,0:T(8,128)S(1)}) custom-call(f32[5,2,40,128]{3,2,1,0:T(8,128)S(1)} %get-tuple-element.60.c_in, f32[5,2,40,128]{3,2,1,0:T(8,128)S(1)} %get-tuple-element.61.u_in, f32[5,2,40,128]{3,2,1,0:T(8,128)S(1)} %get-tuple-element.62.s_in, ...), custom_call_target="tpu_custom_call" | custom-call | flops 800000 | bytes 800000 | tf_op jit(solution)/shard_map/pallas_call | solution.py:803
  53.1 4.9 %collective-permute-start.12 = (f32[2,16,256]{2,1,0:T(8,128)S(1)}, f32[2,16,256]{2,1,0:T(8,128)S(1)}, u32[]{:S(2)}, u32[]{:S(2)}) collective-permute-start(f32[2,16,256]{2,1,0:T(8,128)S(1)} %get-tuple-element.68), channel_id=1, source_target_pairs={{1,2},{2,1},{3,4},{4,3},{5,6},{6,5},{7,8},{8,7},{9,10},{10,9},{11,... | collective-permute-start | bytes 98312 | tf_op jit(solution)/shard_map/ppermute | solution.py:49
  58.2 0.6 shard_map.113
  58.8 2.8 %collective-permute-done.12 = f32[2,16,256]{2,1,0:T(8,128)S(1)} collective-permute-done((f32[2,16,256]{2,1,0:T(8,128)S(1)}, f32[2,16,256]{2,1,0:T(8,128)S(1)}, u32[]{:S(2)}, u32[]{:S(2)}) %collective-permute-start.12) | collective-permute-done | bytes 32800 | tf_op jit(solution)/shard_map/ppermute | solution.py:49
  61.6 0.8 %select_select_fusion = (f32[10,16,256]{2,1,0:T(8,128)}, f32[10,16,256]{2,1,0:T(8,128)}) fusion(f32[10,16,256]{2,1,0:T(8,128)S(1)} %get-tuple-element.73, f32[16,256]{1,0:T(8,128)S(1)} %get-tuple-element.78, f32[16,256]{1,0:T(8,128)S(1)} %get-tuple-element.85, pred[10]{0:T(512)(128)(4,1)S(1)} %get-tuple-element.86, pred[10]{0:T(512)(128)(4,1)S(1)} %get-tuple-element.87, ...), kind=kLoop, calls=%fused_computation.1 | loop fusion | flops 163840 | bytes 720916 | tf_op jit(solution)/shard_map/jit(_where)/select_n | solution.py:900
  (32 shorter events, 2.1 us)
Async XLA Ops:
  0.6 1.4 %copy-start.2 = (s32[129]{0:T(256)S(1)}, s32[129]{0:T(256)}, u32[]{:S(2)}) copy-start(s32[129]{0:T(256)} %bounds.4) | copy-start | bytes 1552
  0.6 1.4 %copy-start = (s32[1024]{0:T(1024)S(1)}, s32[1024]{0:T(1024)}, u32[]{:S(2)}) copy-start(s32[1024]{0:T(1024)} %levels.3) | copy-start | bytes 12292
  0.7 12.1 %copy-start.4 = (s32[1024,6]{0,1:T(8,128)S(1)}, s32[1024,6]{0,1:T(8,128)}, u32[]{:S(2)}) copy-start(s32[1024,6]{0,1:T(8,128)} %param.13) | copy-start | bytes 73732
  2.0 11.3 %copy-start.1 = (s32[1024]{0:T(1024)S(1)}, s32[1024]{0:T(1024)}, u32[]{:S(2)}) copy-start(s32[1024]{0:T(1024)} %refine.1) | copy-start | bytes 12292
  2.7 14.2 %collective-permute-start = (f32[57,8,128]{2,1,0:T(8,128)S(1)}, f32[57,8,128]{2,1,0:T(8,128)S(1)}, u32[]{:S(2)}, u32[]{:S(2)}) collective-permute-start(f32[57,8,128]{2,1,0:T(8,128)S(1)} %get-tuple-element.41), channel_id=1, source_target_pairs={{0,1},{1,0},{2,3},{3,2},{4,5},{5,4},{6,7},{7,6},{8,9},{9,8},{10,11... | collective-permute-start | bytes 700424 | tf_op jit(solution)/shard_map/ppermute | solution.py:49
  4.9 12.0 %collective-permute-start.1 = (f32[24,8,128]{2,1,0:T(8,128)S(1)}, f32[24,8,128]{2,1,0:T(8,128)S(1)}, u32[]{:S(2)}, u32[]{:S(2)}) collective-permute-start(f32[24,8,128]{2,1,0:T(8,128)S(1)} %get-tuple-element.42), channel_id=1, source_target_pairs={{1,2},{2,1},{3,4},{4,3},{5,6},{6,5},{7,8},{8,7},{9,10},{10,9},{11,... | collective-permute-start | bytes 294920 | tf_op jit(solution)/shard_map/ppermute | solution.py:49
  11.9 4.7 %collective-permute-start.2 = (f32[1,8,128]{2,1,0:T(8,128)S(1)}, f32[1,8,128]{2,1,0:T(8,128)S(1)}, u32[]{:S(2)}, u32[]{:S(2)}) collective-permute-start(f32[1,8,128]{2,1,0:T(8,128)S(1)} %get-tuple-element.46.peak), channel_id=1, source_target_pairs={{0,8},{1,9},{2,10},{3,11},{4,12},{5,13},{6,14},{7,15},{8,0},{9,1},... | collective-permute-start | bytes 12296 | tf_op jit(solution)/shard_map/ppermute | solution.py:49
  12.0 4.9 %collective-permute-start.3 = (f32[1,8,128]{2,1,0:T(8,128)S(1)}, f32[1,8,128]{2,1,0:T(8,128)S(1)}, u32[]{:S(2)}, u32[]{:S(2)}) collective-permute-start(f32[1,8,128]{2,1,0:T(8,128)S(1)} %get-tuple-element.46.peak), channel_id=1, source_target_pairs={{0,9},{1,8},{2,11},{3,10},{4,13},{5,12},{6,15},{7,14},{8,1},{9,0},... | collective-permute-start | bytes 12296 | tf_op jit(solution)/shard_map/ppermute | solution.py:49
  16.9 7.9 %collective-permute-start.4 = (f32[32,8,128]{2,1,0:T(8,128)S(1)}, f32[32,8,128]{2,1,0:T(8,128)S(1)}, u32[]{:S(2)}, u32[]{:S(2)}) collective-permute-start(f32[32,8,128]{2,1,0:T(8,128)S(1)} %get-tuple-element.47), channel_id=1, source_target_pairs={{0,64},{1,8},{2,66},{3,10},{4,68},{5,12},{6,70},{7,14},{8,1},{9,73... | collective-permute-start | bytes 393224 | tf_op jit(solution)/shard_map/ppermute | solution.py:49
  20.6 4.3 %collective-permute-start.5 = (f32[1,8,128]{2,1,0:T(8,128)S(1)}, f32[1,8,128]{2,1,0:T(8,128)S(1)}, u32[]{:S(2)}, u32[]{:S(2)}) collective-permute-start(f32[1,8,128]{2,1,0:T(8,128)S(1)} %get-tuple-element.48.peak), channel_id=1, source_target_pairs={{0,64},{1,65},{2,66},{3,67},{4,68},{5,69},{6,70},{7,71},{8,72},{9,... | collective-permute-start | bytes 12296 | tf_op jit(solution)/shard_map/ppermute | solution.py:49
  25.0 7.6 %collective-permute-start.6 = (f32[38,8,128]{2,1,0:T(8,128)S(1)}, f32[38,8,128]{2,1,0:T(8,128)S(1)}, u32[]{:S(2)}, u32[]{:S(2)}) collective-permute-start(f32[38,8,128]{2,1,0:T(8,128)S(1)} %get-tuple-element.49), channel_id=1, source_target_pairs={{0,2},{1,3},{2,0},{3,1},{4,6},{5,7},{6,4},{7,5},{8,10},{9,11},{10,... | collective-permute-start | bytes 466952 | tf_op jit(solution)/shard_map/ppermute | solution.py:49
  27.1 10.7 %collective-permute-start.7 = (f32[38,8,128]{2,1,0:T(8,128)S(1)}, f32[38,8,128]{2,1,0:T(8,128)S(1)}, u32[]{:S(2)}, u32[]{:S(2)}) collective-permute-start(f32[38,8,128]{2,1,0:T(8,128)S(1)} %get-tuple-element.50), channel_id=1, source_target_pairs={{0,18},{1,19},{2,16},{3,17},{4,22},{5,23},{6,20},{7,21},{8,26},{9,... | collective-permute-start | bytes 466952 | tf_op jit(solution)/shard_map/ppermute | solution.py:49
  31.4 1.2 %collective-permute-start.8 = (f32[1,8,128]{2,1,0:T(8,128)S(1)}, f32[1,8,128]{2,1,0:T(8,128)S(1)}, u32[]{:S(2)}, u32[]{:S(2)}) collective-permute-start(f32[1,8,128]{2,1,0:T(8,128)S(1)} %get-tuple-element.51.peak), channel_id=1, source_target_pairs={{0,16},{1,17},{2,18},{3,19},{4,20},{5,21},{6,22},{7,23},{8,24},{9,... | collective-permute-start | bytes 12296 | tf_op jit(solution)/shard_map/ppermute | solution.py:49
  32.2 9.7 %copy-start.3 = (s32[129]{0:T(256)S(1)}, s32[129]{0:T(256)}, u32[]{:S(2)}) copy-start(s32[129]{0:T(256)} %bounds.5) | copy-start | bytes 1552
  39.2 6.3 %collective-permute-start.10 = (f32[39,8,128]{2,1,0:T(8,128)S(1)}, f32[39,8,128]{2,1,0:T(8,128)S(1)}, u32[]{:S(2)}, u32[]{:S(2)}) collective-permute-start(f32[39,8,128]{2,1,0:T(8,128)S(1)} %get-tuple-element.66), channel_id=1, source_target_pairs={{0,36},{1,37},{2,38},{3,39},{4,32},{5,33},{6,34},{7,35},{8,44},{9,... | collective-permute-start | bytes 479240 | tf_op jit(solution)/shard_map/ppermute | solution.py:49
  40.1 8.3 %collective-permute-start.9 = (f32[39,8,128]{2,1,0:T(8,128)S(1)}, f32[39,8,128]{2,1,0:T(8,128)S(1)}, u32[]{:S(2)}, u32[]{:S(2)}) collective-permute-start(f32[39,8,128]{2,1,0:T(8,128)S(1)} %get-tuple-element.65), channel_id=1, source_target_pairs={{0,4},{1,5},{2,6},{3,7},{4,0},{5,1},{6,2},{7,3},{8,12},{9,13},{10,... | collective-permute-start | bytes 479240 | tf_op jit(solution)/shard_map/ppermute | solution.py:49
  41.2 3.3 %collective-permute-start.11 = (f32[1,8,128]{2,1,0:T(8,128)S(1)}, f32[1,8,128]{2,1,0:T(8,128)S(1)}, u32[]{:S(2)}, u32[]{:S(2)}) collective-permute-start(f32[1,8,128]{2,1,0:T(8,128)S(1)} %get-tuple-element.67.peak), channel_id=1, source_target_pairs={{0,32},{1,33},{2,34},{3,35},{4,36},{5,37},{6,38},{7,39},{8,40},{9,... | collective-permute-start | bytes 12296 | tf_op jit(solution)/shard_map/ppermute | solution.py:49
  53.1 8.6 %collective-permute-start.12 = (f32[2,16,256]{2,1,0:T(8,128)S(1)}, f32[2,16,256]{2,1,0:T(8,128)S(1)}, u32[]{:S(2)}, u32[]{:S(2)}) collective-permute-start(f32[2,16,256]{2,1,0:T(8,128)S(1)} %get-tuple-element.68), channel_id=1, source_target_pairs={{1,2},{2,1},{3,4},{4,3},{5,6},{6,5},{7,8},{8,7},{9,10},{10,9},{11,... | collective-permute-start | bytes 98312 | tf_op jit(solution)/shard_map/ppermute | solution.py:49
  58.0 3.6 %collective-permute-start.13 = (f32[2,16,256]{2,1,0:T(8,128)S(1)}, f32[2,16,256]{2,1,0:T(8,128)S(1)}, u32[]{:S(2)}, u32[]{:S(2)}) collective-permute-start(f32[2,16,256]{2,1,0:T(8,128)S(1)} %get-tuple-element.69), channel_id=1, source_target_pairs={{0,1},{1,0},{2,3},{3,2},{4,5},{5,4},{6,7},{7,6},{8,9},{9,8},{10,11... | collective-permute-start | bytes 98312 | tf_op jit(solution)/shard_map/ppermute | solution.py:49

commit v5 on v4

--- a/solution.py
+++ b/solution.py
@@ -32,8 +32,9 @@
     for d in range(DEVS):
         c = list(block_coords(d))
         step = 1 if (c[axis] % 2 == 0) != bool(odd) else -1
-        c[axis] = (c[axis] + step) % count
-        pairs.append((d, PLACE[tuple(c)]))
+        c[axis] += step
+        if 0 <= c[axis] < count:
+            pairs.append((d, PLACE[tuple(c)]))
     return pairs
 
 
@@ -177,7 +178,7 @@
         flags[n] = jnp.full((8, 128), jnp.where(value, 1.0, 0.0), F32)
 
 
-def second_kernel(ib_in, flags, rb, ra, peak, x8, x9, coef, ib, peak_out):
+def second_kernel(ib_in, flags, rb, peak, x8, coef, ib, peak_out):
     d, tree, gi, gj, gk = where_am_i()
     sub, lane = iotas()
     high = gi % 2 == 1
@@ -190,7 +191,7 @@
             for g in range(4):
                 n = (g * 4 + q) * 2 + h
                 ib[n] = jnp.where(flag, groups[g], ib_in[n]) if q in (0, 3) else ib_in[n]
-    peak_out[0] = jnp.maximum(jnp.maximum(peak[0], ra[56]), jnp.maximum(x8[0], x9[0]))
+    peak_out[0] = jnp.maximum(peak[0], x8[0])
 
 
 def block_kernel(own, mine, flags, ra, rb, ext, ia):
@@ -290,7 +291,6 @@
         put(5, 0, b, both)
     top = jnp.maximum(peak[0], x64[0])
     ja[J_BLOCKS] = top
-    jb[J_BLOCKS] = top
     peak_out[0] = top
 
 
@@ -553,7 +553,7 @@
 
 
 def outer_kernel(
-    ja, jb, peak, x16, coef, c_in, u2_in, src_in, prs_in, u1_in, chg_in, ka_in, kb_in,
+    ja, jb, peak, x16, x18, coef, c_in, u2_in, src_in, prs_in, u1_in, chg_in, ka_in, kb_in,
     c40, u2, src, prs, chg, ka, kb, peak_out,
 ):
     d, tree, gi, gj, gk = where_am_i()
@@ -606,15 +606,14 @@
     pack.block((3,), lambda kind, jq, kt, b: kinds[kind][jq, kt, pl.ds(8 * b, 8), :], ka, kb)
     pack.halo(lambda kind, kt, b: kinds[kind][4, kt, pl.ds(8 * b, 8), :], ka, kb)
     top = jnp.maximum(
-        jnp.maximum(peak[0], x16[0]), jnp.maximum(ja[J_BLOCKS], jb[J_BLOCKS])
+        jnp.maximum(peak[0], ja[J_BLOCKS]), jnp.maximum(x16[0], x18[0])
     )
     ka[K_BLOCKS] = top
-    kb[K_BLOCKS] = top
     peak_out[0] = top
 
 
 def main_kernel(
-    c_in, u_in, s_in, p_in, chg_in, ka, kb, peak, x32, coef,
+    c_in, u_in, s_in, p_in, chg_in, ka, kb, peak, x32, x36, coef,
     out_adv, out_p, send_a, send_b,
     c_k, u2, src, p_k, chg_k, p0, p1, adv, mob, hgt, rhs, wts,
 ):
@@ -658,7 +657,7 @@
         return u2[jq] if kt == 2 else u_in[jq, kt]
 
     top = jnp.maximum(
-        jnp.maximum(peak[0], x32[0]), jnp.maximum(ka[K_BLOCKS], kb[K_BLOCKS])
+        jnp.maximum(peak[0], ka[K_BLOCKS]), jnp.maximum(x32[0], x36[0])
     )
     top = jnp.max(top, keepdims=True)
     step = jnp.broadcast_to(CFL / top, (8, 128))
@@ -820,8 +819,9 @@
     ra, rb, peak = call(
         first_kernel, [VM, SM, SM], (blocks(57), blocks(24), one), (old, levels, bounds_old)
     )
-    x8, x9 = send(peak, flip_pairs(8)), send(peak, flip_pairs(9))
     rb, ra = send(rb, ODD_PAIRS), send(ra, EVEN_PAIRS)
+    peak = jnp.maximum(peak, ra[56:57])
+    x8 = send(peak, flip_pairs(8))
     own, mine, flags, ib = call(
         own_kernel,
         [VM, SM],
@@ -838,9 +838,9 @@
     )
     ib, peak = call(
         second_kernel,
-        [VM] * 7 + [pl.BlockSpec(memory_space=pl.ANY)],
+        [VM] * 5 + [pl.BlockSpec(memory_space=pl.ANY)],
         (blocks(32), one),
-        (ib, flags, rb, ra, peak, x8, x9, coef),
+        (ib, flags, rb, peak, x8, coef),
     )
     x64 = send(peak, flip_pairs(64))
     ib = send(ib, axis_pairs(0, 1))
@@ -853,10 +853,10 @@
     ja, jb, peak = call(
         third_kernel,
         [VM] * 5,
-        (blocks(J_BLOCKS + 1), blocks(J_BLOCKS + 1), one),
+        (blocks(J_BLOCKS + 1), blocks(J_BLOCKS), one),
         (ext, ia, ib, peak, x64),
     )
-    x16 = send(peak, flip_pairs(16))
+    x16, x18 = send(peak, flip_pairs(16)), send(peak, flip_pairs(18))
     ja, jb = send(ja, axis_pairs(1, 0)), send(jb, axis_pairs(1, 1))
     inner = call(
         inner_kernel,
@@ -868,20 +868,20 @@
     )
     *early, ka, kb, peak = call(
         outer_kernel,
-        [VM] * 13,
-        (shape(5, 2, 40, 128),) * 5 + (blocks(K_BLOCKS + 1),) * 2 + (one,),
-        (ja, jb, peak, x16, coef, *inner),
+        [VM] * 14,
+        (shape(5, 2, 40, 128),) * 5 + (blocks(K_BLOCKS + 1), blocks(K_BLOCKS), one),
+        (ja, jb, peak, x16, x18, coef, *inner),
         (),
         1,
     )
-    x32 = send(peak, flip_pairs(32))
+    x32, x36 = send(peak, flip_pairs(32)), send(peak, flip_pairs(36))
     ka, kb = send(ka, axis_pairs(2, 0)), send(kb, axis_pairs(2, 1))
     halo, grid = (5, 40, 128), (5, 3, 40, 128)
     adv, prs, sa, sb = call(
         main_kernel,
-        [VM] * 10,
+        [VM] * 11,
         (shape(4, 2, 32, 128),) * 2 + (shape(2, 16, 256),) * 2,
-        (*early, ka, kb, peak, x32, coef),
+        (*early, ka, kb, peak, x32, x36, coef),
         [pltpu.VMEM(halo, F32)] * 5
         + [pltpu.VMEM(grid, F32)] * 6
         + [pltpu.VMEM((6, *grid), F32)],

time: 62.7 us -> 64.2 us (1.024)
  starting transfers between devices: 27.3 us -> 38.9 us
  waiting for transfers between devices: 16.8 us -> 6.67 us
    ppermute x14 -> x15, starting transfers between devices: 27.3 us -> 38.9 us  [send(): return lax.ppermute(x, AXES, pairs)]
    ppermute x14 -> x15, waiting for transfers between devices: 16.8 us -> 6.67 us  [send(): return lax.ppermute(x, AXES, pairs)]
  transfers between devices with their start and end apart: 14 -> 15, of which waited for: 7 -> 5; matrix products, arithmetic and copies ran while one was open for 2% -> 2% of each run, Pallas kernels for 9% -> 8%
where the time goes in v5:
time: 64.2 us; the launch traced here: 64 us
  starting transfers between devices  38.9 us (61%)
  Pallas kernels  12.2 us (19%)
  waiting for transfers between devices  6.67 us (10%)
  between operations  2.89 us (5%)
  other arithmetic  2.19 us (3%)
  local copies, waits for them, and re-layouts  1.18 us (2%)
    ppermute x15, starting transfers between devices, send(): return lax.ppermute(x, AXES, pairs)  38.9 us
    pallas_call x10, Pallas kernels, call(): pl.pallas_call(kernel, out_shape=outs, in_specs=specs, out_specs=jax.tree...  12.2 us
    ppermute x15, waiting for transfers between devices, send(): return lax.ppermute(x, AXES, pairs)  6.67 us
    concatenate x1, other arithmetic, local(): jnp.concatenate([volume[None], velocity, source[None], pressure_prev[None...  1.34 us
  transfers between devices with their start and end apart: 15, of which 5 were waited for; matrix products, arithmetic and copies ran while one was open for 2% of the time, Pallas kernels for 8%

profile of v5, /device:TPU:1, one launch (start us, length us, event | category | flops | bytes accessed | tf_op | source)
XLA Modules:
  0.0 64.0 jit_solution(11830029927128626769)
XLA Ops:
  0.7 1.3 %pad_maximum_fusion.old = f32[6,10,16,256]{3,2,1,0:T(8,128)S(1)} fusion(f32[1,10,16,256]{3,2,1,0:T(8,128)} %bitcast.13, f32[1,10,16,256]{3,2,1,0:T(8,128)} %bitcast.14, f32[3,10,16,256]{3,2,1,0:T(8,128)} %param.10, f32[1,10,16,256]{3,2,1,0:T(8,128)} %bitcast.15), kind=kLoop, calls=%fused_computation | loop fusion | flops 737280 | bytes 1966080 | tf_op jit(solution)/shard_map/concatenate | solution.py:818
  2.0 0.7 %shard_map.105 = (f32[57,8,128]{2,1,0:T(8,128)S(1)}, f32[24,8,128]{2,1,0:T(8,128)S(1)}, f32[1,8,128]{2,1,0:T(8,128)S(1)}) custom-call(f32[6,10,16,256]{3,2,1,0:T(8,128)S(1)} %pad_maximum_fusion.old, s32[1024]{0:T(1024)S(1)} %copy-done, s32[129]{0:T(256)S(1)} %copy-done.2), custom_call_target="tpu_custom_call" | custom-call | flops 100000 | bytes 100000 | tf_op jit(solution)/shard_map/pallas_call | solution.py:802
  2.7 2.1 %collective-permute-start = (f32[57,8,128]{2,1,0:T(8,128)S(1)}, f32[57,8,128]{2,1,0:T(8,128)S(1)}, u32[]{:S(2)}, u32[]{:S(2)}) collective-permute-start(f32[57,8,128]{2,1,0:T(8,128)S(1)} %get-tuple-element.41), channel_id=1, source_target_pairs={{0,1},{1,0},{2,3},{3,2},{4,5},{5,4},{6,7},{7,6},{8,9},{9,8},{10,11... | collective-permute-start | bytes 700424 | tf_op jit(solution)/shard_map/ppermute | solution.py:50
  4.9 7.0 %collective-permute-start.1 = (f32[24,8,128]{2,1,0:T(8,128)S(1)}, f32[24,8,128]{2,1,0:T(8,128)S(1)}, u32[]{:S(2)}, u32[]{:S(2)}) collective-permute-start(f32[24,8,128]{2,1,0:T(8,128)S(1)} %get-tuple-element.42), channel_id=1, source_target_pairs={{1,2},{2,1},{3,4},{4,3},{5,6},{6,5},{7,8},{8,7},{9,10},{10,9},{11,... | collective-permute-start | bytes 294920 | tf_op jit(solution)/shard_map/ppermute | solution.py:50
  11.9 1.2 %collective-permute-start.2 = (f32[1,8,128]{2,1,0:T(8,128)S(1)}, f32[1,8,128]{2,1,0:T(8,128)S(1)}, u32[]{:S(2)}, u32[]{:S(2)}) collective-permute-start(f32[1,8,128]{2,1,0:T(8,128)S(1)} %slice_maximum_fusion.peak), channel_id=1, source_target_pairs={{0,8},{1,9},{2,10},{3,11},{4,12},{5,13},{6,14},{7,15},{8,0},{9,1},... | collective-permute-start | bytes 12296 | tf_op jit(solution)/shard_map/ppermute | solution.py:50
  13.1 0.7 %shard_map.104 = (f32[6,4,2,32,128]{4,3,2,1,0:T(8,128)S(1)}, f32[8,8,128]{2,1,0:T(8,128)S(1)}, f32[6,8,128]{2,1,0:T(8,128)S(1)}, f32[32,8,128]{2,1,0:T(8,128)S(1)}) custom-call(f32[6,10,16,256]{3,2,1,0:T(8,128)S(1)} %pad_maximum_fusion.old, s32[129]{0:T(256)S(1)} %copy-done.2), custom_call_target="tpu_custom_call" | custom-call | flops 100000 | bytes 100000 | tf_op jit(solution)/shard_map/pallas_call | solution.py:802
  14.4 3.2 %shard_map.107.coef = f32[14,3,3,3,8,128]{5,4,3,2,1,0:T(8,128)S(1)} custom-call(s32[6144]{0:T(1024)S(1)} %reshape.17.neighbours, s32[1024]{0:T(1024)S(1)} %copy-done, s32[1024]{0:T(1024)S(1)} %copy-done.1), custom_call_target="tpu_custom_call" | custom-call | flops 500000 | bytes 500000 | tf_op jit(solution)/shard_map/pallas_call | solution.py:802
  17.7 0.7 %collective-permute-start.3 = (f32[32,8,128]{2,1,0:T(8,128)S(1)}, f32[32,8,128]{2,1,0:T(8,128)S(1)}, u32[]{:S(2)}, u32[]{:S(2)}) collective-permute-start(f32[32,8,128]{2,1,0:T(8,128)S(1)} %get-tuple-element.47), channel_id=1, source_target_pairs={{1,8},{3,10},{5,12},{7,14},{8,1},{9,73},{10,3},{11,75},{12,5},{13,... | collective-permute-start | bytes 393224 | tf_op jit(solution)/shard_map/ppermute | solution.py:50
  18.3 3.7 %collective-permute-start.4 = (f32[1,8,128]{2,1,0:T(8,128)S(1)}, f32[1,8,128]{2,1,0:T(8,128)S(1)}, u32[]{:S(2)}, u32[]{:S(2)}) collective-permute-start(f32[1,8,128]{2,1,0:T(8,128)S(1)} %get-tuple-element.48.peak), channel_id=1, source_target_pairs={{0,64},{1,65},{2,66},{3,67},{4,68},{5,69},{6,70},{7,71},{8,72},{9,... | collective-permute-start | bytes 12296 | tf_op jit(solution)/shard_map/ppermute | solution.py:50
  22.1 0.9 %collective-permute-done.4.x64 = f32[1,8,128]{2,1,0:T(8,128)S(1)} collective-permute-done((f32[1,8,128]{2,1,0:T(8,128)S(1)}, f32[1,8,128]{2,1,0:T(8,128)S(1)}, u32[]{:S(2)}, u32[]{:S(2)}) %collective-permute-start.4) | collective-permute-done | bytes 4128 | tf_op jit(solution)/shard_map/ppermute | solution.py:50
  23.1 2.8 %collective-permute-start.5 = (f32[38,8,128]{2,1,0:T(8,128)S(1)}, f32[38,8,128]{2,1,0:T(8,128)S(1)}, u32[]{:S(2)}, u32[]{:S(2)}) collective-permute-start(f32[38,8,128]{2,1,0:T(8,128)S(1)} %get-tuple-element.49), channel_id=1, source_target_pairs={{0,2},{1,3},{2,0},{3,1},{4,6},{5,7},{6,4},{7,5},{8,10},{9,11},{10,... | collective-permute-start | bytes 466952 | tf_op jit(solution)/shard_map/ppermute | solution.py:50
  26.0 5.0 %collective-permute-start.6 = (f32[37,8,128]{2,1,0:T(8,128)S(1)}, f32[37,8,128]{2,1,0:T(8,128)S(1)}, u32[]{:S(2)}, u32[]{:S(2)}) collective-permute-start(f32[37,8,128]{2,1,0:T(8,128)S(1)} %get-tuple-element.50), channel_id=1, source_target_pairs={{2,16},{3,17},{6,20},{7,21},{10,24},{11,25},{14,28},{15,29},{16,2}... | collective-permute-start | bytes 454664 | tf_op jit(solution)/shard_map/ppermute | solution.py:50
  31.3 0.7 %shard_map.110 = (f32[4,2,40,128]{3,2,1,0:T(8,128)S(1)}, f32[4,2,40,128]{3,2,1,0:T(8,128)S(1)}, f32[4,2,40,128]{3,2,1,0:T(8,128)S(1)}, f32[4,2,40,128]{3,2,1,0:T...) custom-call(f32[6,4,2,32,128]{4,3,2,1,0:T(8,128)S(1)} %get-tuple-ele, ...), custom_call_target="tpu_custom_call" | custom-call | flops 200000 | bytes 200000 | tf_op jit(solution)/shard_map/pallas_call | solution.py:802
  32.2 3.5 %collective-permute-done.8.x18 = f32[1,8,128]{2,1,0:T(8,128)S(1)} collective-permute-done((f32[1,8,128]{2,1,0:T(8,128)S(1)}, f32[1,8,128]{2,1,0:T(8,128)S(1)}, u32[]{:S(2)}, u32[]{:S(2)}) %collective-permute-start.8) | collective-permute-done | bytes 4128 | tf_op jit(solution)/shard_map/ppermute | solution.py:50
  35.7 1.4 %shard_map.111 = (f32[5,2,40,128]{3,2,1,0:T(8,128)S(1)}, f32[5,2,40,128]{3,2,1,0:T(8,128)S(1)}, f32[5,2,40,128]{3,2,1,0:T(8,128)S(1)}, f32[5,2,40,128]{3,2,1,0:T...) custom-call(f32[38,8,128]{2,1,0:T(8,128)S(1)} %collective-permute-do, ...), custom_call_target="tpu_custom_call" | custom-call | flops 100000 | bytes 100000 | tf_op jit(solution)/shard_map/pallas_call | solution.py:802
  37.5 0.7 %collective-permute-start.10 = (f32[38,8,128]{2,1,0:T(8,128)S(1)}, f32[38,8,128]{2,1,0:T(8,128)S(1)}, u32[]{:S(2)}, u32[]{:S(2)}) collective-permute-start(f32[38,8,128]{2,1,0:T(8,128)S(1)} %get-tuple-element.66), channel_id=1, source_target_pairs={{4,32},{5,33},{6,34},{7,35},{12,40},{13,41},{14,42},{15,43},{20,48... | collective-permute-start | bytes 466952 | tf_op jit(solution)/shard_map/ppermute | solution.py:50
  38.2 3.6 %collective-permute-start.11 = (f32[1,8,128]{2,1,0:T(8,128)S(1)}, f32[1,8,128]{2,1,0:T(8,128)S(1)}, u32[]{:S(2)}, u32[]{:S(2)}) collective-permute-start(f32[1,8,128]{2,1,0:T(8,128)S(1)} %get-tuple-element.67.peak), channel_id=1, source_target_pairs={{0,32},{1,33},{2,34},{3,35},{4,36},{5,37},{6,38},{7,39},{8,40},{9,... | collective-permute-start | bytes 12296 | tf_op jit(solution)/shard_map/ppermute | solution.py:50
  41.8 1.4 %collective-permute-start.12 = (f32[1,8,128]{2,1,0:T(8,128)S(1)}, f32[1,8,128]{2,1,0:T(8,128)S(1)}, u32[]{:S(2)}, u32[]{:S(2)}) collective-permute-start(f32[1,8,128]{2,1,0:T(8,128)S(1)} %get-tuple-element.67.peak), channel_id=1, source_target_pairs={{0,36},{1,37},{2,38},{3,39},{4,32},{5,33},{6,34},{7,35},{8,44},{9,... | collective-permute-start | bytes 12296 | tf_op jit(solution)/shard_map/ppermute | solution.py:50
  45.8 4.6 %shard_map.112 = (f32[4,2,32,128]{3,2,1,0:T(8,128)S(1)}, f32[4,2,32,128]{3,2,1,0:T(8,128)S(1)}, f32[2,16,256]{2,1,0:T(8,128)S(1)}, f32[2,16,256]{2,1,0:T(8,128)S(1)}) custom-call(f32[5,2,40,128]{3,2,1,0:T(8,128)S(1)} %get-tuple-element.60.c_in, f32[5,2,40,128]{3,2,1,0:T(8,128)S(1)} %get-tuple-element.61.u_in, f32[5,2,40,128]{3,2,1,0:T(8,128)S(1)} %get-tuple-element.62.s_in, ...), custom_call_target="tpu_custom_call" | custom-call | flops 800000 | bytes 800000 | tf_op jit(solution)/shard_map/pallas_call | solution.py:802
  50.4 9.9 %collective-permute-start.13 = (f32[2,16,256]{2,1,0:T(8,128)S(1)}, f32[2,16,256]{2,1,0:T(8,128)S(1)}, u32[]{:S(2)}, u32[]{:S(2)}) collective-permute-start(f32[2,16,256]{2,1,0:T(8,128)S(1)} %get-tuple-element.68), channel_id=1, source_target_pairs={{1,2},{2,1},{3,4},{4,3},{5,6},{6,5},{7,8},{8,7},{9,10},{10,9},{11,... | collective-permute-start | bytes 98312 | tf_op jit(solution)/shard_map/ppermute | solution.py:50
  60.4 0.6 shard_map.113
  61.0 0.8 %collective-permute-done.13 = f32[2,16,256]{2,1,0:T(8,128)S(1)} collective-permute-done((f32[2,16,256]{2,1,0:T(8,128)S(1)}, f32[2,16,256]{2,1,0:T(8,128)S(1)}, u32[]{:S(2)}, u32[]{:S(2)}) %collective-permute-start.13) | collective-permute-done | bytes 32800 | tf_op jit(solution)/shard_map/ppermute | solution.py:50
  61.9 1.3 %collective-permute-done.14 = f32[2,16,256]{2,1,0:T(8,128)S(1)} collective-permute-done((f32[2,16,256]{2,1,0:T(8,128)S(1)}, f32[2,16,256]{2,1,0:T(8,128)S(1)}, u32[]{:S(2)}, u32[]{:S(2)}) %collective-permute-start.14) | collective-permute-done | bytes 32800 | tf_op jit(solution)/shard_map/ppermute | solution.py:50
  63.1 0.8 %select_select_fusion = (f32[10,16,256]{2,1,0:T(8,128)}, f32[10,16,256]{2,1,0:T(8,128)}) fusion(f32[10,16,256]{2,1,0:T(8,128)S(1)} %get-tuple-element.73, f32[16,256]{1,0:T(8,128)S(1)} %get-tuple-element.78, f32[16,256]{1,0:T(8,128)S(1)} %get-tuple-element.85, pred[10]{0:T(512)(128)(4,1)S(1)} %get-tuple-element.86, pred[10]{0:T(512)(128)(4,1)S(1)} %get-tuple-element.87, ...), kind=kLoop, calls=%fused_computation.1 | loop fusion | flops 163840 | bytes 720916 | tf_op jit(solution)/shard_map/jit(_where)/select_n | solution.py:900
  (35 shorter events, 2.5 us)
Async XLA Ops:
  0.6 1.4 %copy-start = (s32[1024]{0:T(1024)S(1)}, s32[1024]{0:T(1024)}, u32[]{:S(2)}) copy-start(s32[1024]{0:T(1024)} %levels.3) | copy-start | bytes 12292
  0.6 1.4 %copy-start.2 = (s32[129]{0:T(256)S(1)}, s32[129]{0:T(256)}, u32[]{:S(2)}) copy-start(s32[129]{0:T(256)} %bounds.4) | copy-start | bytes 1552
  0.7 13.1 %copy-start.4 = (s32[1024,6]{0,1:T(8,128)S(1)}, s32[1024,6]{0,1:T(8,128)}, u32[]{:S(2)}) copy-start(s32[1024,6]{0,1:T(8,128)} %param.13) | copy-start | bytes 73732
  2.0 12.3 %copy-start.1 = (s32[1024]{0:T(1024)S(1)}, s32[1024]{0:T(1024)}, u32[]{:S(2)}) copy-start(s32[1024]{0:T(1024)} %refine.1) | copy-start | bytes 12292
  2.7 9.1 %collective-permute-start = (f32[57,8,128]{2,1,0:T(8,128)S(1)}, f32[57,8,128]{2,1,0:T(8,128)S(1)}, u32[]{:S(2)}, u32[]{:S(2)}) collective-permute-start(f32[57,8,128]{2,1,0:T(8,128)S(1)} %get-tuple-element.41), channel_id=1, source_target_pairs={{0,1},{1,0},{2,3},{3,2},{4,5},{5,4},{6,7},{7,6},{8,9},{9,8},{10,11... | collective-permute-start | bytes 700424 | tf_op jit(solution)/shard_map/ppermute | solution.py:50
  4.9 12.7 %collective-permute-start.1 = (f32[24,8,128]{2,1,0:T(8,128)S(1)}, f32[24,8,128]{2,1,0:T(8,128)S(1)}, u32[]{:S(2)}, u32[]{:S(2)}) collective-permute-start(f32[24,8,128]{2,1,0:T(8,128)S(1)} %get-tuple-element.42), channel_id=1, source_target_pairs={{1,2},{2,1},{3,4},{4,3},{5,6},{6,5},{7,8},{8,7},{9,10},{10,9},{11,... | collective-permute-start | bytes 294920 | tf_op jit(solution)/shard_map/ppermute | solution.py:50
  11.9 5.7 %collective-permute-start.2 = (f32[1,8,128]{2,1,0:T(8,128)S(1)}, f32[1,8,128]{2,1,0:T(8,128)S(1)}, u32[]{:S(2)}, u32[]{:S(2)}) collective-permute-start(f32[1,8,128]{2,1,0:T(8,128)S(1)} %slice_maximum_fusion.peak), channel_id=1, source_target_pairs={{0,8},{1,9},{2,10},{3,11},{4,12},{5,13},{6,14},{7,15},{8,0},{9,1},... | collective-permute-start | bytes 12296 | tf_op jit(solution)/shard_map/ppermute | solution.py:50
  17.7 5.4 %collective-permute-start.3 = (f32[32,8,128]{2,1,0:T(8,128)S(1)}, f32[32,8,128]{2,1,0:T(8,128)S(1)}, u32[]{:S(2)}, u32[]{:S(2)}) collective-permute-start(f32[32,8,128]{2,1,0:T(8,128)S(1)} %get-tuple-element.47), channel_id=1, source_target_pairs={{1,8},{3,10},{5,12},{7,14},{8,1},{9,73},{10,3},{11,75},{12,5},{13,... | collective-permute-start | bytes 393224 | tf_op jit(solution)/shard_map/ppermute | solution.py:50
  18.3 4.7 %collective-permute-start.4 = (f32[1,8,128]{2,1,0:T(8,128)S(1)}, f32[1,8,128]{2,1,0:T(8,128)S(1)}, u32[]{:S(2)}, u32[]{:S(2)}) collective-permute-start(f32[1,8,128]{2,1,0:T(8,128)S(1)} %get-tuple-element.48.peak), channel_id=1, source_target_pairs={{0,64},{1,65},{2,66},{3,67},{4,68},{5,69},{6,70},{7,71},{8,72},{9,... | collective-permute-start | bytes 12296 | tf_op jit(solution)/shard_map/ppermute | solution.py:50
  23.1 12.6 %collective-permute-start.5 = (f32[38,8,128]{2,1,0:T(8,128)S(1)}, f32[38,8,128]{2,1,0:T(8,128)S(1)}, u32[]{:S(2)}, u32[]{:S(2)}) collective-permute-start(f32[38,8,128]{2,1,0:T(8,128)S(1)} %get-tuple-element.49), channel_id=1, source_target_pairs={{0,2},{1,3},{2,0},{3,1},{4,6},{5,7},{6,4},{7,5},{8,10},{9,11},{10,... | collective-permute-start | bytes 466952 | tf_op jit(solution)/shard_map/ppermute | solution.py:50
  26.0 9.7 %collective-permute-start.6 = (f32[37,8,128]{2,1,0:T(8,128)S(1)}, f32[37,8,128]{2,1,0:T(8,128)S(1)}, u32[]{:S(2)}, u32[]{:S(2)}) collective-permute-start(f32[37,8,128]{2,1,0:T(8,128)S(1)} %get-tuple-element.50), channel_id=1, source_target_pairs={{2,16},{3,17},{6,20},{7,21},{10,24},{11,25},{14,28},{15,29},{16,2}... | collective-permute-start | bytes 454664 | tf_op jit(solution)/shard_map/ppermute | solution.py:50
  31.0 1.2 %collective-permute-start.7 = (f32[1,8,128]{2,1,0:T(8,128)S(1)}, f32[1,8,128]{2,1,0:T(8,128)S(1)}, u32[]{:S(2)}, u32[]{:S(2)}) collective-permute-start(f32[1,8,128]{2,1,0:T(8,128)S(1)} %get-tuple-element.51.peak), channel_id=1, source_target_pairs={{0,16},{1,17},{2,18},{3,19},{4,20},{5,21},{6,22},{7,23},{8,24},{9,... | collective-permute-start | bytes 12296 | tf_op jit(solution)/shard_map/ppermute | solution.py:50
  31.1 4.6 %collective-permute-start.8 = (f32[1,8,128]{2,1,0:T(8,128)S(1)}, f32[1,8,128]{2,1,0:T(8,128)S(1)}, u32[]{:S(2)}, u32[]{:S(2)}) collective-permute-start(f32[1,8,128]{2,1,0:T(8,128)S(1)} %get-tuple-element.51.peak), channel_id=1, source_target_pairs={{0,18},{1,19},{2,16},{3,17},{4,22},{5,23},{6,20},{7,21},{8,26},{9,... | collective-permute-start | bytes 12296 | tf_op jit(solution)/shard_map/ppermute | solution.py:50
  32.0 11.2 %copy-start.3 = (s32[129]{0:T(256)S(1)}, s32[129]{0:T(256)}, u32[]{:S(2)}) copy-start(s32[129]{0:T(256)} %bounds.5) | copy-start | bytes 1552
  37.1 8.7 %collective-permute-start.9 = (f32[39,8,128]{2,1,0:T(8,128)S(1)}, f32[39,8,128]{2,1,0:T(8,128)S(1)}, u32[]{:S(2)}, u32[]{:S(2)}) collective-permute-start(f32[39,8,128]{2,1,0:T(8,128)S(1)} %get-tuple-element.65), channel_id=1, source_target_pairs={{0,4},{1,5},{2,6},{3,7},{4,0},{5,1},{6,2},{7,3},{8,12},{9,13},{10,... | collective-permute-start | bytes 479240 | tf_op jit(solution)/shard_map/ppermute | solution.py:50
  37.5 8.2 %collective-permute-start.10 = (f32[38,8,128]{2,1,0:T(8,128)S(1)}, f32[38,8,128]{2,1,0:T(8,128)S(1)}, u32[]{:S(2)}, u32[]{:S(2)}) collective-permute-start(f32[38,8,128]{2,1,0:T(8,128)S(1)} %get-tuple-element.66), channel_id=1, source_target_pairs={{4,32},{5,33},{6,34},{7,35},{12,40},{13,41},{14,42},{15,43},{20,48... | collective-permute-start | bytes 466952 | tf_op jit(solution)/shard_map/ppermute | solution.py:50
  38.2 7.5 %collective-permute-start.11 = (f32[1,8,128]{2,1,0:T(8,128)S(1)}, f32[1,8,128]{2,1,0:T(8,128)S(1)}, u32[]{:S(2)}, u32[]{:S(2)}) collective-permute-start(f32[1,8,128]{2,1,0:T(8,128)S(1)} %get-tuple-element.67.peak), channel_id=1, source_target_pairs={{0,32},{1,33},{2,34},{3,35},{4,36},{5,37},{6,38},{7,39},{8,40},{9,... | collective-permute-start | bytes 12296 | tf_op jit(solution)/shard_map/ppermute | solution.py:50
  41.8 4.0 %collective-permute-start.12 = (f32[1,8,128]{2,1,0:T(8,128)S(1)}, f32[1,8,128]{2,1,0:T(8,128)S(1)}, u32[]{:S(2)}, u32[]{:S(2)}) collective-permute-start(f32[1,8,128]{2,1,0:T(8,128)S(1)} %get-tuple-element.67.peak), channel_id=1, source_target_pairs={{0,36},{1,37},{2,38},{3,39},{4,32},{5,33},{6,34},{7,35},{8,44},{9,... | collective-permute-start | bytes 12296 | tf_op jit(solution)/shard_map/ppermute | solution.py:50
  50.4 11.4 %collective-permute-start.13 = (f32[2,16,256]{2,1,0:T(8,128)S(1)}, f32[2,16,256]{2,1,0:T(8,128)S(1)}, u32[]{:S(2)}, u32[]{:S(2)}) collective-permute-start(f32[2,16,256]{2,1,0:T(8,128)S(1)} %get-tuple-element.68), channel_id=1, source_target_pairs={{1,2},{2,1},{3,4},{4,3},{5,6},{6,5},{7,8},{8,7},{9,10},{10,9},{11,... | collective-permute-start | bytes 98312 | tf_op jit(solution)/shard_map/ppermute | solution.py:50
  60.3 2.8 %collective-permute-start.14 = (f32[2,16,256]{2,1,0:T(8,128)S(1)}, f32[2,16,256]{2,1,0:T(8,128)S(1)}, u32[]{:S(2)}, u32[]{:S(2)}) collective-permute-start(f32[2,16,256]{2,1,0:T(8,128)S(1)} %get-tuple-element.69), channel_id=1, source_target_pairs={{0,1},{1,0},{2,3},{3,2},{4,5},{5,4},{6,7},{7,6},{8,9},{9,8},{10,11... | collective-permute-start | bytes 98312 | tf_op jit(solution)/shard_map/ppermute | solution.py:50

commit v6 on v4

--- a/solution.py
+++ b/solution.py
@@ -177,7 +177,7 @@
         flags[n] = jnp.full((8, 128), jnp.where(value, 1.0, 0.0), F32)
 
 
-def second_kernel(ib_in, flags, rb, ra, peak, x8, x9, coef, ib, peak_out):
+def second_kernel(ib_in, flags, rb, ra, peak, x16, x17, coef, ib, peak_out):
     d, tree, gi, gj, gk = where_am_i()
     sub, lane = iotas()
     high = gi % 2 == 1
@@ -190,7 +190,7 @@
             for g in range(4):
                 n = (g * 4 + q) * 2 + h
                 ib[n] = jnp.where(flag, groups[g], ib_in[n]) if q in (0, 3) else ib_in[n]
-    peak_out[0] = jnp.maximum(jnp.maximum(peak[0], ra[56]), jnp.maximum(x8[0], x9[0]))
+    peak_out[0] = jnp.maximum(jnp.maximum(peak[0], ra[56]), jnp.maximum(x16[0], x17[0]))
 
 
 def block_kernel(own, mine, flags, ra, rb, ext, ia):
@@ -553,13 +553,14 @@
 
 
 def outer_kernel(
-    ja, jb, peak, x16, coef, c_in, u2_in, src_in, prs_in, u1_in, chg_in, ka_in, kb_in,
+    ja, jb, peak, x8, coef, c_in, u2_in, src_in, prs_in, u1_in, chg_in, ka_in, kb_in,
     c40, u2, src, prs, chg, ka, kb, peak_out,
 ):
     d, tree, gi, gj, gk = where_am_i()
     sh = Shifts()
     wide = make_wide(None, ja, jb, gj)
     low5 = sh.lane5 < 64
+    low6 = lax.broadcasted_iota(jnp.int32, (48, 128), 1) < 64
     for jq in range(4):
         for kt in range(2):
             c40[jq, kt], u2[jq, kt] = c_in[jq, kt], u2_in[jq, kt]
@@ -580,19 +581,13 @@
         c40[4, kt] = jnp.where(low5, c_high, c_low)
         u_high, u_low = whole(2, 4, kt), whole(2, 5, kt)
         m_dn, m_up = coefficient(coef, 0, 2, kt), coefficient(coef, 1, 2, kt)
-        side = []
-        for n in range(2):
-            v40 = whole(1, 4 + n, kt)
-            v48 = jnp.concatenate([v40, v40[32:]], axis=0)
-            side.append(sh.change_i(c48[n], v48, m_dn, m_up))
+        v40 = jnp.where(low5, whole(1, 4, kt), whole(1, 5, kt))
+        v48 = jnp.concatenate([v40, v40[32:]], axis=0)
+        along_i = sh.change_i(jnp.where(low6, c48[0], c48[1]), v48, m_dn, m_up)
         m_dn, m_up = coefficient(coef, 2, 2, kt), coefficient(coef, 3, 2, kt)
-        side[0] = side[0] + sh.change_j(
-            c_high, c_low, c_in[3, kt], u_high, u_low, u1_in[3, kt], m_dn, None
-        )
-        side[1] = side[1] + sh.change_j(
-            c_low, c_in[0, kt], c_high, u_low, u1_in[0, kt], u_high, None, m_up
-        )
-        chg[4, kt] = jnp.where(low5, side[0], side[1])
+        high = sh.change_j(c_high, c_low, c_in[3, kt], u_high, u_low, u1_in[3, kt], m_dn, None)
+        low = sh.change_j(c_low, c_in[0, kt], c_high, u_low, u1_in[0, kt], u_high, None, m_up)
+        chg[4, kt] = along_i + jnp.where(low5, high, low)
         chg[0, kt] = chg_in[0, kt] + sh.change_j(
             c_in[0, kt], c_in[1, kt], c_low, u1_in[0, kt], u1_in[1, kt], u_low,
             coefficient(coef, 2, 0, kt), None,
@@ -606,7 +601,7 @@
     pack.block((3,), lambda kind, jq, kt, b: kinds[kind][jq, kt, pl.ds(8 * b, 8), :], ka, kb)
     pack.halo(lambda kind, kt, b: kinds[kind][4, kt, pl.ds(8 * b, 8), :], ka, kb)
     top = jnp.maximum(
-        jnp.maximum(peak[0], x16[0]), jnp.maximum(ja[J_BLOCKS], jb[J_BLOCKS])
+        jnp.maximum(peak[0], x8[0]), jnp.maximum(ja[J_BLOCKS], jb[J_BLOCKS])
     )
     ka[K_BLOCKS] = top
     kb[K_BLOCKS] = top
@@ -742,7 +737,7 @@
 
         for jq in range(4 if last else 5):
             jn, jp = (jq + 1) % 5, (jq + 4) % 5
-            for kt in range(2 if last else 3):
+            for kt in range(2 if last or (sweep == SWEEPS - 2 and jq == 4) else 3):
                 kn, kp = (kt + 1) % 3, (kt + 2) % 3
                 p = old(jq, kt)
                 total = wts[0, jq, kt] * rs(p, 1) + wts[1, jq, kt] * rs(p, -1)
@@ -820,7 +815,7 @@
     ra, rb, peak = call(
         first_kernel, [VM, SM, SM], (blocks(57), blocks(24), one), (old, levels, bounds_old)
     )
-    x8, x9 = send(peak, flip_pairs(8)), send(peak, flip_pairs(9))
+    x16, x17 = send(peak, flip_pairs(16)), send(peak, flip_pairs(17))
     rb, ra = send(rb, ODD_PAIRS), send(ra, EVEN_PAIRS)
     own, mine, flags, ib = call(
         own_kernel,
@@ -840,7 +835,7 @@
         second_kernel,
         [VM] * 7 + [pl.BlockSpec(memory_space=pl.ANY)],
         (blocks(32), one),
-        (ib, flags, rb, ra, peak, x8, x9, coef),
+        (ib, flags, rb, ra, peak, x16, x17, coef),
     )
     x64 = send(peak, flip_pairs(64))
     ib = send(ib, axis_pairs(0, 1))
@@ -856,7 +851,7 @@
         (blocks(J_BLOCKS + 1), blocks(J_BLOCKS + 1), one),
         (ext, ia, ib, peak, x64),
     )
-    x16 = send(peak, flip_pairs(16))
+    x8 = jnp.maximum(send(peak, flip_pairs(8)), send(peak, flip_pairs(10)))
     ja, jb = send(ja, axis_pairs(1, 0)), send(jb, axis_pairs(1, 1))
     inner = call(
         inner_kernel,
@@ -870,7 +865,7 @@
         outer_kernel,
         [VM] * 13,
         (shape(5, 2, 40, 128),) * 5 + (blocks(K_BLOCKS + 1),) * 2 + (one,),
-        (ja, jb, peak, x16, coef, *inner),
+        (ja, jb, peak, x8, coef, *inner),
         (),
         1,
     )

time: 62.7 us -> 62.5 us (level)
  waiting for transfers between devices: 16.8 us -> 14.3 us
  starting transfers between devices: 27.3 us -> 29.3 us
    ppermute x14 -> x15, waiting for transfers between devices: 16.8 us -> 14.3 us  [send(): return lax.ppermute(x, AXES, pairs)]
    ppermute x14 -> x15, starting transfers between devices: 27.3 us -> 29.3 us  [send(): return lax.ppermute(x, AXES, pairs)]
  transfers between devices with their start and end apart: 14 -> 15, of which waited for: 7 -> 5; matrix products, arithmetic and copies ran while one was open for 2% -> 2% of each run, Pallas kernels for 9% -> 9%
where the time goes in v6:
time: 62.5 us; the launch traced here: 62 us
  starting transfers between devices  29.3 us (47%)
  waiting for transfers between devices  14.3 us (23%)
  Pallas kernels  12.1 us (19%)
  between operations  2.86 us (5%)
  other arithmetic  2.19 us (4%)
  local copies, waits for them, and re-layouts  1.18 us (2%)
    ppermute x15, starting transfers between devices, send(): return lax.ppermute(x, AXES, pairs)  29.3 us
    ppermute x15, waiting for transfers between devices, send(): return lax.ppermute(x, AXES, pairs)  14.3 us
    pallas_call x10, Pallas kernels, call(): pl.pallas_call(kernel, out_shape=outs, in_specs=specs, out_specs=jax.tree...  12.1 us
    concatenate x1, other arithmetic, local(): jnp.concatenate([volume[None], velocity, source[None], pressure_prev[None...  1.34 us
  transfers between devices with their start and end apart: 15, of which 5 were waited for; matrix products, arithmetic and copies ran while one was open for 2% of the time, Pallas kernels for 9%

profile of v6, /device:TPU:1, one launch (start us, length us, event | category | flops | bytes accessed | tf_op | source)
XLA Modules:
  0.0 62.0 jit_solution(3502504261188840641)
XLA Ops:
  0.7 1.3 %pad_maximum_fusion.old = f32[6,10,16,256]{3,2,1,0:T(8,128)S(1)} fusion(f32[1,10,16,256]{3,2,1,0:T(8,128)} %bitcast.13, f32[1,10,16,256]{3,2,1,0:T(8,128)} %bitcast.14, f32[3,10,16,256]{3,2,1,0:T(8,128)} %param.10, f32[1,10,16,256]{3,2,1,0:T(8,128)} %bitcast.15), kind=kLoop, calls=%fused_computation | loop fusion | flops 737280 | bytes 1966080 | tf_op jit(solution)/shard_map/concatenate | solution.py:814
  2.0 0.7 %shard_map.105 = (f32[57,8,128]{2,1,0:T(8,128)S(1)}, f32[24,8,128]{2,1,0:T(8,128)S(1)}, f32[1,8,128]{2,1,0:T(8,128)S(1)}) custom-call(f32[6,10,16,256]{3,2,1,0:T(8,128)S(1)} %pad_maximum_fusion.old, s32[1024]{0:T(1024)S(1)} %copy-done, s32[129]{0:T(256)S(1)} %copy-done.2), custom_call_target="tpu_custom_call" | custom-call | flops 100000 | bytes 100000 | tf_op jit(solution)/shard_map/pallas_call | solution.py:798
  2.7 2.1 %collective-permute-start = (f32[57,8,128]{2,1,0:T(8,128)S(1)}, f32[57,8,128]{2,1,0:T(8,128)S(1)}, u32[]{:S(2)}, u32[]{:S(2)}) collective-permute-start(f32[57,8,128]{2,1,0:T(8,128)S(1)} %get-tuple-element.41), channel_id=1, source_target_pairs={{0,1},{1,0},{2,3},{3,2},{4,5},{5,4},{6,7},{7,6},{8,9},{9,8},{10,11... | collective-permute-start | bytes 700424 | tf_op jit(solution)/shard_map/ppermute | solution.py:49
  4.9 7.0 %collective-permute-start.1 = (f32[24,8,128]{2,1,0:T(8,128)S(1)}, f32[24,8,128]{2,1,0:T(8,128)S(1)}, u32[]{:S(2)}, u32[]{:S(2)}) collective-permute-start(f32[24,8,128]{2,1,0:T(8,128)S(1)} %get-tuple-element.42), channel_id=1, source_target_pairs={{1,2},{2,1},{3,4},{4,3},{5,6},{6,5},{7,8},{8,7},{9,10},{10,9},{11,... | collective-permute-start | bytes 294920 | tf_op jit(solution)/shard_map/ppermute | solution.py:49
  12.1 0.7 %shard_map.104 = (f32[6,4,2,32,128]{4,3,2,1,0:T(8,128)S(1)}, f32[8,8,128]{2,1,0:T(8,128)S(1)}, f32[6,8,128]{2,1,0:T(8,128)S(1)}, f32[32,8,128]{2,1,0:T(8,128)S(1)}) custom-call(f32[6,10,16,256]{3,2,1,0:T(8,128)S(1)} %pad_maximum_fusion.old, s32[129]{0:T(256)S(1)} %copy-done.2), custom_call_target="tpu_custom_call" | custom-call | flops 100000 | bytes 100000 | tf_op jit(solution)/shard_map/pallas_call | solution.py:798
  13.0 0.3 reshape.17.neighbours
  13.3 3.2 %shard_map.107.coef = f32[14,3,3,3,8,128]{5,4,3,2,1,0:T(8,128)S(1)} custom-call(s32[6144]{0:T(1024)S(1)} %reshape.17.neighbours, s32[1024]{0:T(1024)S(1)} %copy-done, s32[1024]{0:T(1024)S(1)} %copy-done.1), custom_call_target="tpu_custom_call" | custom-call | flops 500000 | bytes 500000 | tf_op jit(solution)/shard_map/pallas_call | solution.py:798
  16.6 3.7 %collective-permute-start.4 = (f32[32,8,128]{2,1,0:T(8,128)S(1)}, f32[32,8,128]{2,1,0:T(8,128)S(1)}, u32[]{:S(2)}, u32[]{:S(2)}) collective-permute-start(f32[32,8,128]{2,1,0:T(8,128)S(1)} %get-tuple-element.47), channel_id=1, source_target_pairs={{0,64},{1,8},{2,66},{3,10},{4,68},{5,12},{6,70},{7,14},{8,1},{9,73... | collective-permute-start | bytes 393224 | tf_op jit(solution)/shard_map/ppermute | solution.py:49
  20.5 3.9 %collective-permute-done.5.x64 = f32[1,8,128]{2,1,0:T(8,128)S(1)} collective-permute-done((f32[1,8,128]{2,1,0:T(8,128)S(1)}, f32[1,8,128]{2,1,0:T(8,128)S(1)}, u32[]{:S(2)}, u32[]{:S(2)}) %collective-permute-start.5) | collective-permute-done | bytes 4128 | tf_op jit(solution)/shard_map/ppermute | solution.py:49
  24.5 0.9 %collective-permute-start.6 = (f32[38,8,128]{2,1,0:T(8,128)S(1)}, f32[38,8,128]{2,1,0:T(8,128)S(1)}, u32[]{:S(2)}, u32[]{:S(2)}) collective-permute-start(f32[38,8,128]{2,1,0:T(8,128)S(1)} %get-tuple-element.49), channel_id=1, source_target_pairs={{0,2},{1,3},{2,0},{3,1},{4,6},{5,7},{6,4},{7,5},{8,10},{9,11},{10,... | collective-permute-start | bytes 466952 | tf_op jit(solution)/shard_map/ppermute | solution.py:49
  25.4 4.0 %collective-permute-start.7 = (f32[38,8,128]{2,1,0:T(8,128)S(1)}, f32[38,8,128]{2,1,0:T(8,128)S(1)}, u32[]{:S(2)}, u32[]{:S(2)}) collective-permute-start(f32[38,8,128]{2,1,0:T(8,128)S(1)} %get-tuple-element.50), channel_id=1, source_target_pairs={{0,18},{1,19},{2,16},{3,17},{4,22},{5,23},{6,20},{7,21},{8,26},{9,... | collective-permute-start | bytes 466952 | tf_op jit(solution)/shard_map/ppermute | solution.py:49
  29.4 0.9 %collective-permute-start.8 = (f32[1,8,128]{2,1,0:T(8,128)S(1)}, f32[1,8,128]{2,1,0:T(8,128)S(1)}, u32[]{:S(2)}, u32[]{:S(2)}) collective-permute-start(f32[1,8,128]{2,1,0:T(8,128)S(1)} %get-tuple-element.51.peak), channel_id=1, source_target_pairs={{0,8},{1,9},{2,10},{3,11},{4,12},{5,13},{6,14},{7,15},{8,0},{9,1},... | collective-permute-start | bytes 12296 | tf_op jit(solution)/shard_map/ppermute | solution.py:49
  30.3 2.7 %collective-permute-start.9 = (f32[1,8,128]{2,1,0:T(8,128)S(1)}, f32[1,8,128]{2,1,0:T(8,128)S(1)}, u32[]{:S(2)}, u32[]{:S(2)}) collective-permute-start(f32[1,8,128]{2,1,0:T(8,128)S(1)} %get-tuple-element.51.peak), channel_id=1, source_target_pairs={{0,10},{1,11},{2,8},{3,9},{4,14},{5,15},{6,12},{7,13},{8,2},{9,3},... | collective-permute-start | bytes 12296 | tf_op jit(solution)/shard_map/ppermute | solution.py:49
  33.0 0.7 %shard_map.110 = (f32[4,2,40,128]{3,2,1,0:T(8,128)S(1)}, f32[4,2,40,128]{3,2,1,0:T(8,128)S(1)}, f32[4,2,40,128]{3,2,1,0:T(8,128)S(1)}, f32[4,2,40,128]{3,2,1,0:T...) custom-call(f32[6,4,2,32,128]{4,3,2,1,0:T(8,128)S(1)} %get-tuple-ele, ...), custom_call_target="tpu_custom_call" | custom-call | flops 200000 | bytes 200000 | tf_op jit(solution)/shard_map/pallas_call | solution.py:798
  33.8 2.9 %collective-permute-done.9 = f32[1,8,128]{2,1,0:T(8,128)S(1)} collective-permute-done((f32[1,8,128]{2,1,0:T(8,128)S(1)}, f32[1,8,128]{2,1,0:T(8,128)S(1)}, u32[]{:S(2)}, u32[]{:S(2)}) %collective-permute-start.9) | collective-permute-done | bytes 4128 | tf_op jit(solution)/shard_map/ppermute | solution.py:49
  36.7 1.3 %shard_map.111 = (f32[5,2,40,128]{3,2,1,0:T(8,128)S(1)}, f32[5,2,40,128]{3,2,1,0:T(8,128)S(1)}, f32[5,2,40,128]{3,2,1,0:T(8,128)S(1)}, f32[5,2,40,128]{3,2,1,0:T...) custom-call(f32[38,8,128]{2,1,0:T(8,128)S(1)} %collective-permute-do, ...), custom_call_target="tpu_custom_call" | custom-call | flops 100000 | bytes 100000 | tf_op jit(solution)/shard_map/pallas_call | solution.py:798
  38.2 2.5 %collective-permute-start.11 = (f32[39,8,128]{2,1,0:T(8,128)S(1)}, f32[39,8,128]{2,1,0:T(8,128)S(1)}, u32[]{:S(2)}, u32[]{:S(2)}) collective-permute-start(f32[39,8,128]{2,1,0:T(8,128)S(1)} %get-tuple-element.66), channel_id=1, source_target_pairs={{0,36},{1,37},{2,38},{3,39},{4,32},{5,33},{6,34},{7,35},{8,44},{9,... | collective-permute-start | bytes 479240 | tf_op jit(solution)/shard_map/ppermute | solution.py:49
  40.8 0.6 fusion
  43.5 4.5 %collective-permute-done.11.kb = f32[39,8,128]{2,1,0:T(8,128)S(1)} collective-permute-done((f32[39,8,128]{2,1,0:T(8,128)S(1)}, f32[39,8,128]{2,1,0:T(8,128)S(1)}, u32[]{:S(2)}, u32[]{:S(2)}) %collective-permute-start.11) | collective-permute-done | bytes 159776 | tf_op jit(solution)/shard_map/ppermute | solution.py:49
  47.9 4.6 %shard_map.112 = (f32[4,2,32,128]{3,2,1,0:T(8,128)S(1)}, f32[4,2,32,128]{3,2,1,0:T(8,128)S(1)}, f32[2,16,256]{2,1,0:T(8,128)S(1)}, f32[2,16,256]{2,1,0:T(8,128)S(1)}) custom-call(f32[5,2,40,128]{3,2,1,0:T(8,128)S(1)} %get-tuple-element.60.c_in, f32[5,2,40,128]{3,2,1,0:T(8,128)S(1)} %get-tuple-element.61.u_in, f32[5,2,40,128]{3,2,1,0:T(8,128)S(1)} %get-tuple-element.62.s_in, ...), custom_call_target="tpu_custom_call" | custom-call | flops 800000 | bytes 800000 | tf_op jit(solution)/shard_map/pallas_call | solution.py:798
  52.6 4.9 %collective-permute-start.13 = (f32[2,16,256]{2,1,0:T(8,128)S(1)}, f32[2,16,256]{2,1,0:T(8,128)S(1)}, u32[]{:S(2)}, u32[]{:S(2)}) collective-permute-start(f32[2,16,256]{2,1,0:T(8,128)S(1)} %get-tuple-element.68), channel_id=1, source_target_pairs={{1,2},{2,1},{3,4},{4,3},{5,6},{6,5},{7,8},{8,7},{9,10},{10,9},{11,... | collective-permute-start | bytes 98312 | tf_op jit(solution)/shard_map/ppermute | solution.py:49
  57.6 0.6 shard_map.113
  58.2 2.9 %collective-permute-done.13 = f32[2,16,256]{2,1,0:T(8,128)S(1)} collective-permute-done((f32[2,16,256]{2,1,0:T(8,128)S(1)}, f32[2,16,256]{2,1,0:T(8,128)S(1)}, u32[]{:S(2)}, u32[]{:S(2)}) %collective-permute-start.13) | collective-permute-done | bytes 32800 | tf_op jit(solution)/shard_map/ppermute | solution.py:49
  61.2 0.8 %select_select_fusion = (f32[10,16,256]{2,1,0:T(8,128)}, f32[10,16,256]{2,1,0:T(8,128)}) fusion(f32[10,16,256]{2,1,0:T(8,128)S(1)} %get-tuple-element.73, f32[16,256]{1,0:T(8,128)S(1)} %get-tuple-element.78, f32[16,256]{1,0:T(8,128)S(1)} %get-tuple-element.85, pred[10]{0:T(512)(128)(4,1)S(1)} %get-tuple-element.86, pred[10]{0:T(512)(128)(4,1)S(1)} %get-tuple-element.87, ...), kind=kLoop, calls=%fused_computation.1 | loop fusion | flops 163840 | bytes 720916 | tf_op jit(solution)/shard_map/jit(_where)/select_n | solution.py:895
  (35 shorter events, 1.2 us)
Async XLA Ops:
  0.6 1.4 %copy-start.2 = (s32[129]{0:T(256)S(1)}, s32[129]{0:T(256)}, u32[]{:S(2)}) copy-start(s32[129]{0:T(256)} %bounds.4) | copy-start | bytes 1552
  0.6 1.4 %copy-start = (s32[1024]{0:T(1024)S(1)}, s32[1024]{0:T(1024)}, u32[]{:S(2)}) copy-start(s32[1024]{0:T(1024)} %levels.3) | copy-start | bytes 12292
  0.7 12.1 %copy-start.4 = (s32[1024,6]{0,1:T(8,128)S(1)}, s32[1024,6]{0,1:T(8,128)}, u32[]{:S(2)}) copy-start(s32[1024,6]{0,1:T(8,128)} %param.13) | copy-start | bytes 73732
  2.0 11.3 %copy-start.1 = (s32[1024]{0:T(1024)S(1)}, s32[1024]{0:T(1024)}, u32[]{:S(2)}) copy-start(s32[1024]{0:T(1024)} %refine.1) | copy-start | bytes 12292
  2.7 13.8 %collective-permute-start = (f32[57,8,128]{2,1,0:T(8,128)S(1)}, f32[57,8,128]{2,1,0:T(8,128)S(1)}, u32[]{:S(2)}, u32[]{:S(2)}) collective-permute-start(f32[57,8,128]{2,1,0:T(8,128)S(1)} %get-tuple-element.41), channel_id=1, source_target_pairs={{0,1},{1,0},{2,3},{3,2},{4,5},{5,4},{6,7},{7,6},{8,9},{9,8},{10,11... | collective-permute-start | bytes 700424 | tf_op jit(solution)/shard_map/ppermute | solution.py:49
  4.9 11.7 %collective-permute-start.1 = (f32[24,8,128]{2,1,0:T(8,128)S(1)}, f32[24,8,128]{2,1,0:T(8,128)S(1)}, u32[]{:S(2)}, u32[]{:S(2)}) collective-permute-start(f32[24,8,128]{2,1,0:T(8,128)S(1)} %get-tuple-element.42), channel_id=1, source_target_pairs={{1,2},{2,1},{3,4},{4,3},{5,6},{6,5},{7,8},{8,7},{9,10},{10,9},{11,... | collective-permute-start | bytes 294920 | tf_op jit(solution)/shard_map/ppermute | solution.py:49
  11.9 4.7 %collective-permute-start.2 = (f32[1,8,128]{2,1,0:T(8,128)S(1)}, f32[1,8,128]{2,1,0:T(8,128)S(1)}, u32[]{:S(2)}, u32[]{:S(2)}) collective-permute-start(f32[1,8,128]{2,1,0:T(8,128)S(1)} %get-tuple-element.46.peak), channel_id=1, source_target_pairs={{0,16},{1,17},{2,18},{3,19},{4,20},{5,21},{6,22},{7,23},{8,24},{9,... | collective-permute-start | bytes 12296 | tf_op jit(solution)/shard_map/ppermute | solution.py:49
  12.0 4.6 %collective-permute-start.3 = (f32[1,8,128]{2,1,0:T(8,128)S(1)}, f32[1,8,128]{2,1,0:T(8,128)S(1)}, u32[]{:S(2)}, u32[]{:S(2)}) collective-permute-start(f32[1,8,128]{2,1,0:T(8,128)S(1)} %get-tuple-element.46.peak), channel_id=1, source_target_pairs={{0,17},{1,16},{2,19},{3,18},{4,21},{5,20},{6,23},{7,22},{8,25},{9,... | collective-permute-start | bytes 12296 | tf_op jit(solution)/shard_map/ppermute | solution.py:49
  16.6 7.7 %collective-permute-start.4 = (f32[32,8,128]{2,1,0:T(8,128)S(1)}, f32[32,8,128]{2,1,0:T(8,128)S(1)}, u32[]{:S(2)}, u32[]{:S(2)}) collective-permute-start(f32[32,8,128]{2,1,0:T(8,128)S(1)} %get-tuple-element.47), channel_id=1, source_target_pairs={{0,64},{1,8},{2,66},{3,10},{4,68},{5,12},{6,70},{7,14},{8,1},{9,73... | collective-permute-start | bytes 393224 | tf_op jit(solution)/shard_map/ppermute | solution.py:49
  20.3 4.1 %collective-permute-start.5 = (f32[1,8,128]{2,1,0:T(8,128)S(1)}, f32[1,8,128]{2,1,0:T(8,128)S(1)}, u32[]{:S(2)}, u32[]{:S(2)}) collective-permute-start(f32[1,8,128]{2,1,0:T(8,128)S(1)} %get-tuple-element.48.peak), channel_id=1, source_target_pairs={{0,64},{1,65},{2,66},{3,67},{4,68},{5,69},{6,70},{7,71},{8,72},{9,... | collective-permute-start | bytes 12296 | tf_op jit(solution)/shard_map/ppermute | solution.py:49
  24.5 12.2 %collective-permute-start.6 = (f32[38,8,128]{2,1,0:T(8,128)S(1)}, f32[38,8,128]{2,1,0:T(8,128)S(1)}, u32[]{:S(2)}, u32[]{:S(2)}) collective-permute-start(f32[38,8,128]{2,1,0:T(8,128)S(1)} %get-tuple-element.49), channel_id=1, source_target_pairs={{0,2},{1,3},{2,0},{3,1},{4,6},{5,7},{6,4},{7,5},{8,10},{9,11},{10,... | collective-permute-start | bytes 466952 | tf_op jit(solution)/shard_map/ppermute | solution.py:49
  25.4 11.3 %collective-permute-start.7 = (f32[38,8,128]{2,1,0:T(8,128)S(1)}, f32[38,8,128]{2,1,0:T(8,128)S(1)}, u32[]{:S(2)}, u32[]{:S(2)}) collective-permute-start(f32[38,8,128]{2,1,0:T(8,128)S(1)} %get-tuple-element.50), channel_id=1, source_target_pairs={{0,18},{1,19},{2,16},{3,17},{4,22},{5,23},{6,20},{7,21},{8,26},{9,... | collective-permute-start | bytes 466952 | tf_op jit(solution)/shard_map/ppermute | solution.py:49
  29.4 4.3 %collective-permute-start.8 = (f32[1,8,128]{2,1,0:T(8,128)S(1)}, f32[1,8,128]{2,1,0:T(8,128)S(1)}, u32[]{:S(2)}, u32[]{:S(2)}) collective-permute-start(f32[1,8,128]{2,1,0:T(8,128)S(1)} %get-tuple-element.51.peak), channel_id=1, source_target_pairs={{0,8},{1,9},{2,10},{3,11},{4,12},{5,13},{6,14},{7,15},{8,0},{9,1},... | collective-permute-start | bytes 12296 | tf_op jit(solution)/shard_map/ppermute | solution.py:49
  30.3 6.4 %collective-permute-start.9 = (f32[1,8,128]{2,1,0:T(8,128)S(1)}, f32[1,8,128]{2,1,0:T(8,128)S(1)}, u32[]{:S(2)}, u32[]{:S(2)}) collective-permute-start(f32[1,8,128]{2,1,0:T(8,128)S(1)} %get-tuple-element.51.peak), channel_id=1, source_target_pairs={{0,10},{1,11},{2,8},{3,9},{4,14},{5,15},{6,12},{7,13},{8,2},{9,3},... | collective-permute-start | bytes 12296 | tf_op jit(solution)/shard_map/ppermute | solution.py:49
  33.8 7.1 %copy-start.3 = (s32[129]{0:T(256)S(1)}, s32[129]{0:T(256)}, u32[]{:S(2)}) copy-start(s32[129]{0:T(256)} %bounds.5) | copy-start | bytes 1552
  38.1 5.4 %collective-permute-start.10 = (f32[39,8,128]{2,1,0:T(8,128)S(1)}, f32[39,8,128]{2,1,0:T(8,128)S(1)}, u32[]{:S(2)}, u32[]{:S(2)}) collective-permute-start(f32[39,8,128]{2,1,0:T(8,128)S(1)} %get-tuple-element.65), channel_id=1, source_target_pairs={{0,4},{1,5},{2,6},{3,7},{4,0},{5,1},{6,2},{7,3},{8,12},{9,13},{10,... | collective-permute-start | bytes 479240 | tf_op jit(solution)/shard_map/ppermute | solution.py:49
  38.2 9.8 %collective-permute-start.11 = (f32[39,8,128]{2,1,0:T(8,128)S(1)}, f32[39,8,128]{2,1,0:T(8,128)S(1)}, u32[]{:S(2)}, u32[]{:S(2)}) collective-permute-start(f32[39,8,128]{2,1,0:T(8,128)S(1)} %get-tuple-element.66), channel_id=1, source_target_pairs={{0,36},{1,37},{2,38},{3,39},{4,32},{5,33},{6,34},{7,35},{8,44},{9,... | collective-permute-start | bytes 479240 | tf_op jit(solution)/shard_map/ppermute | solution.py:49
  40.7 2.8 %collective-permute-start.12 = (f32[1,8,128]{2,1,0:T(8,128)S(1)}, f32[1,8,128]{2,1,0:T(8,128)S(1)}, u32[]{:S(2)}, u32[]{:S(2)}) collective-permute-start(f32[1,8,128]{2,1,0:T(8,128)S(1)} %get-tuple-element.67.peak), channel_id=1, source_target_pairs={{0,32},{1,33},{2,34},{3,35},{4,36},{5,37},{6,38},{7,39},{8,40},{9,... | collective-permute-start | bytes 12296 | tf_op jit(solution)/shard_map/ppermute | solution.py:49
  52.6 8.6 %collective-permute-start.13 = (f32[2,16,256]{2,1,0:T(8,128)S(1)}, f32[2,16,256]{2,1,0:T(8,128)S(1)}, u32[]{:S(2)}, u32[]{:S(2)}) collective-permute-start(f32[2,16,256]{2,1,0:T(8,128)S(1)} %get-tuple-element.68), channel_id=1, source_target_pairs={{1,2},{2,1},{3,4},{4,3},{5,6},{6,5},{7,8},{8,7},{9,10},{10,9},{11,... | collective-permute-start | bytes 98312 | tf_op jit(solution)/shard_map/ppermute | solution.py:49
  57.4 3.7 %collective-permute-start.14 = (f32[2,16,256]{2,1,0:T(8,128)S(1)}, f32[2,16,256]{2,1,0:T(8,128)S(1)}, u32[]{:S(2)}, u32[]{:S(2)}) collective-permute-start(f32[2,16,256]{2,1,0:T(8,128)S(1)} %get-tuple-element.69), channel_id=1, source_target_pairs={{0,1},{1,0},{2,3},{3,2},{4,5},{5,4},{6,7},{7,6},{8,9},{9,8},{10,11... | collective-permute-start | bytes 98312 | tf_op jit(solution)/shard_map/ppermute | solution.py:49

commit v7 on v6

--- a/solution.py
+++ b/solution.py
@@ -553,7 +553,7 @@
 
 
 def outer_kernel(
-    ja, jb, peak, x8, coef, c_in, u2_in, src_in, prs_in, u1_in, chg_in, ka_in, kb_in,
+    ja, jb, peak, x8, x10, coef, c_in, u2_in, src_in, prs_in, u1_in, chg_in, ka_in, kb_in,
     c40, u2, src, prs, chg, ka, kb, peak_out,
 ):
     d, tree, gi, gj, gk = where_am_i()
@@ -601,7 +601,8 @@
     pack.block((3,), lambda kind, jq, kt, b: kinds[kind][jq, kt, pl.ds(8 * b, 8), :], ka, kb)
     pack.halo(lambda kind, kt, b: kinds[kind][4, kt, pl.ds(8 * b, 8), :], ka, kb)
     top = jnp.maximum(
-        jnp.maximum(peak[0], x8[0]), jnp.maximum(ja[J_BLOCKS], jb[J_BLOCKS])
+        jnp.maximum(jnp.maximum(peak[0], x8[0]), x10[0]),
+        jnp.maximum(ja[J_BLOCKS], jb[J_BLOCKS]),
     )
     ka[K_BLOCKS] = top
     kb[K_BLOCKS] = top
@@ -851,7 +852,7 @@
         (blocks(J_BLOCKS + 1), blocks(J_BLOCKS + 1), one),
         (ext, ia, ib, peak, x64),
     )
-    x8 = jnp.maximum(send(peak, flip_pairs(8)), send(peak, flip_pairs(10)))
+    x8, x10 = send(peak, flip_pairs(8)), send(peak, flip_pairs(10))
     ja, jb = send(ja, axis_pairs(1, 0)), send(jb, axis_pairs(1, 1))
     inner = call(
         inner_kernel,
@@ -863,9 +864,9 @@
     )
     *early, ka, kb, peak = call(
         outer_kernel,
-        [VM] * 13,
+        [VM] * 14,
         (shape(5, 2, 40, 128),) * 5 + (blocks(K_BLOCKS + 1),) * 2 + (one,),
-        (ja, jb, peak, x8, coef, *inner),
+        (ja, jb, peak, x8, x10, coef, *inner),
         (),
         1,
     )

time: 62.5 us -> 62.5 us (level)
  no operation moved by 1% of the time
where the time goes in v7:
time: 62.5 us; the launch traced here: 62 us
  starting transfers between devices  29.3 us (47%)
  waiting for transfers between devices  14.3 us (23%)
  Pallas kernels  12.1 us (19%)
  between operations  2.86 us (5%)
  other arithmetic  2.19 us (4%)
  local copies, waits for them, and re-layouts  1.18 us (2%)
    ppermute x15, starting transfers between devices, send(): return lax.ppermute(x, AXES, pairs)  29.3 us
    ppermute x15, waiting for transfers between devices, send(): return lax.ppermute(x, AXES, pairs)  14.3 us
    pallas_call x10, Pallas kernels, call(): pl.pallas_call(kernel, out_shape=outs, in_specs=specs, out_specs=jax.tree...  12.1 us
    concatenate x1, other arithmetic, local(): jnp.concatenate([volume[None], velocity, source[None], pressure_prev[None...  1.34 us
  transfers between devices with their start and end apart: 15, of which 5 were waited for; matrix products, arithmetic and copies ran while one was open for 2% of the time, Pallas kernels for 9%

profile of v7, /device:TPU:1, one launch (start us, length us, event | category | flops | bytes accessed | tf_op | source)
XLA Modules:
  0.0 62.0 jit_solution(18384375232557990448)
XLA Ops:
  0.7 1.3 %pad_maximum_fusion.old = f32[6,10,16,256]{3,2,1,0:T(8,128)S(1)} fusion(f32[1,10,16,256]{3,2,1,0:T(8,128)} %bitcast.13, f32[1,10,16,256]{3,2,1,0:T(8,128)} %bitcast.14, f32[3,10,16,256]{3,2,1,0:T(8,128)} %param.10, f32[1,10,16,256]{3,2,1,0:T(8,128)} %bitcast.15), kind=kLoop, calls=%fused_computation | loop fusion | flops 737280 | bytes 1966080 | tf_op jit(solution)/shard_map/concatenate | solution.py:815
  2.0 0.7 %shard_map.105 = (f32[57,8,128]{2,1,0:T(8,128)S(1)}, f32[24,8,128]{2,1,0:T(8,128)S(1)}, f32[1,8,128]{2,1,0:T(8,128)S(1)}) custom-call(f32[6,10,16,256]{3,2,1,0:T(8,128)S(1)} %pad_maximum_fusion.old, s32[1024]{0:T(1024)S(1)} %copy-done, s32[129]{0:T(256)S(1)} %copy-done.2), custom_call_target="tpu_custom_call" | custom-call | flops 100000 | bytes 100000 | tf_op jit(solution)/shard_map/pallas_call | solution.py:799
  2.7 2.1 %collective-permute-start = (f32[57,8,128]{2,1,0:T(8,128)S(1)}, f32[57,8,128]{2,1,0:T(8,128)S(1)}, u32[]{:S(2)}, u32[]{:S(2)}) collective-permute-start(f32[57,8,128]{2,1,0:T(8,128)S(1)} %get-tuple-element.41), channel_id=1, source_target_pairs={{0,1},{1,0},{2,3},{3,2},{4,5},{5,4},{6,7},{7,6},{8,9},{9,8},{10,11... | collective-permute-start | bytes 700424 | tf_op jit(solution)/shard_map/ppermute | solution.py:49
  4.9 7.0 %collective-permute-start.1 = (f32[24,8,128]{2,1,0:T(8,128)S(1)}, f32[24,8,128]{2,1,0:T(8,128)S(1)}, u32[]{:S(2)}, u32[]{:S(2)}) collective-permute-start(f32[24,8,128]{2,1,0:T(8,128)S(1)} %get-tuple-element.42), channel_id=1, source_target_pairs={{1,2},{2,1},{3,4},{4,3},{5,6},{6,5},{7,8},{8,7},{9,10},{10,9},{11,... | collective-permute-start | bytes 294920 | tf_op jit(solution)/shard_map/ppermute | solution.py:49
  12.1 0.7 %shard_map.104 = (f32[6,4,2,32,128]{4,3,2,1,0:T(8,128)S(1)}, f32[8,8,128]{2,1,0:T(8,128)S(1)}, f32[6,8,128]{2,1,0:T(8,128)S(1)}, f32[32,8,128]{2,1,0:T(8,128)S(1)}) custom-call(f32[6,10,16,256]{3,2,1,0:T(8,128)S(1)} %pad_maximum_fusion.old, s32[129]{0:T(256)S(1)} %copy-done.2), custom_call_target="tpu_custom_call" | custom-call | flops 100000 | bytes 100000 | tf_op jit(solution)/shard_map/pallas_call | solution.py:799
  13.0 0.3 reshape.17.neighbours
  13.3 3.2 %shard_map.107.coef = f32[14,3,3,3,8,128]{5,4,3,2,1,0:T(8,128)S(1)} custom-call(s32[6144]{0:T(1024)S(1)} %reshape.17.neighbours, s32[1024]{0:T(1024)S(1)} %copy-done, s32[1024]{0:T(1024)S(1)} %copy-done.1), custom_call_target="tpu_custom_call" | custom-call | flops 500000 | bytes 500000 | tf_op jit(solution)/shard_map/pallas_call | solution.py:799
  16.6 3.7 %collective-permute-start.4 = (f32[32,8,128]{2,1,0:T(8,128)S(1)}, f32[32,8,128]{2,1,0:T(8,128)S(1)}, u32[]{:S(2)}, u32[]{:S(2)}) collective-permute-start(f32[32,8,128]{2,1,0:T(8,128)S(1)} %get-tuple-element.47), channel_id=1, source_target_pairs={{0,64},{1,8},{2,66},{3,10},{4,68},{5,12},{6,70},{7,14},{8,1},{9,73... | collective-permute-start | bytes 393224 | tf_op jit(solution)/shard_map/ppermute | solution.py:49
  20.5 3.9 %collective-permute-done.5.x64 = f32[1,8,128]{2,1,0:T(8,128)S(1)} collective-permute-done((f32[1,8,128]{2,1,0:T(8,128)S(1)}, f32[1,8,128]{2,1,0:T(8,128)S(1)}, u32[]{:S(2)}, u32[]{:S(2)}) %collective-permute-start.5) | collective-permute-done | bytes 4128 | tf_op jit(solution)/shard_map/ppermute | solution.py:49
  24.5 0.9 %collective-permute-start.6 = (f32[38,8,128]{2,1,0:T(8,128)S(1)}, f32[38,8,128]{2,1,0:T(8,128)S(1)}, u32[]{:S(2)}, u32[]{:S(2)}) collective-permute-start(f32[38,8,128]{2,1,0:T(8,128)S(1)} %get-tuple-element.49), channel_id=1, source_target_pairs={{0,2},{1,3},{2,0},{3,1},{4,6},{5,7},{6,4},{7,5},{8,10},{9,11},{10,... | collective-permute-start | bytes 466952 | tf_op jit(solution)/shard_map/ppermute | solution.py:49
  25.4 4.0 %collective-permute-start.7 = (f32[38,8,128]{2,1,0:T(8,128)S(1)}, f32[38,8,128]{2,1,0:T(8,128)S(1)}, u32[]{:S(2)}, u32[]{:S(2)}) collective-permute-start(f32[38,8,128]{2,1,0:T(8,128)S(1)} %get-tuple-element.50), channel_id=1, source_target_pairs={{0,18},{1,19},{2,16},{3,17},{4,22},{5,23},{6,20},{7,21},{8,26},{9,... | collective-permute-start | bytes 466952 | tf_op jit(solution)/shard_map/ppermute | solution.py:49
  29.4 0.9 %collective-permute-start.8 = (f32[1,8,128]{2,1,0:T(8,128)S(1)}, f32[1,8,128]{2,1,0:T(8,128)S(1)}, u32[]{:S(2)}, u32[]{:S(2)}) collective-permute-start(f32[1,8,128]{2,1,0:T(8,128)S(1)} %get-tuple-element.51.peak), channel_id=1, source_target_pairs={{0,8},{1,9},{2,10},{3,11},{4,12},{5,13},{6,14},{7,15},{8,0},{9,1},... | collective-permute-start | bytes 12296 | tf_op jit(solution)/shard_map/ppermute | solution.py:49
  30.3 2.7 %collective-permute-start.9 = (f32[1,8,128]{2,1,0:T(8,128)S(1)}, f32[1,8,128]{2,1,0:T(8,128)S(1)}, u32[]{:S(2)}, u32[]{:S(2)}) collective-permute-start(f32[1,8,128]{2,1,0:T(8,128)S(1)} %get-tuple-element.51.peak), channel_id=1, source_target_pairs={{0,10},{1,11},{2,8},{3,9},{4,14},{5,15},{6,12},{7,13},{8,2},{9,3},... | collective-permute-start | bytes 12296 | tf_op jit(solution)/shard_map/ppermute | solution.py:49
  33.0 0.7 %shard_map.110 = (f32[4,2,40,128]{3,2,1,0:T(8,128)S(1)}, f32[4,2,40,128]{3,2,1,0:T(8,128)S(1)}, f32[4,2,40,128]{3,2,1,0:T(8,128)S(1)}, f32[4,2,40,128]{3,2,1,0:T...) custom-call(f32[6,4,2,32,128]{4,3,2,1,0:T(8,128)S(1)} %get-tuple-ele, ...), custom_call_target="tpu_custom_call" | custom-call | flops 200000 | bytes 200000 | tf_op jit(solution)/shard_map/pallas_call | solution.py:799
  33.8 2.9 %collective-permute-done.9.x10 = f32[1,8,128]{2,1,0:T(8,128)S(1)} collective-permute-done((f32[1,8,128]{2,1,0:T(8,128)S(1)}, f32[1,8,128]{2,1,0:T(8,128)S(1)}, u32[]{:S(2)}, u32[]{:S(2)}) %collective-permute-start.9) | collective-permute-done | bytes 4128 | tf_op jit(solution)/shard_map/ppermute | solution.py:49
  36.7 1.3 %shard_map.111 = (f32[5,2,40,128]{3,2,1,0:T(8,128)S(1)}, f32[5,2,40,128]{3,2,1,0:T(8,128)S(1)}, f32[5,2,40,128]{3,2,1,0:T(8,128)S(1)}, f32[5,2,40,128]{3,2,1,0:T...) custom-call(f32[38,8,128]{2,1,0:T(8,128)S(1)} %collective-permute-do, ...), custom_call_target="tpu_custom_call" | custom-call | flops 100000 | bytes 100000 | tf_op jit(solution)/shard_map/pallas_call | solution.py:799
  38.2 2.5 %collective-permute-start.11 = (f32[39,8,128]{2,1,0:T(8,128)S(1)}, f32[39,8,128]{2,1,0:T(8,128)S(1)}, u32[]{:S(2)}, u32[]{:S(2)}) collective-permute-start(f32[39,8,128]{2,1,0:T(8,128)S(1)} %get-tuple-element.66), channel_id=1, source_target_pairs={{0,36},{1,37},{2,38},{3,39},{4,32},{5,33},{6,34},{7,35},{8,44},{9,... | collective-permute-start | bytes 479240 | tf_op jit(solution)/shard_map/ppermute | solution.py:49
  40.8 0.6 fusion
  43.4 4.5 %collective-permute-done.11.kb = f32[39,8,128]{2,1,0:T(8,128)S(1)} collective-permute-done((f32[39,8,128]{2,1,0:T(8,128)S(1)}, f32[39,8,128]{2,1,0:T(8,128)S(1)}, u32[]{:S(2)}, u32[]{:S(2)}) %collective-permute-start.11) | collective-permute-done | bytes 159776 | tf_op jit(solution)/shard_map/ppermute | solution.py:49
  47.9 4.6 %shard_map.112 = (f32[4,2,32,128]{3,2,1,0:T(8,128)S(1)}, f32[4,2,32,128]{3,2,1,0:T(8,128)S(1)}, f32[2,16,256]{2,1,0:T(8,128)S(1)}, f32[2,16,256]{2,1,0:T(8,128)S(1)}) custom-call(f32[5,2,40,128]{3,2,1,0:T(8,128)S(1)} %get-tuple-element.60.c_in, f32[5,2,40,128]{3,2,1,0:T(8,128)S(1)} %get-tuple-element.61.u_in, f32[5,2,40,128]{3,2,1,0:T(8,128)S(1)} %get-tuple-element.62.s_in, ...), custom_call_target="tpu_custom_call" | custom-call | flops 800000 | bytes 800000 | tf_op jit(solution)/shard_map/pallas_call | solution.py:799
  52.6 4.9 %collective-permute-start.13 = (f32[2,16,256]{2,1,0:T(8,128)S(1)}, f32[2,16,256]{2,1,0:T(8,128)S(1)}, u32[]{:S(2)}, u32[]{:S(2)}) collective-permute-start(f32[2,16,256]{2,1,0:T(8,128)S(1)} %get-tuple-element.68), channel_id=1, source_target_pairs={{1,2},{2,1},{3,4},{4,3},{5,6},{6,5},{7,8},{8,7},{9,10},{10,9},{11,... | collective-permute-start | bytes 98312 | tf_op jit(solution)/shard_map/ppermute | solution.py:49
  57.6 0.6 shard_map.113
  58.2 2.9 %collective-permute-done.13 = f32[2,16,256]{2,1,0:T(8,128)S(1)} collective-permute-done((f32[2,16,256]{2,1,0:T(8,128)S(1)}, f32[2,16,256]{2,1,0:T(8,128)S(1)}, u32[]{:S(2)}, u32[]{:S(2)}) %collective-permute-start.13) | collective-permute-done | bytes 32800 | tf_op jit(solution)/shard_map/ppermute | solution.py:49
  61.1 0.8 %select_select_fusion = (f32[10,16,256]{2,1,0:T(8,128)}, f32[10,16,256]{2,1,0:T(8,128)}) fusion(f32[10,16,256]{2,1,0:T(8,128)S(1)} %get-tuple-element.73, f32[16,256]{1,0:T(8,128)S(1)} %get-tuple-element.78, f32[16,256]{1,0:T(8,128)S(1)} %get-tuple-element.85, pred[10]{0:T(512)(128)(4,1)S(1)} %get-tuple-element.86, pred[10]{0:T(512)(128)(4,1)S(1)} %get-tuple-element.87, ...), kind=kLoop, calls=%fused_computation.1 | loop fusion | flops 163840 | bytes 720916 | tf_op jit(solution)/shard_map/jit(_where)/select_n | solution.py:896
  (34 shorter events, 1.2 us)
Async XLA Ops:
  0.6 1.4 %copy-start.2 = (s32[129]{0:T(256)S(1)}, s32[129]{0:T(256)}, u32[]{:S(2)}) copy-start(s32[129]{0:T(256)} %bounds.4) | copy-start | bytes 1552
  0.6 1.4 %copy-start = (s32[1024]{0:T(1024)S(1)}, s32[1024]{0:T(1024)}, u32[]{:S(2)}) copy-start(s32[1024]{0:T(1024)} %levels.3) | copy-start | bytes 12292
  0.7 12.1 %copy-start.4 = (s32[1024,6]{0,1:T(8,128)S(1)}, s32[1024,6]{0,1:T(8,128)}, u32[]{:S(2)}) copy-start(s32[1024,6]{0,1:T(8,128)} %param.13) | copy-start | bytes 73732
  2.0 11.3 %copy-start.1 = (s32[1024]{0:T(1024)S(1)}, s32[1024]{0:T(1024)}, u32[]{:S(2)}) copy-start(s32[1024]{0:T(1024)} %refine.1) | copy-start | bytes 12292
  2.7 13.8 %collective-permute-start = (f32[57,8,128]{2,1,0:T(8,128)S(1)}, f32[57,8,128]{2,1,0:T(8,128)S(1)}, u32[]{:S(2)}, u32[]{:S(2)}) collective-permute-start(f32[57,8,128]{2,1,0:T(8,128)S(1)} %get-tuple-element.41), channel_id=1, source_target_pairs={{0,1},{1,0},{2,3},{3,2},{4,5},{5,4},{6,7},{7,6},{8,9},{9,8},{10,11... | collective-permute-start | bytes 700424 | tf_op jit(solution)/shard_map/ppermute | solution.py:49
  4.9 11.7 %collective-permute-start.1 = (f32[24,8,128]{2,1,0:T(8,128)S(1)}, f32[24,8,128]{2,1,0:T(8,128)S(1)}, u32[]{:S(2)}, u32[]{:S(2)}) collective-permute-start(f32[24,8,128]{2,1,0:T(8,128)S(1)} %get-tuple-element.42), channel_id=1, source_target_pairs={{1,2},{2,1},{3,4},{4,3},{5,6},{6,5},{7,8},{8,7},{9,10},{10,9},{11,... | collective-permute-start | bytes 294920 | tf_op jit(solution)/shard_map/ppermute | solution.py:49
  11.9 4.7 %collective-permute-start.2 = (f32[1,8,128]{2,1,0:T(8,128)S(1)}, f32[1,8,128]{2,1,0:T(8,128)S(1)}, u32[]{:S(2)}, u32[]{:S(2)}) collective-permute-start(f32[1,8,128]{2,1,0:T(8,128)S(1)} %get-tuple-element.46.peak), channel_id=1, source_target_pairs={{0,16},{1,17},{2,18},{3,19},{4,20},{5,21},{6,22},{7,23},{8,24},{9,... | collective-permute-start | bytes 12296 | tf_op jit(solution)/shard_map/ppermute | solution.py:49
  12.0 4.6 %collective-permute-start.3 = (f32[1,8,128]{2,1,0:T(8,128)S(1)}, f32[1,8,128]{2,1,0:T(8,128)S(1)}, u32[]{:S(2)}, u32[]{:S(2)}) collective-permute-start(f32[1,8,128]{2,1,0:T(8,128)S(1)} %get-tuple-element.46.peak), channel_id=1, source_target_pairs={{0,17},{1,16},{2,19},{3,18},{4,21},{5,20},{6,23},{7,22},{8,25},{9,... | collective-permute-start | bytes 12296 | tf_op jit(solution)/shard_map/ppermute | solution.py:49
  16.6 7.7 %collective-permute-start.4 = (f32[32,8,128]{2,1,0:T(8,128)S(1)}, f32[32,8,128]{2,1,0:T(8,128)S(1)}, u32[]{:S(2)}, u32[]{:S(2)}) collective-permute-start(f32[32,8,128]{2,1,0:T(8,128)S(1)} %get-tuple-element.47), channel_id=1, source_target_pairs={{0,64},{1,8},{2,66},{3,10},{4,68},{5,12},{6,70},{7,14},{8,1},{9,73... | collective-permute-start | bytes 393224 | tf_op jit(solution)/shard_map/ppermute | solution.py:49
  20.3 4.1 %collective-permute-start.5 = (f32[1,8,128]{2,1,0:T(8,128)S(1)}, f32[1,8,128]{2,1,0:T(8,128)S(1)}, u32[]{:S(2)}, u32[]{:S(2)}) collective-permute-start(f32[1,8,128]{2,1,0:T(8,128)S(1)} %get-tuple-element.48.peak), channel_id=1, source_target_pairs={{0,64},{1,65},{2,66},{3,67},{4,68},{5,69},{6,70},{7,71},{8,72},{9,... | collective-permute-start | bytes 12296 | tf_op jit(solution)/shard_map/ppermute | solution.py:49
  24.5 12.2 %collective-permute-start.6 = (f32[38,8,128]{2,1,0:T(8,128)S(1)}, f32[38,8,128]{2,1,0:T(8,128)S(1)}, u32[]{:S(2)}, u32[]{:S(2)}) collective-permute-start(f32[38,8,128]{2,1,0:T(8,128)S(1)} %get-tuple-element.49), channel_id=1, source_target_pairs={{0,2},{1,3},{2,0},{3,1},{4,6},{5,7},{6,4},{7,5},{8,10},{9,11},{10,... | collective-permute-start | bytes 466952 | tf_op jit(solution)/shard_map/ppermute | solution.py:49
  25.4 11.3 %collective-permute-start.7 = (f32[38,8,128]{2,1,0:T(8,128)S(1)}, f32[38,8,128]{2,1,0:T(8,128)S(1)}, u32[]{:S(2)}, u32[]{:S(2)}) collective-permute-start(f32[38,8,128]{2,1,0:T(8,128)S(1)} %get-tuple-element.50), channel_id=1, source_target_pairs={{0,18},{1,19},{2,16},{3,17},{4,22},{5,23},{6,20},{7,21},{8,26},{9,... | collective-permute-start | bytes 466952 | tf_op jit(solution)/shard_map/ppermute | solution.py:49
  29.4 4.3 %collective-permute-start.8 = (f32[1,8,128]{2,1,0:T(8,128)S(1)}, f32[1,8,128]{2,1,0:T(8,128)S(1)}, u32[]{:S(2)}, u32[]{:S(2)}) collective-permute-start(f32[1,8,128]{2,1,0:T(8,128)S(1)} %get-tuple-element.51.peak), channel_id=1, source_target_pairs={{0,8},{1,9},{2,10},{3,11},{4,12},{5,13},{6,14},{7,15},{8,0},{9,1},... | collective-permute-start | bytes 12296 | tf_op jit(solution)/shard_map/ppermute | solution.py:49
  30.3 6.4 %collective-permute-start.9 = (f32[1,8,128]{2,1,0:T(8,128)S(1)}, f32[1,8,128]{2,1,0:T(8,128)S(1)}, u32[]{:S(2)}, u32[]{:S(2)}) collective-permute-start(f32[1,8,128]{2,1,0:T(8,128)S(1)} %get-tuple-element.51.peak), channel_id=1, source_target_pairs={{0,10},{1,11},{2,8},{3,9},{4,14},{5,15},{6,12},{7,13},{8,2},{9,3},... | collective-permute-start | bytes 12296 | tf_op jit(solution)/shard_map/ppermute | solution.py:49
  33.8 7.0 %copy-start.3 = (s32[129]{0:T(256)S(1)}, s32[129]{0:T(256)}, u32[]{:S(2)}) copy-start(s32[129]{0:T(256)} %bounds.5) | copy-start | bytes 1552
  38.1 5.4 %collective-permute-start.10 = (f32[39,8,128]{2,1,0:T(8,128)S(1)}, f32[39,8,128]{2,1,0:T(8,128)S(1)}, u32[]{:S(2)}, u32[]{:S(2)}) collective-permute-start(f32[39,8,128]{2,1,0:T(8,128)S(1)} %get-tuple-element.65), channel_id=1, source_target_pairs={{0,4},{1,5},{2,6},{3,7},{4,0},{5,1},{6,2},{7,3},{8,12},{9,13},{10,... | collective-permute-start | bytes 479240 | tf_op jit(solution)/shard_map/ppermute | solution.py:49
  38.2 9.8 %collective-permute-start.11 = (f32[39,8,128]{2,1,0:T(8,128)S(1)}, f32[39,8,128]{2,1,0:T(8,128)S(1)}, u32[]{:S(2)}, u32[]{:S(2)}) collective-permute-start(f32[39,8,128]{2,1,0:T(8,128)S(1)} %get-tuple-element.66), channel_id=1, source_target_pairs={{0,36},{1,37},{2,38},{3,39},{4,32},{5,33},{6,34},{7,35},{8,44},{9,... | collective-permute-start | bytes 479240 | tf_op jit(solution)/shard_map/ppermute | solution.py:49
  40.7 2.8 %collective-permute-start.12 = (f32[1,8,128]{2,1,0:T(8,128)S(1)}, f32[1,8,128]{2,1,0:T(8,128)S(1)}, u32[]{:S(2)}, u32[]{:S(2)}) collective-permute-start(f32[1,8,128]{2,1,0:T(8,128)S(1)} %get-tuple-element.67.peak), channel_id=1, source_target_pairs={{0,32},{1,33},{2,34},{3,35},{4,36},{5,37},{6,38},{7,39},{8,40},{9,... | collective-permute-start | bytes 12296 | tf_op jit(solution)/shard_map/ppermute | solution.py:49
  52.6 8.6 %collective-permute-start.13 = (f32[2,16,256]{2,1,0:T(8,128)S(1)}, f32[2,16,256]{2,1,0:T(8,128)S(1)}, u32[]{:S(2)}, u32[]{:S(2)}) collective-permute-start(f32[2,16,256]{2,1,0:T(8,128)S(1)} %get-tuple-element.68), channel_id=1, source_target_pairs={{1,2},{2,1},{3,4},{4,3},{5,6},{6,5},{7,8},{8,7},{9,10},{10,9},{11,... | collective-permute-start | bytes 98312 | tf_op jit(solution)/shard_map/ppermute | solution.py:49
  57.4 3.7 %collective-permute-start.14 = (f32[2,16,256]{2,1,0:T(8,128)S(1)}, f32[2,16,256]{2,1,0:T(8,128)S(1)}, u32[]{:S(2)}, u32[]{:S(2)}) collective-permute-start(f32[2,16,256]{2,1,0:T(8,128)S(1)} %get-tuple-element.69), channel_id=1, source_target_pairs={{0,1},{1,0},{2,3},{3,2},{4,5},{5,4},{6,7},{7,6},{8,9},{9,8},{10,11... | collective-permute-start | bytes 98312 | tf_op jit(solution)/shard_map/ppermute | solution.py:49
